TPU v7x, 32 devices: a whole 2x2x4 slice. The times are simulated.
32 devices in a mesh: ctx: 16 (over z, x, core), wsh: 2 (over y).
Axes of the slice: x: 2, y: 2, z: 4, core: 2. Of those that a mesh axis runs over, the one named last changes fastest.
Arguments:
- patches: bfloat16 [2, 4096, 768], P('wsh', 'ctx'), may hold values from -6 to 6
- doc_lengths: int32 [2, 8], P('wsh'), may hold values from 1 to 2048, 4096 in all within a row
- norm1_gain: bfloat16 [768], P('wsh'), may hold values from 0.5 to 1.5
- norm1_bias: bfloat16 [768], P('wsh'), may hold values from -3 to 3
- w_qkv: bfloat16 [768, 2304], P('wsh'), may hold values from -0.21875 to 0.21875
- b_qv: bfloat16 [1536], P('wsh'), may hold values from -3 to 3
- w_out: bfloat16 [768, 768], P('wsh'), may hold values from -6 to 6
- b_out: bfloat16 [768], P('wsh'), may hold values from -2 to 2
- norm2_gain: bfloat16 [768], P('wsh'), may hold values from 0.5 to 1.5
- norm2_bias: bfloat16 [768], P('wsh'), may hold values from -3 to 3
- w_up: bfloat16 [768, 3072], P('wsh'), may hold values from -0.21875 to 0.21875
- b_up: bfloat16 [3072], P('wsh'), may hold values from -3 to 3
- w_down: bfloat16 [3072, 768], P('wsh'), may hold values from -0.109375 to 0.109375
- b_down: bfloat16 [768], P('wsh'), may hold values from -3 to 3
- cotangent: bfloat16 [2, 4096, 768], P('wsh', 'ctx'), may hold values from -6 to 6
Outputs:
- mixed: bfloat16 [2, 4096, 768], P('wsh', 'ctx')
- patches_grad: float32 [2, 4096, 768], P('wsh', 'ctx')
- norm1_gain_grad: float32 [768], P('wsh')
- norm1_bias_grad: float32 [768], P('wsh')
- w_qkv_grad: float32 [768, 2304], P('wsh')
- b_qv_grad: float32 [1536], P('wsh')
- w_out_grad: float32 [768, 768], P('wsh')
- b_out_grad: float32 [768], P('wsh')
- norm2_gain_grad: float32 [768], P('wsh')
- norm2_bias_grad: float32 [768], P('wsh')
- w_up_grad: float32 [768, 3072], P('wsh')
- b_up_grad: float32 [3072], P('wsh')
- w_down_grad: float32 [3072, 768], P('wsh')
- b_down_grad: float32 [768], P('wsh')
Inputs may be any that keep to these rules, and one draw needn't show every extreme that they name: Each row of doc_lengths sums to 4096, and its largest entry is exactly 2048.
All inputs are finite; a program needn't handle non-finite values.
Results may differ from a plain program's by a relative error of at most 0.02.
Values may be sent and summed in bfloat16 or wider, within the bound.
A program may use at most 128 MiB of HBM per device.

v0:
```python
import functools

import jax
import jax.numpy as jnp
from jax import lax
from jax.experimental import pallas as pl
from jax.experimental.pallas import tpu as pltpu
from jax.sharding import PartitionSpec as P

H = 12
HD = 64
GROUPS = 4
PER_GROUP = H // GROUPS
PEERS = 4
MESH = pl.DeviceIdType.MESH
MIB = 2**20

epsilon = 1e-05
masked_score = -1e30


def params(vmem_mib, collective_id=None):
    if collective_id is None:
        return pltpu.CompilerParams(vmem_limit_bytes=vmem_mib * MIB)
    return pltpu.CompilerParams(
        vmem_limit_bytes=vmem_mib * MIB, collective_id=collective_id, has_side_effects=True
    )


def here():
    ctx = lax.axis_index("ctx")
    return ctx // PEERS, (ctx // 2) % 2, ctx % 2, lax.axis_index("wsh")


def at(z, x, core, y):
    return (z * PEERS + x * 2 + core, y)


def remote(src, dst, send, recv, device):
    return pltpu.make_async_remote_copy(
        src_ref=src,
        dst_ref=dst,
        send_sem=send,
        recv_sem=recv,
        device_id=device,
        device_id_type=MESH,
    )


def greet(devices):
    barrier = pltpu.get_barrier_semaphore()
    for device in devices:
        pl.semaphore_signal(barrier, inc=1, device_id=device, device_id_type=MESH)
    pl.semaphore_wait(barrier, len(devices))


def weight_pieces(shapes, most):
    pieces = []
    for index, (rows, columns) in enumerate(shapes):
        quarter = rows // PEERS
        step = quarter
        while step * columns * 2 > most and step % 32 == 0:
            step //= 2
        pieces += [(index, first, step) for first in range(0, quarter, step)]
    return pieces


def weights_kernel(count, pieces, *refs):
    halves, fulls = refs[: count + 1], refs[count + 1 : 2 * count + 2]
    local, ysend, yrecv, xsend, xrecv, csend, crecv, fsend, frecv, small_sem = refs[2 * count + 2 :]
    z, x, core, y = here()
    over_y, over_x, over_core = at(z, x, core, 1 - y), at(z, 1 - x, core, y), at(z, x, 1 - core, y)
    greet([over_y, over_x, over_core])
    small = remote(halves[count], fulls[count].at[y], small_sem.at[0], small_sem.at[1], over_y)
    small.start()
    own = [
        pltpu.make_async_copy(halves[i], fulls[i].at[y], local.at[i]) for i in range(count + 1)
    ]

    def spot(piece, px, pcore):
        index, first, rows = piece
        quarter = fulls[index].shape[1] // PEERS
        return pl.ds((px * 2 + pcore) * quarter + first, rows)

    sends = []
    for k, piece in enumerate(pieces):
        index = piece[0]
        rows = spot(piece, x, core)
        copy = remote(
            halves[index].at[rows], fulls[index].at[y, rows], ysend.at[k], yrecv.at[k], over_y
        )
        copy.start()
        sends.append(copy)
    for copy in own:
        copy.start()

    def landing(k, px, pcore, sem):
        index = pieces[k][0]
        view = fulls[index].at[1 - y, spot(pieces[k], px, pcore)]
        return remote(view, view, sem, sem, over_core)

    def forward(k, px, pcore, send, recv, device):
        index = pieces[k][0]
        view = fulls[index].at[1 - y, spot(pieces[k], px, pcore)]
        copy = remote(view, view, send.at[k], recv.at[k], device)
        copy.start()
        sends.append(copy)

    total = len(pieces)
    for k in range(total + 1):
        if k < total:
            landing(k, x, core, yrecv.at[k]).wait_recv()
            forward(k, x, core, xsend, xrecv, over_x)
            forward(k, x, core, csend, crecv, over_core)
        if k >= 1:
            landing(k - 1, 1 - x, core, xrecv.at[k - 1]).wait_recv()
            forward(k - 1, 1 - x, core, fsend, frecv, over_core)
    for k in range(total):
        landing(k, x, 1 - core, crecv.at[k]).wait_recv()
        landing(k, 1 - x, 1 - core, frecv.at[k]).wait_recv()
    small.wait()
    for copy in own:
        copy.wait()
    for copy in sends:
        copy.wait_send()


def gather_weights(halves, small):
    pieces = weight_pieces([half.shape for half in halves], 320 * 1024)
    count, total = len(halves), len(pieces)
    everything = list(halves) + [small]
    anywhere = pl.BlockSpec(memory_space=pltpu.HBM)
    sems = [pltpu.SemaphoreType.DMA((count + 1,))]
    sems += [pltpu.SemaphoreType.DMA((total,))] * 8 + [pltpu.SemaphoreType.DMA((2,))]
    return pl.pallas_call(
        functools.partial(weights_kernel, count, pieces),
        out_shape=[jax.ShapeDtypeStruct((2,) + a.shape, a.dtype) for a in everything],
        in_specs=[anywhere] * (count + 1),
        out_specs=[anywhere] * (count + 1),
        scratch_shapes=sems,
        compiler_params=params(16, 1),
        name="gather_weights",
    )(*everything)


def spread_kernel(mine, query, keys, local, zsend, zrecv, xsend, xrecv, csend, crecv, fsend, frecv):
    z, x, core, y = here()
    width = query.shape[1]
    over_x, over_core = at(z, 1 - x, core, y), at(z, x, 1 - core, y)
    around = [at((z + d) % GROUPS, x, core, y) for d in range(1, GROUPS)]
    greet(around + [over_x, over_core])
    sends = []

    def go(src, dst, send, recv, device):
        copy = remote(src, dst, send, recv, device)
        copy.start()
        sends.append(copy)

    def block(pz, px, pcore):
        return keys.at[pz * PEERS + px * 2 + pcore]

    own_query = pltpu.make_async_copy(mine.at[z, pl.ds(0, width)], query.at[z], local.at[0])
    own_keys = pltpu.make_async_copy(
        mine.at[z, pl.ds(width, 2 * width)], block(z, x, core), local.at[1]
    )
    own_keys.start()
    own_query.start()
    for d in (2, 1, 3):
        target = (z + d) % GROUPS
        src = mine.at[target, pl.ds(width, 2 * width)]
        go(src, block(z, x, core), zsend.at[d], zrecv.at[d], around[d - 1])
    for d in (2, 1, 3):
        target = (z + d) % GROUPS
        src = mine.at[target, pl.ds(0, width)]
        go(src, query.at[z], zsend.at[GROUPS + d], zrecv.at[GROUPS + d], around[d - 1])
    order = (0, 3, 1, 2)
    for step in range(GROUPS + 1):
        if step < GROUPS:
            d = order[step]
            pz = (z + GROUPS - d) % GROUPS
            view = block(pz, x, core)
            if d == 0:
                own_keys.wait()
            else:
                remote(view, view, zsend.at[d], zrecv.at[d], over_x).wait_recv()
            go(view, view, xsend.at[d], xrecv.at[d], over_x)
            go(view, view, csend.at[d], crecv.at[d], over_core)
        if step >= 1:
            d = order[step - 1]
            view = block((z + GROUPS - d) % GROUPS, 1 - x, core)
            remote(view, view, xsend.at[d], xrecv.at[d], over_x).wait_recv()
            go(view, view, fsend.at[d], frecv.at[d], over_core)
    for d in range(GROUPS):
        pz = (z + GROUPS - d) % GROUPS
        near, far = block(pz, x, 1 - core), block(pz, 1 - x, 1 - core)
        remote(near, near, csend.at[d], crecv.at[d], over_core).wait_recv()
        remote(far, far, fsend.at[d], frecv.at[d], over_core).wait_recv()
        if d > 0:
            part = query.at[pz]
            sem = GROUPS + d
            remote(part, part, zsend.at[sem], zrecv.at[sem], over_x).wait_recv()
    own_query.wait()
    for copy in sends:
        copy.wait_send()


def spread_heads(projected):
    groups, width, rows = projected.shape
    width //= 3
    anywhere = pl.BlockSpec(memory_space=pltpu.HBM)
    sems = [pltpu.SemaphoreType.DMA((2,))] + [pltpu.SemaphoreType.DMA((2 * groups,))] * 2
    sems += [pltpu.SemaphoreType.DMA((groups,))] * 6
    return pl.pallas_call(
        spread_kernel,
        out_shape=[
            jax.ShapeDtypeStruct((groups, width, rows), projected.dtype),
            jax.ShapeDtypeStruct((groups * PEERS, 2 * width, rows), projected.dtype),
        ],
        in_specs=[anywhere],
        out_specs=[anywhere] * 2,
        scratch_shapes=sems,
        compiler_params=params(16, 2),
        name="spread_heads",
    )(projected)


def dot(left, right):
    return jnp.dot(left, right, preferred_element_type=jnp.float32)


def dot_turned(left, right):
    return lax.dot_general(
        left, right, (((1,), (1,)), ((), ())), preferred_element_type=jnp.float32
    )


def normalise(values):
    centre = jnp.mean(values, axis=-1, keepdims=True)
    shifted = values - centre
    spread = jnp.mean(shifted * shifted, axis=-1, keepdims=True)
    scale = lax.rsqrt(spread + epsilon)
    return shifted * scale, scale


def normalise_back(grad, gain, normed, scale):
    inner = grad * gain
    centre = jnp.mean(inner, axis=-1, keepdims=True)
    along = jnp.mean(inner * normed, axis=-1, keepdims=True)
    gain_grad = jnp.sum(grad * normed, axis=0, keepdims=True)
    bias_grad = jnp.sum(grad, axis=0, keepdims=True)
    return scale * (inner - centre - normed * along), gain_grad, bias_grad


LANES = 128


class Packed:
    names = ("gain1", "bias1", "bqv", "bout", "gain2", "bias2", "bup", "bdown")

    def __init__(self, sizes):
        self.sizes = dict(zip(self.names, sizes))
        self.starts, row = {}, 0
        for name in self.names:
            self.starts[name] = row
            row += self.sizes[name] // LANES
        self.used = row
        self.rows = row + -row % 8

    def pack(self, halves):
        flat = jnp.concatenate([half.astype(jnp.float32) for half in halves])
        return jnp.pad(flat.reshape(-1, LANES), ((0, self.rows - self.used), (0, 0)))

    def read(self, ref, name, first=0, count=None):
        count = 2 * self.sizes[name] if count is None else count
        parts = []
        for lane in range(first, first + count, LANES):
            y, inner = divmod(lane, self.sizes[name])
            row = self.starts[name] + inner // LANES
            parts.append(ref[y, row : row + 1])
        return jnp.concatenate(parts, axis=1)

    def write(self, ref, name, values, first=0):
        for lane in range(0, values.shape[1], LANES):
            y, inner = divmod(first + lane, self.sizes[name])
            row = self.starts[name] + inner // LANES
            ref[y, row : row + 1] = values[:, lane : lane + LANES]

    def unpack(self, rows):
        flat = rows[: self.used].reshape(-1)
        parts, start = [], 0
        for name in self.names:
            parts.append(flat[start : start + self.sizes[name]])
            start += self.sizes[name]
        return parts


class Sender:
    def __init__(self):
        self.copies = []

    def __call__(self, src, dst, send, recv, device):
        copy = remote(src, dst, send, recv, device)
        copy.start()
        self.copies.append(copy)

    def finish(self):
        for copy in self.copies:
            copy.wait_send()


def split_rows(first, x, y, quarter):
    if first == "y":
        return [((1 - y) * 2 * quarter, 2 * quarter)], [(y * 2 * quarter, 2 * quarter)]
    other, mine = (1 - x) * quarter, x * quarter
    return (
        [(other, quarter), (2 * quarter + other, quarter)],
        [(mine, quarter), (2 * quarter + mine, quarter)],
    )


def core_sum(first, own, land, send_ref, keep_ref, x, y):
    quarter = land.shape[0] // 4
    gone, kept = split_rows(first, x, y, quarter)
    for ref, parts in ((send_ref, gone), (keep_ref, kept)):
        place = 0
        for start, count in parts:
            rows = pl.ds(start, count)
            total = own(rows).astype(jnp.float32) + land[rows].astype(jnp.float32)
            ref[pl.ds(place, count)] = total.astype(ref.dtype)
            place += count


def middle_kernel(
    pack,
    firsts,
    heads,
    patches,
    out_grad,
    small,
    w_out,
    w_up,
    w_down_half,
    w_down_far,
    mixed,
    hidden_grad,
    grad_heads,
    send_over_x,
    send_over_y,
    keep,
    vector,
    o_land,
    o_grad,
    wout,
    wup,
    wdown,
    act_grad,
    act_turned,
    pre_grad,
    bup_rows,
    grads,
    c_land,
    local,
    osend,
    orecv,
    gsend,
    grecv,
    wsem,
    csend,
    crecv,
):
    f32, bf16 = jnp.float32, jnp.bfloat16
    z, x, core, y = here()
    over_core = at(z, x, 1 - core, y)
    around = [at((z + d) % GROUPS, x, core, y) for d in range(1, GROUPS)]
    rows, width = patches.shape
    tiles = wdown.shape[0] // width
    half = w_down_half.shape[0]
    far = w_down_far.shape[0]
    greet(around + [over_core])
    go = Sender()
    far_rows = pl.ds((1 - y) * half + core * far, far)
    other_rows = pl.ds((1 - y) * half + (1 - core) * far, far)
    for d in (2, 1, 3):
        go(heads.at[(z + d) % GROUPS], o_land.at[z], osend.at[d], orecv.at[d], around[d - 1])
    go(w_down_far, wdown.at[far_rows], wsem.at[0], wsem.at[1], over_core)
    down_copies = [
        pltpu.make_async_copy(w_down_half, wdown.at[pl.ds(y * half, half)], local.at[0]),
        pltpu.make_async_copy(w_down_far, wdown.at[far_rows], local.at[1]),
    ]
    copies = [
        pltpu.make_async_copy(heads.at[z], o_land.at[z], local.at[2]),
        pltpu.make_async_copy(w_out, wout, local.at[3]),
        pltpu.make_async_copy(w_up, wup, local.at[4]),
    ]
    for copy in down_copies + copies:
        copy.start()
    dy = out_grad[...]
    vector[...] = jnp.zeros(vector.shape, f32)
    pack.write(vector, "bdown", jnp.sum(dy.astype(f32), axis=0, keepdims=True))
    for f in range(tiles):
        bup_rows[f, 0:1] = pack.read(small, "bup", f * width, width)
    for copy in down_copies:
        copy.wait()
    landed = wdown.at[other_rows]
    remote(landed, landed, wsem.at[0], wsem.at[1], over_core).wait_recv()

    def tile(f):
        return pl.ds(pl.multiple_of(f * width, width), width)

    def first_grad(f, carry):
        act_grad[f] = dot_turned(dy, wdown[tile(f)])
        return carry

    lax.fori_loop(0, tiles, first_grad, 0)
    for copy in copies:
        copy.wait()
    for d in range(1, GROUPS):
        landed = o_land.at[(z + GROUPS - d) % GROUPS]
        remote(landed, landed, osend.at[d], orecv.at[d], over_core).wait_recv()
    turned = o_land[...].reshape(width, rows)
    hidden = patches[...].astype(f32) + (dot(turned.T, wout[...]) + pack.read(small, "bout"))
    gain2 = pack.read(small, "gain2")
    normed, scale = normalise(hidden)
    c = (normed * gain2 + pack.read(small, "bias2")).astype(bf16)
    mixed_acc = hidden + pack.read(small, "bdown")
    c_grad = jnp.zeros((rows, width), f32)

    def forward_back(f, carry):
        mixed_acc, c_grad = carry
        up = wup[:, tile(f)]
        pre = dot(c, up) + bup_rows[f, 0:1]
        share = 0.5 + 0.5 * lax.erf(pre * (0.5**0.5))
        slope = share + pre * jnp.exp(-0.5 * pre * pre) * ((0.5 / jnp.pi) ** 0.5)
        act = (pre * share).astype(bf16)
        grad = (act_grad[f] * slope).astype(bf16)
        act_turned[tile(f)] = act.T
        pre_grad[f] = grad
        bup_rows[f, 0:1] = jnp.sum(grad.astype(f32), axis=0, keepdims=True)
        return (
            mixed_acc + dot(act, wdown[tile(f)]),
            c_grad + dot_turned(grad, up),
        )

    mixed_acc, c_grad = lax.fori_loop(0, tiles, forward_back, (mixed_acc, c_grad))
    mixed[...] = mixed_acc.astype(bf16)
    for f in range(tiles):
        pack.write(vector, "bup", bup_rows[f, 0:1], f * width)
    part, gain_grad, bias_grad = normalise_back(c_grad, gain2, normed, scale)
    pack.write(vector, "gain2", gain_grad)
    pack.write(vector, "bias2", bias_grad)
    whole = dy.astype(f32) + part
    hidden_grad[...] = whole
    dz = whole.astype(bf16)
    pack.write(vector, "bout", jnp.sum(dz.astype(f32), axis=0, keepdims=True))
    o_grad[...] = dot_turned(wout[...], dz).astype(bf16).reshape(o_grad.shape)
    for d in (2, 1, 3):
        go(o_grad.at[(z + d) % GROUPS], grad_heads.at[z], gsend.at[d], grecv.at[d], around[d - 1])
    own = pltpu.make_async_copy(o_grad.at[z], grad_heads.at[z], local.at[5])
    own.start()

    columns = c_land.shape[2]
    count, ahead = grads.shape[0], send_over_x.shape[0]
    mine = pl.ds(pl.multiple_of(core * columns, columns), columns)
    others = pl.ds(pl.multiple_of((1 - core) * columns, columns), columns)

    def over(k):
        go(grads.at[k, :, others], c_land.at[k], csend.at[k], crecv.at[k], over_core)

    def settle(k):
        landed = c_land.at[k]
        remote(landed, landed, csend.at[k], crecv.at[k], over_core).wait_recv()
        sent = send_over_x.at[k] if k < ahead else send_over_y.at[k - ahead]
        core_sum(firsts[k], lambda r: grads[k, r, mine], c_land.at[k], sent, keep.at[k], x, y)

    c_turned = c.T
    piece = half // tiles
    for k in range(count):
        if k < tiles:
            for top in range(2):
                grads[k, top * piece : (top + 1) * piece] = dot(
                    act_turned[top * half + k * piece : top * half + (k + 1) * piece], dy
                ).astype(bf16)
        elif k < 2 * tiles:
            grads[k] = dot(c_turned, pre_grad[k - tiles]).astype(bf16)
        else:
            grads[k] = dot(turned, dz).astype(bf16)
        over(k)
        if k >= 2:
            settle(k - 2)
    settle(count - 2)
    settle(count - 1)
    for d in range(1, GROUPS):
        landed = grad_heads.at[(z + GROUPS - d) % GROUPS]
        remote(landed, landed, gsend.at[d], grecv.at[d], over_core).wait_recv()
    own.wait()
    go.finish()


def middle(pack, firsts, ahead, heads, patches, out_grad, small, w_out, w_up, w_down_half, w_down_far):
    rows, width = patches.shape
    hidden = w_up.shape[1]
    tiles = hidden // width
    count = 2 * tiles + 1
    f32, bf16 = jnp.float32, jnp.bfloat16
    vmem = pl.BlockSpec(memory_space=pltpu.VMEM)
    hbm = pl.BlockSpec(memory_space=pltpu.HBM)
    dma = pltpu.SemaphoreType.DMA
    return pl.pallas_call(
        functools.partial(middle_kernel, pack, firsts),
        out_shape=[
            jax.ShapeDtypeStruct((rows, width), bf16),
            jax.ShapeDtypeStruct((rows, width), f32),
            jax.ShapeDtypeStruct(heads.shape, bf16),
            jax.ShapeDtypeStruct((ahead, width // 2, width // 2), bf16),
            jax.ShapeDtypeStruct((count - ahead, width // 2, width // 2), bf16),
            jax.ShapeDtypeStruct((count, width // 2, width // 2), bf16),
            jax.ShapeDtypeStruct((2, pack.rows, LANES), f32),
        ],
        in_specs=[hbm, vmem, vmem, vmem, hbm, hbm, hbm, hbm],
        out_specs=[vmem] * 7,
        scratch_shapes=[
            pltpu.VMEM(heads.shape, bf16),
            pltpu.VMEM(heads.shape, bf16),
            pltpu.VMEM((width, width), bf16),
            pltpu.VMEM((width, hidden), bf16),
            pltpu.VMEM((hidden, width), bf16),
            pltpu.VMEM((tiles, rows, width), f32),
            pltpu.VMEM((hidden, rows), bf16),
            pltpu.VMEM((tiles, rows, width), bf16),
            pltpu.VMEM((tiles, 8, width), f32),
            pltpu.VMEM((count, width, width), bf16),
            pltpu.VMEM((count, width, width // 2), bf16),
            dma((6,)),
            dma((GROUPS,)),
            dma((GROUPS,)),
            dma((GROUPS,)),
            dma((GROUPS,)),
            dma((2,)),
            dma((count,)),
            dma((count,)),
        ],
        compiler_params=params(60, 3),
        name="middle",
    )(heads, patches, out_grad, small, w_out, w_up, w_down_half, w_down_far)


class Totals:
    def __init__(self, refs, tiles):
        self.refs, self.tiles = refs, tiles

    def place(self, k, row, count, column, columns):
        down, up, out, qkv = self.refs
        width = out.shape[1]
        if k < self.tiles:
            rows = pl.ds(k * (width // 2) + row, count)
            return down, rows, pl.ds(pl.multiple_of(column, LANES), columns)
        if k < 2 * self.tiles:
            ref, start = up, (k - self.tiles) * width
        elif k == 2 * self.tiles:
            ref, start = out, 0
        else:
            ref, start = qkv, (k - 2 * self.tiles - 1) * width
        return ref, pl.ds(row, count), pl.ds(pl.multiple_of(start + column, LANES), columns)

    def view(self, *place):
        ref, rows, columns = self.place(*place)
        return ref.at[rows, columns]

    def store(self, values, *place):
        ref, rows, columns = self.place(*place)
        ref[rows, columns] = values.astype(ref.dtype)


def last_kernel(
    pack,
    firsts,
    tiles,
    query_grad,
    key_grad,
    normed_low,
    w_qkv,
    patches,
    hidden_grad,
    small,
    landed_ahead,
    send_on,
    keep,
    vector_in,
    inputs_grad,
    down_total,
    up_total,
    out_total,
    qkv_total,
    vector_out,
    got,
    near,
    both,
    far,
    own,
    wqkv,
    grads,
    c_land,
    late_send,
    first_land,
    half_sum,
    second_land,
    quarter_sum,
    z_land,
    eighth_sum,
    far_land,
    vectors,
    v_land,
    local,
    n_send,
    n_recv,
    f_send,
    f_recv,
    q_send,
    q_recv,
    csend,
    crecv,
    asend,
    arecv,
    bsend,
    brecv,
    zsend,
    zrecv,
    wsend,
    wrecv,
    dsend,
    drecv,
    gsend,
    grecv,
    hsend,
    hrecv,
    isend,
    irecv,
    vsend,
    vrecv,
):
    f32, bf16 = jnp.float32, jnp.bfloat16
    z, x, core, y = here()
    over_x, over_core, over_y = (
        at(z, 1 - x, core, y),
        at(z, x, 1 - core, y),
        at(z, x, core, 1 - y),
    )
    around = [at((z + d) % GROUPS, x, core, y) for d in range(1, GROUPS)]
    peer = {"y": over_y, "x": over_x}
    greet(around + [over_x, over_core, over_y])
    go = Sender()
    totals = Totals((down_total, up_total, out_total, qkv_total), tiles)
    part = query_grad.shape[1]
    rows, width = patches.shape
    ahead, chunks = landed_ahead.shape[0], len(firsts)
    early = ahead + send_on.shape[0]
    pair, side = z // 2, z % 2
    over_near, over_far = at(z + 1 - 2 * side, x, core, y), around[1]
    half = c_land.shape[2]
    quarter, shard = width // 4, width // 16

    def landed(view, sem):
        remote(view, view, sem, sem, over_core).wait_recv()

    order = (2, 1, 3, 0)
    for d in order:
        pz = (z + d) % GROUPS
        for k in range(2):
            px = (x + 1 + k) % 2
            slot = 2 * d + k
            src = key_grad.at[pz * PEERS + px * 2 + 1 - core]
            go(src, near.at[slot], n_send.at[slot], n_recv.at[slot], over_core)
    for d in (2, 1, 3):
        pz = (z + d) % GROUPS
        go(query_grad.at[pz], got.at[z, pl.ds(0, part)], q_send.at[d], q_recv.at[d], around[d - 1])
    own_query = pltpu.make_async_copy(query_grad.at[z], got.at[z, pl.ds(0, part)], local.at[0])
    own_query.start()
    weights = pltpu.make_async_copy(w_qkv, wqkv, local.at[2])
    weights.start()

    def start_first(k, src):
        go(src, first_land.at[k], asend.at[k], arecv.at[k], peer[firsts[k]])

    for k in range(ahead, early):
        start_first(k, send_on.at[k - ahead])
    for step in range(GROUPS + 1):
        if step < GROUPS:
            d = order[step]
            pz = (z + d) % GROUPS
            for k in range(2):
                px = (x + 1 + k) % 2
                slot = 2 * d + k
                landed(near.at[slot], n_recv.at[slot])
                mine = key_grad[pz * PEERS + px * 2 + core].astype(f32)
                both[slot] = (mine + near[slot].astype(f32)).astype(bf16)
                if k == 0:
                    go(both.at[slot], far.at[d], f_send.at[d], f_recv.at[d], over_x)
        if step >= 1:
            d = order[step - 1]
            landed(far.at[d], f_recv.at[d])
            own[d] = (both[2 * d + 1].astype(f32) + far[d].astype(f32)).astype(bf16)
            place = got.at[z, pl.ds(part, 2 * part)]
            if d == 0:
                own_keys = pltpu.make_async_copy(own.at[0], place, local.at[1])
                own_keys.start()
            else:
                sem = GROUPS + d
                go(own.at[d], place, q_send.at[sem], q_recv.at[sem], around[d - 1])
    normed_turned = normed_low[...].T
    normed, scale = normalise(patches[...].astype(f32))
    gain1 = pack.read(small, "gain1")
    def kept(k):
        return keep[k] if k < early else half_sum[k]

    def stage_core(k):
        i = k - early
        landed(c_land.at[i], crecv.at[i])
        mine = pl.ds(pl.multiple_of(core * half, half), half)
        core_sum(
            firsts[k],
            lambda r: grads[i, r, mine],
            c_land.at[i],
            late_send.at[i],
            half_sum.at[k],
            x,
            y,
        )
        start_first(k, late_send.at[i])

    def stage_first(k):
        if k < ahead:
            arrived = landed_ahead[k]
        else:
            landed(first_land.at[k], arecv.at[k])
            arrived = first_land[k]
        half_sum[k] = (kept(k).astype(f32) + arrived.astype(f32)).astype(bf16)
        place = x if firsts[k] == "y" else y
        other = half_sum.at[k, pl.ds((1 - place) * quarter, quarter)]
        second = over_x if firsts[k] == "y" else over_y
        go(other, second_land.at[k], bsend.at[k], brecv.at[k], second)

    def stage_second(k):
        landed(second_land.at[k], brecv.at[k])
        place = x if firsts[k] == "y" else y
        total = half_sum[k, pl.ds(place * quarter, quarter)].astype(f32)
        quarter_sum[k] = (total + second_land[k].astype(f32)).astype(bf16)
        other = quarter_sum.at[k, pl.ds((1 - side) * 2 * shard, 2 * shard)]
        go(other, z_land.at[k], zsend.at[k], zrecv.at[k], over_near)

    def stage_near(k):
        landed(z_land.at[k], zrecv.at[k])
        total = quarter_sum[k, pl.ds(side * 2 * shard, 2 * shard)].astype(f32)
        eighth_sum[k] = (total + z_land[k].astype(f32)).astype(bf16)
        other = eighth_sum.at[k, pl.ds((1 - pair) * shard, shard)]
        go(other, far_land.at[k], wsend.at[k], wrecv.at[k], over_far)

    def spot(k, px, pside, ppair, count):
        row = px * quarter + pside * 2 * shard + ppair * shard
        return totals.view(k, row, count, core * half, half)

    def stage_far(k):
        landed(far_land.at[k], wrecv.at[k])
        total = eighth_sum[k, pl.ds(pair * shard, shard)].astype(f32) + far_land[k].astype(f32)
        row = x * quarter + side * 2 * shard + pair * shard
        totals.store(total, k, row, shard, core * half, half)
        view = spot(k, x, side, pair, shard)
        go(view, view, dsend.at[k], drecv.at[k], over_far)

    def stage_back(k):
        landed(spot(k, x, side, 1 - pair, shard), drecv.at[k])
        view = spot(k, x, side, 0, 2 * shard)
        go(view, view, gsend.at[k], grecv.at[k], over_near)

    def stage_out(k):
        landed(spot(k, x, 1 - side, 0, 2 * shard), grecv.at[k])
        view = spot(k, x, 0, 0, quarter)
        go(view, view, hsend.at[k], hrecv.at[k], over_x)
        go(view, view, isend.at[2 * k], irecv.at[2 * k], over_core)

    def stage_last(k):
        view = spot(k, 1 - x, 0, 0, quarter)
        landed(view, hrecv.at[k])
        go(view, view, isend.at[2 * k + 1], irecv.at[2 * k + 1], over_core)

    stages = (
        stage_first,
        stage_second,
        stage_near,
        stage_far,
        stage_back,
        stage_out,
        stage_last,
    )

    def turn(step):
        for depth, stage in enumerate(stages):
            if 0 <= step - depth < chunks:
                stage(step - depth)

    before = min(early, 4)
    for step in range(before):
        turn(step)

    for d in range(1, GROUPS):
        pz = (z + GROUPS - d) % GROUPS
        landed(got.at[pz, pl.ds(0, part)], q_recv.at[d])
        landed(got.at[pz, pl.ds(part, 2 * part)], q_recv.at[GROUPS + d])
    own_query.wait()
    own_keys.wait()
    weights.wait()

    for k in range(early, chunks):
        i = k - early
        turned = got[:, i * part : (i + 1) * part].reshape(width, rows)
        grads[i] = dot_turned(normed_turned, turned).astype(bf16)
        others = pl.ds(pl.multiple_of((1 - core) * half, half), half)
        go(grads.at[i, :, others], c_land.at[i], csend.at[i], crecv.at[i], over_core)
    vectors[0] = vector_in[...]
    ones = jnp.ones((8, rows), bf16)
    normed_grad = jnp.zeros((width, rows), f32)
    for i in range(chunks - early):
        turned = got[:, i * part : (i + 1) * part].reshape(width, rows)
        if i != 1:
            sums = dot_turned(ones, turned)[0:1]
            pack.write(vectors.at[0], "bqv", sums, (i // 2) * width)
        normed_grad += dot(wqkv[:, i * width : (i + 1) * width], turned)
    change, gain_grad, bias_grad = normalise_back(normed_grad.T, gain1, normed, scale)
    inputs_grad[...] = hidden_grad[...] + change
    pack.write(vectors.at[0], "gain1", gain_grad)
    pack.write(vectors.at[0], "bias1", bias_grad)
    go(vectors.at[0], v_land.at[0], vsend.at[0], vrecv.at[0], over_core)

    def vector_step(n):
        if n == 0:
            landed(v_land.at[0], vrecv.at[0])
            vectors[1] = vectors[0] + v_land[0]
            go(vectors.at[1], v_land.at[1], vsend.at[1], vrecv.at[1], over_x)
        elif n == 1:
            landed(v_land.at[1], vrecv.at[1])
            vectors[2] = vectors[1] + v_land[1]
            go(vectors.at[2], v_land.at[2], vsend.at[2], vrecv.at[2], over_y)
        elif n == 2:
            landed(v_land.at[2], vrecv.at[2])
            vectors[3] = vectors[2] + v_land[2]
            for d in range(1, GROUPS):
                sem = 2 + d
                go(vectors.at[3], v_land.at[sem], vsend.at[sem], vrecv.at[sem], around[d - 1])
        elif n == 3:
            total = vectors[3]
            for d in range(1, GROUPS):
                landed(v_land.at[2 + d], vrecv.at[2 + d])
                total += v_land[2 + d]
            v_land[0] = total
            vector_out[...] = v_land[0, y]

    for k in range(early, chunks):
        stage_core(k)
    for step in range(before, chunks + len(stages) - 1):
        turn(step)
        vector_step(step - before)
    for k in range(chunks):
        for px in range(2):
            place = (x + px) % 2
            view = totals.view(k, place * quarter, quarter, (1 - core) * half, half)
            landed(view, irecv.at[2 * k + px])
    go.finish()


def last(
    pack, firsts, query_grad, key_grad, normed_low, w_qkv, patches, hidden_grad, small,
    landed_ahead, send_on, keep, vector
):
    f32, bf16 = jnp.float32, jnp.bfloat16
    vmem = pl.BlockSpec(memory_space=pltpu.VMEM)
    hbm = pl.BlockSpec(memory_space=pltpu.HBM)
    groups, part, rows = query_grad.shape
    width = patches.shape[1]
    early, half = keep.shape[0], width // 2
    tiles, chunks, late = (early - 1) // 2, len(firsts), len(firsts) - early
    piece = (2 * part, rows)
    dma = pltpu.SemaphoreType.DMA

    def pair(n):
        return [dma((n,))] * 2

    return pl.pallas_call(
        functools.partial(last_kernel, pack, firsts, tiles),
        out_shape=[
            jax.ShapeDtypeStruct((rows, width), f32),
            jax.ShapeDtypeStruct((tiles * half, width), bf16),
            jax.ShapeDtypeStruct((half, tiles * width), bf16),
            jax.ShapeDtypeStruct((half, width), bf16),
            jax.ShapeDtypeStruct((half, late * width), bf16),
            jax.ShapeDtypeStruct(vector.shape[1:], f32),
        ],
        in_specs=[hbm, vmem, vmem, hbm, vmem, vmem, vmem, vmem, hbm, vmem, vmem],
        out_specs=[vmem] * 6,
        scratch_shapes=[
            pltpu.VMEM((groups, 3 * part, rows), bf16),
            pltpu.VMEM((2 * groups,) + piece, bf16),
            pltpu.VMEM((2 * groups,) + piece, bf16),
            pltpu.VMEM((groups,) + piece, bf16),
            pltpu.VMEM((groups,) + piece, bf16),
            pltpu.VMEM(w_qkv.shape, bf16),
            pltpu.VMEM((late, width, width), bf16),
            pltpu.VMEM((late, width, half), bf16),
            pltpu.VMEM((late, half, half), bf16),
            pltpu.VMEM((chunks, half, half), bf16),
            pltpu.VMEM((chunks, half, half), bf16),
            pltpu.VMEM((chunks, half // 2, half), bf16),
            pltpu.VMEM((chunks, half // 2, half), bf16),
            pltpu.VMEM((chunks, half // 4, half), bf16),
            pltpu.VMEM((chunks, half // 4, half), bf16),
            pltpu.VMEM((chunks, half // 8, half), bf16),
            pltpu.VMEM((4,) + vector.shape, f32),
            pltpu.VMEM((6,) + vector.shape, f32),
            dma((3,)),
        ]
        + pair(2 * groups)
        + pair(groups)
        + pair(2 * groups)
        + pair(late)
        + pair(chunks)
        + pair(chunks)
        + pair(chunks) * 5
        + pair(2 * chunks)
        + pair(6),
        compiler_params=params(60, 4),
        name="last",
    )(
        query_grad, key_grad, normed_low, w_qkv, patches, hidden_grad, small, landed_ahead, send_on,
        keep, vector
    )


def attend_kernel(spans, query, keys, marks, veto, out, out_low, sums, key_rows, query_aug, acc, stat):
    blocks, rows = keys.shape[0], keys.shape[2]
    width = query.shape[1]
    groups = query.shape[0]

    def turn(j, carry):
        mark = marks[j]
        for h in range(PER_GROUP):
            both = jnp.concatenate([keys[j, h * HD : (h + 1) * HD], mark], axis=0)
            key_rows[h, j] = both.T
        return carry

    lax.fori_loop(0, blocks, turn, 0)
    for i in range(groups):
        for h in range(PER_GROUP):
            query_aug[h, :HD] = query[i, h * HD : (h + 1) * HD] * jnp.bfloat16(0.125)
            query_aug[h, HD:] = veto[i]
        stat[0] = jnp.full(stat.shape[1:], masked_score, jnp.float32)
        stat[1] = jnp.zeros(stat.shape[1:], jnp.float32)
        acc[...] = jnp.zeros(acc.shape, jnp.float32)

        def step(j, carry):
            for h in range(PER_GROUP):
                scores = dot(key_rows[h, j], query_aug[h])
                old = stat[0, h : h + 1]
                new = jnp.maximum(old, jnp.max(scores, axis=0, keepdims=True))
                probs = jnp.exp(scores - new)
                factor = jnp.exp(old - new)
                stat[0, h : h + 1] = new
                stat[1, h : h + 1] = stat[1, h : h + 1] * factor + jnp.sum(
                    probs, axis=0, keepdims=True
                )
                values = keys[j, width + h * HD : width + (h + 1) * HD]
                acc[h] = acc[h] * factor + dot(values, probs.astype(jnp.bfloat16))
            return carry

        lax.fori_loop(spans[i, 0], spans[i, 1], step, 0)
        for h in range(PER_GROUP):
            total = stat[1, h : h + 1]
            shared = acc[h] / total
            out[i, h * HD : (h + 1) * HD] = shared
            out_low[i, h * HD : (h + 1) * HD] = shared.astype(jnp.bfloat16)
            sums[i, h : h + 1] = stat[0, h : h + 1] + jnp.log(total)


def attend(spans, query, keys, marks, veto):
    groups, width, rows = query.shape
    blocks = keys.shape[0]
    vmem = pl.BlockSpec(memory_space=pltpu.VMEM)
    return pl.pallas_call(
        attend_kernel,
        out_shape=[
            jax.ShapeDtypeStruct(query.shape, jnp.float32),
            jax.ShapeDtypeStruct(query.shape, jnp.bfloat16),
            jax.ShapeDtypeStruct((groups, 8, rows), jnp.float32),
        ],
        in_specs=[pl.BlockSpec(memory_space=pltpu.SMEM)] + [vmem] * 4,
        out_specs=[vmem] * 3,
        scratch_shapes=[
            pltpu.VMEM((PER_GROUP, blocks, rows, 2 * HD), jnp.bfloat16),
            pltpu.VMEM((PER_GROUP, 2 * HD, rows), jnp.bfloat16),
            pltpu.VMEM((PER_GROUP, HD, rows), jnp.float32),
            pltpu.VMEM((2, 8, rows), jnp.float32),
        ],
        compiler_params=params(40),
        name="attend",
    )(spans, query, keys, marks, veto)


def three_parts(values):
    high = values.astype(jnp.bfloat16)
    rest = values - high.astype(jnp.float32)
    middle = rest.astype(jnp.bfloat16)
    low = (rest - middle.astype(jnp.float32)).astype(jnp.bfloat16)
    return high, middle, low


def attend_back_kernel(
    spans,
    query,
    keys,
    marks,
    veto,
    out,
    sums,
    out_grad,
    query_grad,
    key_grad,
    key_rows,
    value_rows,
    query_aug,
    grad_aug,
    query_rows,
    grad_rows,
    query_acc,
    key_acc,
):
    blocks, rows = keys.shape[0], keys.shape[2]
    width = query.shape[1]
    groups = query.shape[0]
    bf16 = jnp.bfloat16

    def turn(j, carry):
        mark = marks[j]
        for h in range(PER_GROUP):
            both = jnp.concatenate([keys[j, h * HD : (h + 1) * HD], mark], axis=0)
            key_rows[h, j] = both.T
            values = keys[j, width + h * HD : width + (h + 1) * HD]
            value_rows[h, j] = jnp.concatenate([values, mark], axis=0).T
            key_acc[h, j] = jnp.zeros(key_acc.shape[2:], jnp.float32)
        return carry

    lax.fori_loop(0, blocks, turn, 0)
    index = lax.broadcasted_iota(jnp.int32, (HD, rows), 0)
    none = jnp.zeros((HD, rows), bf16)

    def spread(values):
        high, middle, low = three_parts(-values)
        wide = jnp.where(index == 8, high.astype(jnp.float32), 0.0)
        wide = jnp.where(index == 9, middle.astype(jnp.float32), wide)
        return jnp.where(index == 10, low.astype(jnp.float32), wide).astype(bf16)

    for i in range(groups):
        for h in range(PER_GROUP):
            span = slice(h * HD, (h + 1) * HD)
            part = query[i, span] * bf16(0.125)
            grad = out_grad[i, span]
            delta = jnp.sum(grad.astype(jnp.float32) * out[i, span], axis=0, keepdims=True)
            query_aug[h, :HD] = part
            query_aug[h, HD:] = veto[i] + spread(sums[i, h : h + 1])
            grad_aug[h, :HD] = grad
            grad_aug[h, HD:] = spread(delta)
            query_rows[h] = jnp.concatenate([part, none], axis=0).T
            grad_rows[h] = jnp.concatenate([none, grad], axis=0).T
        query_acc[...] = jnp.zeros(query_acc.shape, jnp.float32)

        def step(j, carry):
            for h in range(PER_GROUP):
                probs = jnp.exp(dot(key_rows[h, j], query_aug[h]))
                change = (probs * dot(value_rows[h, j], grad_aug[h])).astype(bf16)
                key_acc[h, j] += dot(probs.astype(bf16), grad_rows[h]) + dot(change, query_rows[h])
                query_acc[h] += dot(keys[j, h * HD : (h + 1) * HD], change)
            return carry

        lax.fori_loop(spans[i, 0], spans[i, 1], step, 0)
        for h in range(PER_GROUP):
            query_grad[i, h * HD : (h + 1) * HD] = (query_acc[h] * 0.125).astype(bf16)

    def finish(j, carry):
        for h in range(PER_GROUP):
            both = key_acc[h, j].T.astype(bf16)
            key_grad[j, h * HD : (h + 1) * HD] = both[:HD]
            key_grad[j, width + h * HD : width + (h + 1) * HD] = both[HD:]
        return carry

    lax.fori_loop(0, blocks, finish, 0)


def attend_back(spans, query, keys, marks, veto, out, sums, out_grad):
    groups, width, rows = query.shape
    blocks = keys.shape[0]
    vmem = pl.BlockSpec(memory_space=pltpu.VMEM)
    bf16 = jnp.bfloat16
    return pl.pallas_call(
        attend_back_kernel,
        out_shape=[
            jax.ShapeDtypeStruct(query.shape, bf16),
            jax.ShapeDtypeStruct(keys.shape, bf16),
        ],
        in_specs=[pl.BlockSpec(memory_space=pltpu.SMEM)] + [vmem] * 7,
        out_specs=[vmem] * 2,
        scratch_shapes=[
            pltpu.VMEM((PER_GROUP, blocks, rows, 2 * HD), bf16),
            pltpu.VMEM((PER_GROUP, blocks, rows, 2 * HD), bf16),
            pltpu.VMEM((PER_GROUP, 2 * HD, rows), bf16),
            pltpu.VMEM((PER_GROUP, 2 * HD, rows), bf16),
            pltpu.VMEM((PER_GROUP, rows, 2 * HD), bf16),
            pltpu.VMEM((PER_GROUP, rows, 2 * HD), bf16),
            pltpu.VMEM((PER_GROUP, HD, rows), jnp.float32),
            pltpu.VMEM((PER_GROUP, blocks, rows, 2 * HD), jnp.float32),
        ],
        compiler_params=params(56),
        name="attend_back",
    )(spans, query, keys, marks, veto, out, sums, out_grad)


def layer_norm(values, gain, offset):
    centre = jnp.mean(values, axis=-1, keepdims=True)
    shifted = values - centre
    spread = jnp.mean(shifted * shifted, axis=-1, keepdims=True)
    return shifted * lax.rsqrt(spread + epsilon) * gain + offset


def exact_gelu(values):
    return jax.nn.gelu(values, approximate=False)


def doc_index(positions, doc_starts):
    hits = (doc_starts[None, :] <= positions[:, None]).astype(jnp.int32)
    return jnp.sum(hits, axis=1) - 1


def doc_tables(doc_lengths, ctx_place, blocks, rows):
    bf16 = jnp.bfloat16
    lengths = doc_lengths[0]
    ends = jnp.cumsum(lengths)
    starts = ends - lengths
    count = lengths.shape[0]
    docs = doc_index(jnp.arange(blocks * rows, dtype=jnp.int32), starts).reshape(blocks, 1, rows)
    number = lax.broadcasted_iota(jnp.int32, (blocks, HD, rows), 1)
    ones = (number >= 8) & (number < 16)
    marks = ((number == docs) | ones).astype(bf16)
    mine = PEERS * jnp.arange(GROUPS, dtype=jnp.int32) + ctx_place % PEERS
    my_docs = docs.reshape(GROUPS, PEERS, 1, rows)[:, ctx_place % PEERS]
    number = number[:GROUPS]
    veto = jnp.where((number != my_docs) & (number < count), masked_score, 0.0).astype(bf16)
    first = doc_index(mine * rows, starts)
    last = doc_index(mine * rows + rows - 1, starts)
    spans = jnp.stack([starts[first] // rows, (ends[last] + rows - 1) // rows], axis=1)
    return spans.astype(jnp.int32), marks, veto


def body(
    patches,
    doc_lengths,
    norm1_gain,
    norm1_bias,
    w_qkv,
    b_qv,
    w_out,
    b_out,
    norm2_gain,
    norm2_bias,
    w_up,
    b_up,
    w_down,
    b_down,
    cotangent,
):
    f32, bf16 = jnp.float32, jnp.bfloat16
    rows, width = patches.shape[1:]
    ctx_place = lax.axis_index("ctx")
    blocks = lax.axis_size("ctx")
    spans, marks, veto = doc_tables(doc_lengths, ctx_place, blocks, rows)
    vectors = [norm1_gain, norm1_bias, b_qv, b_out, norm2_gain, norm2_bias, b_up, b_down]
    pack = Packed([v.shape[0] for v in vectors])
    wqkv2, wout2, wup2, small = gather_weights([w_qkv, w_out, w_up], pack.pack(vectors))
    wqkv = wqkv2.reshape(width, -1)
    wout = wout2.reshape(width, -1)
    wup = wup2.reshape(width, -1)
    far = w_down.shape[0] // 2
    down_part = lax.dynamic_slice_in_dim(w_down, (ctx_place % 2) * far, far)
    down_far = lax.ppermute(down_part, "wsh", [(0, 1), (1, 0)])

    def whole(name):
        start = pack.starts[name]
        part = small[:, start : start + pack.sizes[name] // LANES]
        return part.reshape(-1)

    inputs = patches[0].astype(f32)
    normed1 = layer_norm(inputs, whole("gain1"), whole("bias1")).astype(bf16)
    projected = jnp.dot(normed1, wqkv, preferred_element_type=f32)
    bqv = whole("bqv")
    offset = jnp.concatenate([bqv[:width], jnp.zeros((width,), f32), bqv[width:]])
    projected = (projected + offset).astype(bf16)
    part = width // GROUPS
    by_group = projected.reshape(rows, 3, GROUPS, part).transpose(2, 1, 3, 0)
    query, keys = spread_heads(by_group.reshape(GROUPS, 3 * part, rows))
    out_heads, heads_low, sums = attend(spans, query, keys, marks, veto)
    tiles = w_up.shape[1] // width
    chunks = 2 * tiles + 1 + w_qkv.shape[1] // width
    ahead = 4
    firsts = ["x"] * ahead + ["y"] * (chunks - ahead)
    mixed, hidden_grad, grad_heads, send_over_x, send_over_y, keep, vector = middle(
        pack, firsts, ahead, heads_low, patches[0], cotangent[0], small, wout, wup, w_down, down_far
    )
    across = [(c, c + 2 - c // 2 % 2 * 4) for c in range(blocks)]
    landed_ahead = lax.ppermute(send_over_x, "ctx", across)
    query_grad, key_grad = attend_back(
        spans, query, keys, marks, veto, out_heads, sums, grad_heads
    )
    inputs_grad, down_total, up_total, out_total, qkv_total, vector_total = last(
        pack, firsts, query_grad, key_grad, normed1, wqkv, patches[0], hidden_grad, small,
        landed_ahead, send_over_y, keep, vector,
    )
    shares = pack.unpack(vector_total)
    return (
        mixed[None],
        inputs_grad[None],
        shares[0],
        shares[1],
        qkv_total.astype(f32),
        shares[2],
        out_total.astype(f32),
        shares[3],
        shares[4],
        shares[5],
        up_total.astype(f32),
        shares[6],
        down_total.astype(f32),
        shares[7],
    )


def shifted_2(block, axis, distance):
    devices = range(lax.axis_size(axis))
    route = [((i - distance) % len(devices), i) for i in devices]
    return lax.ppermute(block, axis, route)


def any_mesh_body(
    patches,
    doc_lengths,
    norm1_gain,
    norm1_bias,
    w_qkv,
    b_qv,
    w_out,
    b_out,
    norm2_gain,
    norm2_bias,
    w_up,
    b_up,
    w_down,
    b_down,
    cotangent,
):
    tok_rows = patches.shape[1]
    model_width = patches.shape[2]
    ctx_size = lax.axis_size("ctx")
    ctx_place = lax.axis_index("ctx")
    gathered = (
        lax.all_gather(norm1_gain, "wsh", axis=0, tiled=True),
        lax.all_gather(norm1_bias, "wsh", axis=0, tiled=True),
        lax.all_gather(w_qkv, "wsh", axis=0, tiled=True),
        lax.all_gather(b_qv, "wsh", axis=0, tiled=True),
        lax.all_gather(w_out, "wsh", axis=0, tiled=True),
        lax.all_gather(b_out, "wsh", axis=0, tiled=True),
        lax.all_gather(norm2_gain, "wsh", axis=0, tiled=True),
        lax.all_gather(norm2_bias, "wsh", axis=0, tiled=True),
        lax.all_gather(w_up, "wsh", axis=0, tiled=True),
        lax.all_gather(b_up, "wsh", axis=0, tiled=True),
        lax.all_gather(w_down, "wsh", axis=0, tiled=True),
        lax.all_gather(b_down, "wsh", axis=0, tiled=True),
    )
    (
        gain1,
        bias1,
        wqkv_full,
        bqv_full,
        wout_full,
        bout_full,
        gain2,
        bias2,
        wup_full,
        bup_full,
        wdown_full,
        bdown_full,
    ) = gathered
    inputs = patches[0].astype(jnp.float32)
    lengths = doc_lengths[0]
    doc_starts = jnp.cumsum(lengths) - lengths
    row_offsets = lax.iota(jnp.int32, tok_rows)
    query_docs = doc_index(ctx_place * tok_rows + row_offsets, doc_starts)
    gain1_float = gain1.astype(jnp.float32)
    bias1_float = bias1.astype(jnp.float32)
    normed1 = layer_norm(inputs, gain1_float, bias1_float).astype(jnp.bfloat16)
    projected = jnp.dot(normed1, wqkv_full, preferred_element_type=jnp.float32)
    bqv_float = bqv_full.astype(jnp.float32)
    query_low = (projected[:, :model_width] + bqv_float[:model_width]).astype(jnp.bfloat16)
    key_low = projected[:, model_width : 2 * model_width].astype(jnp.bfloat16)
    value_low = (projected[:, 2 * model_width :] + bqv_float[model_width:]).astype(jnp.bfloat16)
    query_heads = query_low.reshape(tok_rows, H, HD)

    def attend_block(state, key_block, value_block, key_start):
        run_max, run_total, run_acc = state
        key_docs = doc_index(key_start + row_offsets, doc_starts)
        same_doc = (query_docs[:, None] == key_docs[None, :])[None]
        scores = (
            jnp.einsum(
                "qhd,khd->hqk",
                query_heads,
                key_block.reshape(tok_rows, H, HD),
                preferred_element_type=jnp.float32,
            )
            * 0.125
        )
        scores = jnp.where(same_doc, scores, masked_score)
        new_max = jnp.maximum(run_max, jnp.max(scores, axis=2))
        weights = jnp.where(same_doc, jnp.exp(scores - new_max[:, :, None]), 0.0)
        factor = jnp.exp(run_max - new_max)
        new_total = run_total * factor + jnp.sum(weights, axis=2)
        new_acc = run_acc * factor[:, :, None] + jnp.einsum(
            "hqk,khd->hqd",
            weights.astype(jnp.bfloat16),
            value_block.reshape(tok_rows, H, HD),
            preferred_element_type=jnp.float32,
        )
        return (new_max, new_total, new_acc)

    initial = (
        jnp.full((H, tok_rows), masked_score, jnp.float32),
        jnp.zeros((H, tok_rows), jnp.float32),
        jnp.zeros((H, tok_rows, HD), jnp.float32),
    )
    state = initial
    key_piece = lax.all_gather(key_low, "ctx", axis=0, tiled=True)
    value_piece = lax.all_gather(value_low, "ctx", axis=0, tiled=True)
    blocks = key_piece.shape[0] // tok_rows
    key_blocks = key_piece.reshape(blocks, tok_rows, model_width)
    value_blocks = value_piece.reshape(blocks, tok_rows, model_width)
    block_starts = tok_rows * lax.iota(jnp.int32, blocks)

    def one_block(inner, item):
        key_block, value_block, key_start = item
        return (attend_block(inner, key_block, value_block, key_start), None)

    state, unused = lax.scan(one_block, state, (key_blocks, value_blocks, block_starts))
    run_max, run_total, run_acc = state
    log_total = run_max + jnp.log(run_total)
    attended = jnp.transpose(run_acc / run_total[:, :, None], (1, 0, 2)).reshape(
        tok_rows, model_width
    )
    attended_low = attended.astype(jnp.bfloat16)
    branch = jnp.dot(
        attended_low, wout_full, preferred_element_type=jnp.float32
    ) + bout_full.astype(jnp.float32)
    hidden_sum = inputs + branch
    gain2_float = gain2.astype(jnp.float32)
    bias2_float = bias2.astype(jnp.float32)
    normed2 = layer_norm(hidden_sum, gain2_float, bias2_float).astype(jnp.bfloat16)
    pre_act = jnp.dot(normed2, wup_full, preferred_element_type=jnp.float32) + bup_full.astype(
        jnp.float32
    )
    activated = exact_gelu(pre_act).astype(jnp.bfloat16)
    mixed = (
        hidden_sum
        + jnp.dot(activated, wdown_full, preferred_element_type=jnp.float32)
        + bdown_full.astype(jnp.float32)
    )
    back_gain1 = gathered[0].astype(jnp.float32)
    back_bias1 = gathered[1].astype(jnp.float32)
    back_wqkv = gathered[2]
    back_wout = gathered[4]
    back_gain2 = gathered[6].astype(jnp.float32)
    back_bias2 = gathered[7].astype(jnp.float32)
    back_wup = gathered[8]
    back_wdown = gathered[10]
    out_grad = cotangent[0]
    wdown_grad = jnp.einsum("tf,td->fd", activated, out_grad, preferred_element_type=jnp.float32)
    bdown_grad = jnp.sum(out_grad.astype(jnp.float32), axis=0)
    act_grad = jnp.einsum("td,fd->tf", out_grad, back_wdown, preferred_element_type=jnp.float32)
    unused_act, gelu_back = jax.vjp(exact_gelu, pre_act)
    pre_grad = gelu_back(act_grad)[0].astype(jnp.bfloat16)
    wup_grad = jnp.einsum("tc,tf->cf", normed2, pre_grad, preferred_element_type=jnp.float32)
    bup_grad = jnp.sum(pre_grad.astype(jnp.float32), axis=0)
    normed2_grad = jnp.einsum("tf,cf->tc", pre_grad, back_wup, preferred_element_type=jnp.float32)
    unused_norm2, norm2_back = jax.vjp(layer_norm, hidden_sum, back_gain2, back_bias2)
    hidden_part, gain2_grad, bias2_grad = norm2_back(normed2_grad)
    hidden_grad = out_grad.astype(jnp.float32) + hidden_part
    branch_grad = hidden_grad.astype(jnp.bfloat16)
    wout_grad = jnp.einsum(
        "tc,td->cd", attended_low, branch_grad, preferred_element_type=jnp.float32
    )
    bout_grad = jnp.sum(branch_grad.astype(jnp.float32), axis=0)
    attended_grad = jnp.einsum(
        "td,cd->tc", branch_grad, back_wout, preferred_element_type=jnp.float32
    ).astype(jnp.bfloat16)
    delta = jnp.sum(
        (attended_grad.astype(jnp.float32) * attended).reshape(tok_rows, H, HD), axis=2
    ).T
    grad_heads = attended_grad.reshape(tok_rows, H, HD)

    def back_block(state, anchor):
        key_start = anchor * tok_rows
        key_cur, value_cur, key_grad, value_grad, query_grad = state
        key_docs = doc_index(key_start + row_offsets, doc_starts)
        same_doc = (query_docs[:, None] == key_docs[None, :])[None]
        key_heads = key_cur.reshape(tok_rows, H, HD)
        scores = (
            jnp.einsum("qhd,khd->hqk", query_heads, key_heads, preferred_element_type=jnp.float32)
            * 0.125
        )
        probs = jnp.where(same_doc, jnp.exp(scores - log_total[:, :, None]), 0.0)
        value_grad = value_grad + jnp.einsum(
            "hqk,qhd->khd",
            probs.astype(jnp.bfloat16),
            grad_heads,
            preferred_element_type=jnp.float32,
        ).reshape(tok_rows, model_width)
        prob_grad = jnp.einsum(
            "qhd,khd->hqk",
            grad_heads,
            value_cur.reshape(tok_rows, H, HD),
            preferred_element_type=jnp.float32,
        )
        score_grad = (probs * (prob_grad - delta[:, :, None])).astype(jnp.bfloat16)
        query_grad = (
            query_grad
            + jnp.einsum(
                "hqk,khd->qhd", score_grad, key_heads, preferred_element_type=jnp.float32
            ).reshape(tok_rows, model_width)
            * 0.125
        )
        key_grad = (
            key_grad
            + jnp.einsum(
                "hqk,qhd->khd", score_grad, query_heads, preferred_element_type=jnp.float32
            ).reshape(tok_rows, model_width)
            * 0.125
        )
        return (key_cur, value_cur, key_grad, value_grad, query_grad)

    def pass_on(state):
        key_cur, value_cur, key_grad, value_grad, query_grad = state
        moved_keys = shifted_2((key_cur, value_cur), "ctx", 1)
        moved_sums = (
            shifted_2(key_grad.astype(jnp.bfloat16), "ctx", 1).astype(key_grad.dtype),
            shifted_2(value_grad.astype(jnp.bfloat16), "ctx", 1).astype(value_grad.dtype),
        )
        return (moved_keys[0], moved_keys[1], moved_sums[0], moved_sums[1], query_grad)

    def two_steps(turn, state):
        state = pass_on(back_block(state, (ctx_place - 2 * turn) % ctx_size))
        state = pass_on(back_block(state, (ctx_place - 2 * turn - 1) % ctx_size))
        return state

    zero_rows = jnp.zeros((tok_rows, model_width), jnp.float32)
    final_state = lax.fori_loop(
        0, ctx_size // 2, two_steps, (key_low, value_low, zero_rows, zero_rows, zero_rows)
    )
    key_grad_low = final_state[2].astype(jnp.bfloat16)
    value_grad_low = final_state[3].astype(jnp.bfloat16)
    query_grad_low = final_state[4].astype(jnp.bfloat16)
    projected_grad = jnp.concatenate([query_grad_low, key_grad_low, value_grad_low], axis=1)
    wqkv_grad = jnp.einsum("tc,te->ce", normed1, projected_grad, preferred_element_type=jnp.float32)
    bqv_grad = jnp.concatenate(
        [
            jnp.sum(query_grad_low.astype(jnp.float32), axis=0),
            jnp.sum(value_grad_low.astype(jnp.float32), axis=0),
        ]
    )
    normed1_grad = jnp.einsum(
        "te,ce->tc", projected_grad, back_wqkv, preferred_element_type=jnp.float32
    )
    unused_norm1, norm1_back = jax.vjp(layer_norm, inputs, back_gain1, back_bias1)
    input_part, gain1_grad, bias1_grad = norm1_back(normed1_grad)
    inputs_grad = hidden_grad + input_part
    shares = (
        lax.psum_scatter(
            gain1_grad.astype(jnp.bfloat16), "wsh", scatter_dimension=0, tiled=True
        ).astype(jnp.float32),
        lax.psum_scatter(
            bias1_grad.astype(jnp.bfloat16), "wsh", scatter_dimension=0, tiled=True
        ).astype(jnp.float32),
        lax.psum_scatter(
            wqkv_grad.astype(jnp.bfloat16), "wsh", scatter_dimension=0, tiled=True
        ).astype(jnp.float32),
        lax.psum_scatter(
            bqv_grad.astype(jnp.bfloat16), "wsh", scatter_dimension=0, tiled=True
        ).astype(jnp.float32),
        lax.psum_scatter(
            wout_grad.astype(jnp.bfloat16), "wsh", scatter_dimension=0, tiled=True
        ).astype(jnp.float32),
        lax.psum_scatter(
            bout_grad.astype(jnp.bfloat16), "wsh", scatter_dimension=0, tiled=True
        ).astype(jnp.float32),
        lax.psum_scatter(
            gain2_grad.astype(jnp.bfloat16), "wsh", scatter_dimension=0, tiled=True
        ).astype(jnp.float32),
        lax.psum_scatter(
            bias2_grad.astype(jnp.bfloat16), "wsh", scatter_dimension=0, tiled=True
        ).astype(jnp.float32),
        lax.psum_scatter(
            wup_grad.astype(jnp.bfloat16), "wsh", scatter_dimension=0, tiled=True
        ).astype(jnp.float32),
        lax.psum_scatter(
            bup_grad.astype(jnp.bfloat16), "wsh", scatter_dimension=0, tiled=True
        ).astype(jnp.float32),
        lax.psum_scatter(
            wdown_grad.astype(jnp.bfloat16), "wsh", scatter_dimension=0, tiled=True
        ).astype(jnp.float32),
        lax.psum_scatter(
            bdown_grad.astype(jnp.bfloat16), "wsh", scatter_dimension=0, tiled=True
        ).astype(jnp.float32),
    )
    totals = (
        lax.psum(shares[0].astype(jnp.bfloat16), "ctx").astype(jnp.float32),
        lax.psum(shares[1].astype(jnp.bfloat16), "ctx").astype(jnp.float32),
        lax.psum(shares[2].astype(jnp.bfloat16), "ctx").astype(jnp.float32),
        lax.psum(shares[3].astype(jnp.bfloat16), "ctx").astype(jnp.float32),
        lax.psum(shares[4].astype(jnp.bfloat16), "ctx").astype(jnp.float32),
        lax.psum(shares[5].astype(jnp.bfloat16), "ctx").astype(jnp.float32),
        lax.psum(shares[6].astype(jnp.bfloat16), "ctx").astype(jnp.float32),
        lax.psum(shares[7].astype(jnp.bfloat16), "ctx").astype(jnp.float32),
        lax.psum(shares[8].astype(jnp.bfloat16), "ctx").astype(jnp.float32),
        lax.psum(shares[9].astype(jnp.bfloat16), "ctx").astype(jnp.float32),
        lax.psum(shares[10].astype(jnp.bfloat16), "ctx").astype(jnp.float32),
        lax.psum(shares[11].astype(jnp.bfloat16), "ctx").astype(jnp.float32),
    )
    return (
        mixed.astype(jnp.bfloat16)[None],
        inputs_grad[None],
        totals[0],
        totals[1],
        totals[2],
        totals[3],
        totals[4],
        totals[5],
        totals[6],
        totals[7],
        totals[8],
        totals[9],
        totals[10],
        totals[11],
    )


def solution(mesh):
    as_planned = mesh.shape["ctx"] == GROUPS * PEERS and mesh.shape["wsh"] == 2
    return jax.shard_map(
        body if as_planned else any_mesh_body,
        mesh=mesh,
        in_specs=(
            P("wsh", "ctx", None),
            P("wsh", None),
            P("wsh"),
            P("wsh"),
            P("wsh", None),
            P("wsh"),
            P("wsh", None),
            P("wsh"),
            P("wsh"),
            P("wsh"),
            P("wsh", None),
            P("wsh"),
            P("wsh", None),
            P("wsh"),
            P("wsh", "ctx", None),
        ),
        out_specs=(
            P("wsh", "ctx", None),
            P("wsh", "ctx", None),
            P("wsh"),
            P("wsh"),
            P("wsh", None),
            P("wsh"),
            P("wsh", None),
            P("wsh"),
            P("wsh"),
            P("wsh"),
            P("wsh", None),
            P("wsh"),
            P("wsh", None),
            P("wsh"),
        ),
        check_vma=False,
    )
```

profile of v0, /device:TPU:1, one launch (start us, length us, event | category | flops | bytes accessed | tf_op | source)
XLA Modules:
  0.0 401.8 jit_solution(7065748979990218260)
XLA Ops:
  0.8 2.4 constant_dynamic-slice_fusion
  3.2 2.1 collective-permute-start
  8.3 1.7 copy-done.4
  9.9 1.5 copy-done.5
  11.4 1.1 copy-done.10
  12.5 55.0 %gather_weights.1 = (bf16[2,384,2304]{2,1,0:T(8,128)(2,1)S(1)}, bf16[2,384,768]{2,1,0:T(8,128)(2,1)S(1)}, bf16[2,384,3072]{2,1,0:T(8,128)(2,1)S(1)}, f32[2,40,128]{2,1,0:T(8,128)S(1)}) custom-call(bf16[384,2304]{1,0:T(8,128)(2,1)S(1)} %copy-done.5, bf16[384,768]{1,0:T(8,128)(2,1)S(1)} %copy-done.10, bf16[384,3072]{1,0:T(8,128)(2,1)S(1)} %copy-done.4, ...), custom_call_target="tpu_custom_call" | custom-call | tf_op jit(solution)/shard_map/gather_weights/pallas_call | solution.py:135
  67.5 2.2 copy-done.1
  72.5 1.3 sub.72
  73.8 1.4 convert_reduce_fusion.3
  75.7 1.3 copy.60
  77.0 1.3 copy.61
  79.7 1.2 add_bitcast_fusion.2
  80.9 1.3 copy.67
  82.2 1.3 copy.68
  85.0 1.3 gather_fusion.1
  86.2 1.2 add_bitcast_fusion
  87.4 1.1 convert_reduce_fusion
  89.1 1.2 fusion.5
  92.4 3.2 fusion
  98.4 1.6 copy.74
  100.1 30.9 %spread_heads.1 = (bf16[4,192,256]{2,1,0:T(8,128)(2,1)S(1)}, bf16[16,384,256]{2,1,0:T(8,128)(2,1)S(1)}) custom-call(bf16[4,576,256]{2,1,0:T(8,128)(2,1)S(1)} %bitcast.65), custom_call_target="tpu_custom_call" | custom-call | tf_op jit(solution)/shard_map/spread_heads/pallas_call | solution.py:213
  131.5 35.8 %attend.1 = (f32[4,192,256]{2,1,0:T(8,128)S(1)}, bf16[4,192,256]{2,1,0:T(8,128)(2,1)S(1)}, f32[4,8,256]{2,1,0:T(8,128)S(1)}) custom-call(s32[4,2]{1,0:T(4,128)S(1)} %pad_add_fusion.spans, bf16[4,192,256]{2,1,0:T(8,128)(2,1)S(1)} %get-tuple-element.40.query, bf16[16,384,256]{2,1,0:T(8,128)(2,1)S(1)} %get-tuple-element.41.keys, ...), custom_call_target="tpu_custom_call" | custom-call | tf_op jit(solution)/shard_map/attend/pallas_call | solution.py:985
  169.6 38.8 %middle.1 = (bf16[256,768]{1,0:T(8,128)(2,1)}, f32[256,768]{1,0:T(8,128)}, bf16[4,192,256]{2,1,0:T(8,128)(2,1)}, bf16[4,384,384]{2,1,0:T(8,128)(2,1)}, bf16[5,38...) custom-call(bf16[4,192,256]{2,1,0:T(8,128)(2,1)} %copy-done.11, ...), custom_call_target="tpu_custom_call" | custom-call | tf_op jit(solution)/shard_map/middle/pallas_call | solution.py:508
  209.5 40.4 %attend_back.1 = (bf16[4,192,256]{2,1,0:T(8,128)(2,1)}, bf16[16,384,256]{2,1,0:T(8,128)(2,1)}) custom-call(s32[4,2]{1,0:T(4,128)} %copy-done.14, bf16[4,192,256]{2,1,0:T(8,128)(2,1)} %copy-done.6, bf16[16,384,256]{2,1,0:T(8,128)(2,1)} %copy-done, bf16[16,64,256]{2,1,0:T(8,128)(2,1)} %copy-done.2, bf16[4,64,256]{2,1,0:T(8,128)(2,1)} %copy-done.8, ...), custom_call_target="tpu_custom_call" | custom-call | tf_op jit(solution)/shard_map/attend_back/pallas_call | solution.py:1099
  250.9 135.1 %last.1 = (f32[256,768]{1,0:T(8,128)}, bf16[1536,768]{1,0:T(8,128)(2,1)}, bf16[384,3072]{1,0:T(8,128)(2,1)}, bf16[384,768]{1,0:T(8,128)(2,1)}, bf16[384,2304]{1,0:T(8,128)(2,1)}, /*index=5*/f32[40,128]{1,0:T(8,128)}) custom-call(bf16[4,192,256]{2,1,0:T(8,128)(2,1)} %get-tuple-element.49.query_grad, bf16[16,384,256]{2,1,0:T(8,128)(2,1)} %get-tuple-element.50.key_grad, ...), custom_call_target="tpu_custom_call" | custom-call | tf_op jit(solution)/shard_map/last/pallas_call | solution.py:886
  386.0 1.4 slice_bitcast_fusion.4
  387.3 1.3 slice_bitcast_fusion
  388.7 1.3 slice_bitcast_fusion.1
  389.9 4.6 %convert_element_type.66 = f32[384,3072]{1,0:T(8,128)} convert(bf16[384,3072]{1,0:T(8,128)(2,1)} %get-tuple-element.60) | non-fusion elementwise | flops 1179648 | bytes 7077888 | tf_op jit(solution)/shard_map/convert_element_type | solution.py:1233
  394.5 2.5 convert_element_type.67
  397.1 2.0 convert_element_type.64
  399.1 1.1 convert_element_type.65
  (117 shorter events, 21.1 us)
Async XLA Ops:
  0.6 5.1 %copy-start.35 = (s32[1,8]{1,0:T(1,128)S(1)}, s32[1,8]{1,0:T(1,128)}, u32[]{:S(2)}) copy-start(s32[1,8]{1,0:T(1,128)} %param.16) | copy-start | bytes 100
  0.7 5.8 %copy-start.28 = (bf16[384]{0:T(512)(128)(2,1)S(1)}, bf16[384]{0:T(512)(128)(2,1)}, u32[]{:S(2)}) copy-start(bf16[384]{0:T(512)(128)(2,1)} %param.17) | copy-start | bytes 2308
  0.7 6.0 %copy-start.29 = (bf16[384]{0:T(512)(128)(2,1)S(1)}, bf16[384]{0:T(512)(128)(2,1)}, u32[]{:S(2)}) copy-start(bf16[384]{0:T(512)(128)(2,1)} %param.18) | copy-start | bytes 2308
  0.7 6.3 %copy-start.27 = (bf16[768]{0:T(1024)(128)(2,1)S(1)}, bf16[768]{0:T(1024)(128)(2,1)}, u32[]{:S(2)}) copy-start(bf16[768]{0:T(1024)(128)(2,1)} %param.20) | copy-start | bytes 4612
  0.7 6.5 %copy-start.30 = (bf16[384]{0:T(512)(128)(2,1)S(1)}, bf16[384]{0:T(512)(128)(2,1)}, u32[]{:S(2)}) copy-start(bf16[384]{0:T(512)(128)(2,1)} %param.22) | copy-start | bytes 2308
  0.7 6.7 %copy-start.31 = (bf16[384]{0:T(512)(128)(2,1)S(1)}, bf16[384]{0:T(512)(128)(2,1)}, u32[]{:S(2)}) copy-start(bf16[384]{0:T(512)(128)(2,1)} %param.23) | copy-start | bytes 2308
  0.7 6.9 %copy-start.32 = (bf16[384]{0:T(512)(128)(2,1)S(1)}, bf16[384]{0:T(512)(128)(2,1)}, u32[]{:S(2)}) copy-start(bf16[384]{0:T(512)(128)(2,1)} %param.24) | copy-start | bytes 2308
  0.7 7.1 %copy-start.25 = (bf16[1536]{0:T(1024)(128)(2,1)S(1)}, bf16[1536]{0:T(1024)(128)(2,1)}, u32[]{:S(2)}) copy-start(bf16[1536]{0:T(1024)(128)(2,1)} %param.26) | copy-start | bytes 9220
  0.7 7.3 %copy-start.33 = (bf16[384]{0:T(512)(128)(2,1)S(1)}, bf16[384]{0:T(512)(128)(2,1)}, u32[]{:S(2)}) copy-start(bf16[384]{0:T(512)(128)(2,1)} %param.28) | copy-start | bytes 2308
  3.2 166.4 %collective-permute-start = (bf16[768,768]{1,0:T(8,128)(2,1)}, bf16[768,768]{1,0:T(8,128)(2,1)}, u32[]{:S(2)}, u32[]{:S(2)}) collective-permute-start(bf16[768,768]{1,0:T(8,128)(2,1)} %constant_dynamic-slice_fusion), channel_id=1, source_target_pairs={{0,1},{1,0},{2,3},{3,2},{4,5},{5,4},{6,7},{7,6},{8,9},{9,8},{10,11... | collective-permute-start | bytes 3538952 | tf_op jit(solution)/shard_map/ppermute | solution.py:1188
  8.3 1.7 copy-start.4
  9.9 1.5 copy-start.5
  11.4 1.1 copy-start.10
  12.5 58.8 %copy-start.26 = (s32[8]{0:T(128)S(1)}, s32[8]{0:T(128)}, u32[]{:S(2)}) copy-start(s32[8]{0:T(128)} %fusion.22) | copy-start | bytes 100
  67.5 2.2 copy-start.1
  69.7 1.0 copy-start.7
  70.7 24.9 %copy-start.3 = (bf16[2,384,2304]{2,1,0:T(8,128)(2,1)}, bf16[2,384,2304]{2,1,0:T(8,128)(2,1)S(1)}, u32[]{:S(2)}) copy-start(bf16[2,384,2304]{2,1,0:T(8,128)(2,1)S(1)} %get-tuple-element.39) | copy-start | bytes 10616836
  100.0 31.1 %copy-start.34 = (pred[64]{0:T(512)(128)(4,1)S(1)}, pred[64]{0:T(512)(128)(4,1)}, u32[]{:S(2)}) copy-start(pred[64]{0:T(512)(128)(4,1)} %iota_compare_fusion.3) | copy-start | bytes 196
  131.0 36.3 %copy-start = (bf16[16,384,256]{2,1,0:T(8,128)(2,1)}, bf16[16,384,256]{2,1,0:T(8,128)(2,1)S(1)}, u32[]{:S(2)}) copy-start(bf16[16,384,256]{2,1,0:T(8,128)(2,1)S(1)} %get-tuple-element.41.keys) | copy-start | bytes 9437188
  131.0 36.3 %copy-start.6 = (bf16[4,192,256]{2,1,0:T(8,128)(2,1)}, bf16[4,192,256]{2,1,0:T(8,128)(2,1)S(1)}, u32[]{:S(2)}) copy-start(bf16[4,192,256]{2,1,0:T(8,128)(2,1)S(1)} %get-tuple-element.40.query) | copy-start | bytes 1179652
  131.1 36.2 %copy-start.14 = (s32[4,2]{1,0:T(4,128)}, s32[4,2]{1,0:T(4,128)S(1)}, u32[]{:S(2)}) copy-start(s32[4,2]{1,0:T(4,128)S(1)} %pad_add_fusion.spans) | copy-start | bytes 100
  131.2 36.1 %copy-start.8 = (bf16[4,64,256]{2,1,0:T(8,128)(2,1)}, bf16[4,64,256]{2,1,0:T(8,128)(2,1)S(1)}, u32[]{:S(2)}) copy-start(bf16[4,64,256]{2,1,0:T(8,128)(2,1)S(1)} %select_convert_fusion.veto) | copy-start | bytes 393220
  131.5 76.9 %copy-start.2 = (bf16[16,64,256]{2,1,0:T(8,128)(2,1)}, bf16[16,64,256]{2,1,0:T(8,128)(2,1)S(1)}, u32[]{:S(2)}) copy-start(bf16[16,64,256]{2,1,0:T(8,128)(2,1)S(1)} %fusion.2.marks) | copy-start | bytes 1572868
  169.5 38.9 %copy-start.15 = (bf16[1,256,768]{2,1,0:T(8,128)(2,1)S(1)}, bf16[1,256,768]{2,1,0:T(8,128)(2,1)}, u32[]{:S(2)}) copy-start(bf16[1,256,768]{2,1,0:T(8,128)(2,1)} %param.15) | copy-start | bytes 1179652
  169.5 38.9 %copy-start.23 = (f32[256]{0:T(256)S(1)}, f32[256]{0:T(256)}, u32[]{:S(2)}) copy-start(f32[256]{0:T(256)} %copy-done.22) | copy-start | bytes 3076
  169.6 38.9 %copy-start.24 = (f32[256]{0:T(256)S(1)}, f32[256]{0:T(256)}, u32[]{:S(2)}) copy-start(f32[256]{0:T(256)} %add_rsqrt_fusion) | copy-start | bytes 3076
  208.4 41.5 %collective-permute-start.1 = (bf16[4,384,384]{2,1,0:T(8,128)(2,1)}, bf16[4,384,384]{2,1,0:T(8,128)(2,1)S(1)}, u32[]{:S(2)}, u32[]{:S(2)}) collective-permute-start(bf16[4,384,384]{2,1,0:T(8,128)(2,1)} %get-tuple-element.52), channel_id=1, source_target_pairs={{0,4},{2,6},{4,0},{6,2},{8,12},{10,14},{12,8},{14,10},{16,20},{18,... | collective-permute-start | bytes 3538952 | tf_op jit(solution)/shard_map/ppermute | solution.py:1213
  389.9 4.6 %copy-start.16 = (bf16[1536,768]{1,0:T(8,128)(2,1)S(1)}, bf16[1536,768]{1,0:T(8,128)(2,1)}, u32[]{:S(2)}) copy-start(bf16[1536,768]{1,0:T(8,128)(2,1)} %get-tuple-element.61) | copy-start | bytes 7077892
  394.5 2.5 copy-start.17
  397.1 2.0 copy-start.20
  397.1 3.1 copy-start.21
  399.1 1.8 copy-start.19
  (6 other events, 4.4 us)
where the time goes:
time: 400 us; the launch traced here: 402 us
  Pallas kernels  336 us (84%)
  local copies, waits for them, and re-layouts  34.3 us (9%)
  other arithmetic  25.3 us (6%)
    pallas_call x1, Pallas kernels, last(): pl.pallas_call(functools.partial(last_kernel, pack, firsts, tiles), out_s...  135 us
    pallas_call x1, Pallas kernels, gather_weights(): pl.pallas_call(functools.partial(weights_kernel, count, pieces), out_shap...  55 us
    pallas_call x1, Pallas kernels, attend_back(): pl.pallas_call(attend_back_kernel, out_shape=[jax.ShapeDtypeStruct(query....  40.4 us
    pallas_call x1, Pallas kernels, middle(): pl.pallas_call(functools.partial(middle_kernel, pack, firsts), out_shape=...  38.8 us
    pallas_call x1, Pallas kernels, attend(): pl.pallas_call(attend_kernel, out_shape=[jax.ShapeDtypeStruct(query.shape...  35.8 us
    pallas_call x1, Pallas kernels, spread_heads(): pl.pallas_call(spread_kernel, out_shape=[jax.ShapeDtypeStruct((groups, wi...  30.9 us
    unnamed x82, local copies, waits for them, and re-layouts  14.5 us
  transfers between devices with their start and end apart: 2, of which 0 were waited for; matrix products, arithmetic and copies ran while one was open for 8% of the time, Pallas kernels for 40%

commit v1 on v0

--- a/solution.py
+++ b/solution.py
@@ -54,176 +54,6 @@
     pl.semaphore_wait(barrier, len(devices))
 
 
-def weight_pieces(shapes, most):
-    pieces = []
-    for index, (rows, columns) in enumerate(shapes):
-        quarter = rows // PEERS
-        step = quarter
-        while step * columns * 2 > most and step % 32 == 0:
-            step //= 2
-        pieces += [(index, first, step) for first in range(0, quarter, step)]
-    return pieces
-
-
-def weights_kernel(count, pieces, *refs):
-    halves, fulls = refs[: count + 1], refs[count + 1 : 2 * count + 2]
-    local, ysend, yrecv, xsend, xrecv, csend, crecv, fsend, frecv, small_sem = refs[2 * count + 2 :]
-    z, x, core, y = here()
-    over_y, over_x, over_core = at(z, x, core, 1 - y), at(z, 1 - x, core, y), at(z, x, 1 - core, y)
-    greet([over_y, over_x, over_core])
-    small = remote(halves[count], fulls[count].at[y], small_sem.at[0], small_sem.at[1], over_y)
-    small.start()
-    own = [
-        pltpu.make_async_copy(halves[i], fulls[i].at[y], local.at[i]) for i in range(count + 1)
-    ]
-
-    def spot(piece, px, pcore):
-        index, first, rows = piece
-        quarter = fulls[index].shape[1] // PEERS
-        return pl.ds((px * 2 + pcore) * quarter + first, rows)
-
-    sends = []
-    for k, piece in enumerate(pieces):
-        index = piece[0]
-        rows = spot(piece, x, core)
-        copy = remote(
-            halves[index].at[rows], fulls[index].at[y, rows], ysend.at[k], yrecv.at[k], over_y
-        )
-        copy.start()
-        sends.append(copy)
-    for copy in own:
-        copy.start()
-
-    def landing(k, px, pcore, sem):
-        index = pieces[k][0]
-        view = fulls[index].at[1 - y, spot(pieces[k], px, pcore)]
-        return remote(view, view, sem, sem, over_core)
-
-    def forward(k, px, pcore, send, recv, device):
-        index = pieces[k][0]
-        view = fulls[index].at[1 - y, spot(pieces[k], px, pcore)]
-        copy = remote(view, view, send.at[k], recv.at[k], device)
-        copy.start()
-        sends.append(copy)
-
-    total = len(pieces)
-    for k in range(total + 1):
-        if k < total:
-            landing(k, x, core, yrecv.at[k]).wait_recv()
-            forward(k, x, core, xsend, xrecv, over_x)
-            forward(k, x, core, csend, crecv, over_core)
-        if k >= 1:
-            landing(k - 1, 1 - x, core, xrecv.at[k - 1]).wait_recv()
-            forward(k - 1, 1 - x, core, fsend, frecv, over_core)
-    for k in range(total):
-        landing(k, x, 1 - core, crecv.at[k]).wait_recv()
-        landing(k, 1 - x, 1 - core, frecv.at[k]).wait_recv()
-    small.wait()
-    for copy in own:
-        copy.wait()
-    for copy in sends:
-        copy.wait_send()
-
-
-def gather_weights(halves, small):
-    pieces = weight_pieces([half.shape for half in halves], 320 * 1024)
-    count, total = len(halves), len(pieces)
-    everything = list(halves) + [small]
-    anywhere = pl.BlockSpec(memory_space=pltpu.HBM)
-    sems = [pltpu.SemaphoreType.DMA((count + 1,))]
-    sems += [pltpu.SemaphoreType.DMA((total,))] * 8 + [pltpu.SemaphoreType.DMA((2,))]
-    return pl.pallas_call(
-        functools.partial(weights_kernel, count, pieces),
-        out_shape=[jax.ShapeDtypeStruct((2,) + a.shape, a.dtype) for a in everything],
-        in_specs=[anywhere] * (count + 1),
-        out_specs=[anywhere] * (count + 1),
-        scratch_shapes=sems,
-        compiler_params=params(16, 1),
-        name="gather_weights",
-    )(*everything)
-
-
-def spread_kernel(mine, query, keys, local, zsend, zrecv, xsend, xrecv, csend, crecv, fsend, frecv):
-    z, x, core, y = here()
-    width = query.shape[1]
-    over_x, over_core = at(z, 1 - x, core, y), at(z, x, 1 - core, y)
-    around = [at((z + d) % GROUPS, x, core, y) for d in range(1, GROUPS)]
-    greet(around + [over_x, over_core])
-    sends = []
-
-    def go(src, dst, send, recv, device):
-        copy = remote(src, dst, send, recv, device)
-        copy.start()
-        sends.append(copy)
-
-    def block(pz, px, pcore):
-        return keys.at[pz * PEERS + px * 2 + pcore]
-
-    own_query = pltpu.make_async_copy(mine.at[z, pl.ds(0, width)], query.at[z], local.at[0])
-    own_keys = pltpu.make_async_copy(
-        mine.at[z, pl.ds(width, 2 * width)], block(z, x, core), local.at[1]
-    )
-    own_keys.start()
-    own_query.start()
-    for d in (2, 1, 3):
-        target = (z + d) % GROUPS
-        src = mine.at[target, pl.ds(width, 2 * width)]
-        go(src, block(z, x, core), zsend.at[d], zrecv.at[d], around[d - 1])
-    for d in (2, 1, 3):
-        target = (z + d) % GROUPS
-        src = mine.at[target, pl.ds(0, width)]
-        go(src, query.at[z], zsend.at[GROUPS + d], zrecv.at[GROUPS + d], around[d - 1])
-    order = (0, 3, 1, 2)
-    for step in range(GROUPS + 1):
-        if step < GROUPS:
-            d = order[step]
-            pz = (z + GROUPS - d) % GROUPS
-            view = block(pz, x, core)
-            if d == 0:
-                own_keys.wait()
-            else:
-                remote(view, view, zsend.at[d], zrecv.at[d], over_x).wait_recv()
-            go(view, view, xsend.at[d], xrecv.at[d], over_x)
-            go(view, view, csend.at[d], crecv.at[d], over_core)
-        if step >= 1:
-            d = order[step - 1]
-            view = block((z + GROUPS - d) % GROUPS, 1 - x, core)
-            remote(view, view, xsend.at[d], xrecv.at[d], over_x).wait_recv()
-            go(view, view, fsend.at[d], frecv.at[d], over_core)
-    for d in range(GROUPS):
-        pz = (z + GROUPS - d) % GROUPS
-        near, far = block(pz, x, 1 - core), block(pz, 1 - x, 1 - core)
-        remote(near, near, csend.at[d], crecv.at[d], over_core).wait_recv()
-        remote(far, far, fsend.at[d], frecv.at[d], over_core).wait_recv()
-        if d > 0:
-            part = query.at[pz]
-            sem = GROUPS + d
-            remote(part, part, zsend.at[sem], zrecv.at[sem], over_x).wait_recv()
-    own_query.wait()
-    for copy in sends:
-        copy.wait_send()
-
-
-def spread_heads(projected):
-    groups, width, rows = projected.shape
-    width //= 3
-    anywhere = pl.BlockSpec(memory_space=pltpu.HBM)
-    sems = [pltpu.SemaphoreType.DMA((2,))] + [pltpu.SemaphoreType.DMA((2 * groups,))] * 2
-    sems += [pltpu.SemaphoreType.DMA((groups,))] * 6
-    return pl.pallas_call(
-        spread_kernel,
-        out_shape=[
-            jax.ShapeDtypeStruct((groups, width, rows), projected.dtype),
-            jax.ShapeDtypeStruct((groups * PEERS, 2 * width, rows), projected.dtype),
-        ],
-        in_specs=[anywhere],
-        out_specs=[anywhere] * 2,
-        scratch_shapes=sems,
-        compiler_params=params(16, 2),
-        name="spread_heads",
-    )(projected)
-
-
 def dot(left, right):
     return jnp.dot(left, right, preferred_element_type=jnp.float32)
 
@@ -267,8 +97,12 @@
         self.rows = row + -row % 8
 
     def pack(self, halves):
-        flat = jnp.concatenate([half.astype(jnp.float32) for half in halves])
-        return jnp.pad(flat.reshape(-1, LANES), ((0, self.rows - self.used), (0, 0)))
+        total, flat = self.rows * LANES, 0.0
+        for name, half in zip(self.names, halves):
+            start = self.starts[name] * LANES
+            after = total - start - half.shape[0]
+            flat += jnp.pad(half.astype(jnp.float32), (start, after))
+        return flat.reshape(-1, LANES)
 
     def read(self, ref, name, first=0, count=None):
         count = 2 * self.sizes[name] if count is None else count
@@ -306,6 +140,216 @@
     def finish(self):
         for copy in self.copies:
             copy.wait_send()
+
+
+def front_kernel(
+    pack,
+    patches,
+    small_half,
+    qkv_half,
+    out_half,
+    up_half,
+    down_half,
+    query,
+    keys,
+    normed_low,
+    small,
+    qkv_far,
+    out_far,
+    up_far,
+    down_part,
+    qkv_own,
+    staged,
+    local,
+    small_sem,
+    ysend,
+    yrecv,
+    xsend,
+    xrecv,
+    csend,
+    crecv,
+    fsend,
+    frecv,
+    psend,
+    precv,
+    nsend,
+    nrecv,
+    query_send,
+    query_recv,
+    zsend,
+    zrecv,
+    kxsend,
+    kxrecv,
+    kcsend,
+    kcrecv,
+    kfsend,
+    kfrecv,
+):
+    bf16 = jnp.bfloat16
+    z, x, core, y = here()
+    over_x, over_core, over_y = (
+        at(z, 1 - x, core, y),
+        at(z, x, 1 - core, y),
+        at(z, x, core, 1 - y),
+    )
+    around = [at((z + d) % GROUPS, x, core, y) for d in range(1, GROUPS)]
+    rows, width = patches.shape
+    part = query.shape[1]
+    half = qkv_half.shape[0]
+    quarter = half // PEERS
+    down = down_part.shape[0]
+    greet(around + [over_x, over_core, over_y])
+    go = Sender()
+
+    def landed(view, sem):
+        remote(view, view, sem, sem, over_core).wait_recv()
+
+    def columns(b):
+        return pl.ds(b * width, width)
+
+    def share(px, pcore, b):
+        return qkv_far.at[pl.ds((px * 2 + pcore) * quarter, quarter), columns(b)]
+
+    order = (1, 2, 0)
+    go(small_half, small.at[y], small_sem.at[0], small_sem.at[1], over_y)
+    for b in order:
+        src = qkv_half.at[pl.ds((x * 2 + core) * quarter, quarter), columns(b)]
+        go(src, share(x, core, b), ysend.at[b], yrecv.at[b], over_y)
+    copies = [
+        pltpu.make_async_copy(small_half, small.at[y], local.at[0]),
+        pltpu.make_async_copy(qkv_half, qkv_own, local.at[1]),
+        pltpu.make_async_copy(down_half.at[pl.ds(core * down, down)], down_part, local.at[2]),
+    ]
+    for copy in copies:
+        copy.start()
+
+    pieces = [(out_half, out_far, half // 2, 0)]
+    pieces += [(up_half, up_far, half // 8, first) for first in range(0, half // 2, half // 8)]
+
+    def piece_rows(k, pcore):
+        return pl.ds(pcore * (half // 2) + pieces[k][3], pieces[k][2])
+
+    for k, (src, full, count, first) in enumerate(pieces):
+        span = piece_rows(k, core)
+        go(src.at[span], full.at[span], psend.at[k], precv.at[k], over_y)
+
+    copies[0].wait()
+    landed(small.at[1 - y], small_sem.at[1])
+    normed, scale = normalise(patches[...].astype(jnp.float32))
+    low = (normed * pack.read(small, "gain1") + pack.read(small, "bias1")).astype(bf16)
+    normed_low[...] = low
+    low_own = jnp.where(y == 0, low[:, :half], low[:, half:])
+    low_far = jnp.where(y == 0, low[:, half:], low[:, :half])
+    for i, b in enumerate(order):
+        view = share(x, core, b)
+        landed(view, yrecv.at[b])
+        go(view, view, xsend.at[b], xrecv.at[b], over_x)
+        go(view, view, csend.at[b], crecv.at[b], over_core)
+    copies[1].wait()
+
+    def block(pz, px, pcore, b):
+        return keys.at[pz * PEERS + px * 2 + pcore, pl.ds((b - 1) * part, part)]
+
+    own = []
+    for i, b in enumerate(order):
+        view = share(1 - x, core, b)
+        landed(view, xrecv.at[b])
+        go(view, view, fsend.at[b], frecv.at[b], over_core)
+        landed(share(x, 1 - core, b), crecv.at[b])
+        landed(share(1 - x, 1 - core, b), frecv.at[b])
+        made = dot(low_own, qkv_own[:, b * width : (b + 1) * width])
+        made = made + dot(low_far, qkv_far[:, b * width : (b + 1) * width])
+        if b != 1:
+            made = made + pack.read(small, "bqv", (b // 2) * width, width)
+        staged[b] = made.astype(bf16).T.reshape(GROUPS, part, rows)
+        for d in (2, 1, 3):
+            target = (z + d) % GROUPS
+            if b == 0:
+                dst, sems = query.at[z], (query_send.at[d], query_recv.at[d])
+            else:
+                sem = (b - 1) * GROUPS + d
+                dst, sems = block(z, x, core, b), (zsend.at[sem], zrecv.at[sem])
+            go(staged.at[b, target], dst, sems[0], sems[1], around[d - 1])
+        dst = query.at[z] if b == 0 else block(z, x, core, b)
+        own.append(pltpu.make_async_copy(staged.at[b, z], dst, local.at[3 + i]))
+        own[-1].start()
+        if b > 0:
+            sem = (b - 1) * GROUPS
+            go(staged.at[b, z], dst, kxsend.at[sem], kxrecv.at[sem], over_x)
+            go(staged.at[b, z], dst, kcsend.at[sem], kcrecv.at[sem], over_core)
+
+    sequence = [(1, 0), (2, 0)] + [(b, d) for b in (1, 2) for d in (1, 3, 2)]
+    for i in range(len(sequence) + 1):
+        if i < len(sequence):
+            b, d = sequence[i]
+            sem = (b - 1) * GROUPS + d
+            if d > 0:
+                view = block((z + GROUPS - d) % GROUPS, x, core, b)
+                landed(view, zrecv.at[sem])
+                go(view, view, kxsend.at[sem], kxrecv.at[sem], over_x)
+                go(view, view, kcsend.at[sem], kcrecv.at[sem], over_core)
+        if i >= 1:
+            b, d = sequence[i - 1]
+            sem = (b - 1) * GROUPS + d
+            view = block((z + GROUPS - d) % GROUPS, 1 - x, core, b)
+            landed(view, kxrecv.at[sem])
+            go(view, view, kfsend.at[sem], kfrecv.at[sem], over_core)
+    for k, (src, full, count, first) in enumerate(pieces):
+        view = full.at[piece_rows(k, core)]
+        landed(view, precv.at[k])
+        go(view, view, nsend.at[k], nrecv.at[k], over_core)
+    for b, d in sequence:
+        sem = (b - 1) * GROUPS + d
+        pz = (z + GROUPS - d) % GROUPS
+        landed(block(pz, x, 1 - core, b), kcrecv.at[sem])
+        landed(block(pz, 1 - x, 1 - core, b), kfrecv.at[sem])
+    for d in range(1, GROUPS):
+        landed(query.at[(z + GROUPS - d) % GROUPS], query_recv.at[d])
+    for k, (src, full, count, first) in enumerate(pieces):
+        landed(full.at[piece_rows(k, 1 - core)], nrecv.at[k])
+    for copy in copies[2:] + own:
+        copy.wait()
+    go.finish()
+
+
+def front(pack, patches, small_half, qkv_half, out_half, up_half, down_half):
+    f32, bf16 = jnp.float32, jnp.bfloat16
+    vmem = pl.BlockSpec(memory_space=pltpu.VMEM)
+    hbm = pl.BlockSpec(memory_space=pltpu.HBM)
+    rows, width = patches.shape
+    part, half = width // GROUPS, qkv_half.shape[0]
+    dma = pltpu.SemaphoreType.DMA
+
+    def pair(n):
+        return [dma((n,))] * 2
+
+    return pl.pallas_call(
+        functools.partial(front_kernel, pack),
+        out_shape=[
+            jax.ShapeDtypeStruct((GROUPS, part, rows), bf16),
+            jax.ShapeDtypeStruct((GROUPS * PEERS, 2 * part, rows), bf16),
+            jax.ShapeDtypeStruct((rows, width), bf16),
+            jax.ShapeDtypeStruct((2,) + small_half.shape, f32),
+            jax.ShapeDtypeStruct(qkv_half.shape, bf16),
+            jax.ShapeDtypeStruct(out_half.shape, bf16),
+            jax.ShapeDtypeStruct(up_half.shape, bf16),
+            jax.ShapeDtypeStruct((down_half.shape[0] // 2, width), bf16),
+        ],
+        in_specs=[vmem, hbm, hbm, hbm, hbm, hbm],
+        out_specs=[vmem] * 8,
+        scratch_shapes=[
+            pltpu.VMEM(qkv_half.shape, bf16),
+            pltpu.VMEM((3, GROUPS, part, rows), bf16),
+            dma((6,)),
+        ]
+        + [dma((2,))]
+        + pair(3) * 4
+        + pair(5) * 2
+        + pair(GROUPS)
+        + pair(2 * GROUPS) * 4,
+        compiler_params=params(60, 1),
+        name="front",
+    )(patches, small_half, qkv_half, out_half, up_half, down_half)
 
 
 def split_rows(first, x, y, quarter):
@@ -338,7 +382,9 @@
     out_grad,
     small,
     w_out,
+    w_out_far,
     w_up,
+    w_up_far,
     w_down_half,
     w_down_far,
     mixed,
@@ -389,9 +435,13 @@
     ]
     copies = [
         pltpu.make_async_copy(heads.at[z], o_land.at[z], local.at[2]),
-        pltpu.make_async_copy(w_out, wout, local.at[3]),
-        pltpu.make_async_copy(w_up, wup, local.at[4]),
     ]
+    pairs = [(w_out, wout, y), (w_out_far, wout, 1 - y), (w_up, wup, y), (w_up_far, wup, 1 - y)]
+    for i, (src, dst, side) in enumerate(pairs):
+        count = src.shape[0]
+        span = pl.ds(side * count, count)
+        copies.append(pltpu.make_async_copy(src, dst.at[span], local.at[4 + i]))
+
     for copy in down_copies + copies:
         copy.start()
     dy = out_grad[...]
@@ -455,7 +505,7 @@
     o_grad[...] = dot_turned(wout[...], dz).astype(bf16).reshape(o_grad.shape)
     for d in (2, 1, 3):
         go(o_grad.at[(z + d) % GROUPS], grad_heads.at[z], gsend.at[d], grecv.at[d], around[d - 1])
-    own = pltpu.make_async_copy(o_grad.at[z], grad_heads.at[z], local.at[5])
+    own = pltpu.make_async_copy(o_grad.at[z], grad_heads.at[z], local.at[3])
     own.start()
 
     columns = c_land.shape[2]
@@ -496,9 +546,9 @@
     go.finish()
 
 
-def middle(pack, firsts, ahead, heads, patches, out_grad, small, w_out, w_up, w_down_half, w_down_far):
+def middle(pack, firsts, ahead, heads, patches, out_grad, small, *weights):
     rows, width = patches.shape
-    hidden = w_up.shape[1]
+    hidden = weights[2].shape[1]
     tiles = hidden // width
     count = 2 * tiles + 1
     f32, bf16 = jnp.float32, jnp.bfloat16
@@ -516,7 +566,7 @@
             jax.ShapeDtypeStruct((count, width // 2, width // 2), bf16),
             jax.ShapeDtypeStruct((2, pack.rows, LANES), f32),
         ],
-        in_specs=[hbm, vmem, vmem, vmem, hbm, hbm, hbm, hbm],
+        in_specs=[hbm, vmem, vmem, vmem] + [hbm] * 6,
         out_specs=[vmem] * 7,
         scratch_shapes=[
             pltpu.VMEM(heads.shape, bf16),
@@ -530,7 +580,7 @@
             pltpu.VMEM((tiles, 8, width), f32),
             pltpu.VMEM((count, width, width), bf16),
             pltpu.VMEM((count, width, width // 2), bf16),
-            dma((6,)),
+            dma((8,)),
             dma((GROUPS,)),
             dma((GROUPS,)),
             dma((GROUPS,)),
@@ -541,7 +591,7 @@
         ],
         compiler_params=params(60, 3),
         name="middle",
-    )(heads, patches, out_grad, small, w_out, w_up, w_down_half, w_down_far)
+    )(heads, patches, out_grad, small, *weights)
 
 
 class Totals:
@@ -579,6 +629,7 @@
     key_grad,
     normed_low,
     w_qkv,
+    w_qkv_far,
     patches,
     hidden_grad,
     small,
@@ -675,8 +726,13 @@
         go(query_grad.at[pz], got.at[z, pl.ds(0, part)], q_send.at[d], q_recv.at[d], around[d - 1])
     own_query = pltpu.make_async_copy(query_grad.at[z], got.at[z, pl.ds(0, part)], local.at[0])
     own_query.start()
-    weights = pltpu.make_async_copy(w_qkv, wqkv, local.at[2])
-    weights.start()
+    count = w_qkv.shape[0]
+    weights = [
+        pltpu.make_async_copy(w_qkv, wqkv.at[pl.ds(y * count, count)], local.at[2]),
+        pltpu.make_async_copy(w_qkv_far, wqkv.at[pl.ds((1 - y) * count, count)], local.at[3]),
+    ]
+    for copy in weights:
+        copy.start()
 
     def start_first(k, src):
         go(src, first_land.at[k], asend.at[k], arecv.at[k], peer[firsts[k]])
@@ -807,7 +863,8 @@
         landed(got.at[pz, pl.ds(part, 2 * part)], q_recv.at[GROUPS + d])
     own_query.wait()
     own_keys.wait()
-    weights.wait()
+    for copy in weights:
+        copy.wait()
 
     for k in range(early, chunks):
         i = k - early
@@ -867,7 +924,7 @@
 
 
 def last(
-    pack, firsts, query_grad, key_grad, normed_low, w_qkv, patches, hidden_grad, small,
+    pack, firsts, query_grad, key_grad, normed_low, w_qkv, w_qkv_far, patches, hidden_grad, small,
     landed_ahead, send_on, keep, vector
 ):
     f32, bf16 = jnp.float32, jnp.bfloat16
@@ -893,7 +950,7 @@
             jax.ShapeDtypeStruct((half, late * width), bf16),
             jax.ShapeDtypeStruct(vector.shape[1:], f32),
         ],
-        in_specs=[hbm, vmem, vmem, hbm, vmem, vmem, vmem, vmem, hbm, vmem, vmem],
+        in_specs=[hbm, vmem, vmem, hbm, hbm, vmem, vmem, vmem, vmem, hbm, vmem, vmem],
         out_specs=[vmem] * 6,
         scratch_shapes=[
             pltpu.VMEM((groups, 3 * part, rows), bf16),
@@ -901,7 +958,7 @@
             pltpu.VMEM((2 * groups,) + piece, bf16),
             pltpu.VMEM((groups,) + piece, bf16),
             pltpu.VMEM((groups,) + piece, bf16),
-            pltpu.VMEM(w_qkv.shape, bf16),
+            pltpu.VMEM((width, late * width), bf16),
             pltpu.VMEM((late, width, width), bf16),
             pltpu.VMEM((late, width, half), bf16),
             pltpu.VMEM((late, half, half), bf16),
@@ -914,7 +971,7 @@
             pltpu.VMEM((chunks, half // 8, half), bf16),
             pltpu.VMEM((4,) + vector.shape, f32),
             pltpu.VMEM((6,) + vector.shape, f32),
-            dma((3,)),
+            dma((4,)),
         ]
         + pair(2 * groups)
         + pair(groups)
@@ -928,18 +985,58 @@
         compiler_params=params(60, 4),
         name="last",
     )(
-        query_grad, key_grad, normed_low, w_qkv, patches, hidden_grad, small, landed_ahead, send_on,
-        keep, vector
-    )
-
-
-def attend_kernel(spans, query, keys, marks, veto, out, out_low, sums, key_rows, query_aug, acc, stat):
+        query_grad, key_grad, normed_low, w_qkv, w_qkv_far, patches, hidden_grad, small,
+        landed_ahead, send_on, keep, vector,
+    )
+
+
+class Documents:
+    def __init__(self, lengths, rows):
+        self.rows, self.count = rows, lengths.shape[1]
+        self.starts, self.ends, place = [], [], 0
+        for d in range(self.count):
+            self.starts.append(place)
+            place = place + lengths[0, d]
+            self.ends.append(place)
+
+    def span(self, block):
+        first, last = block * self.rows, (block + 1) * self.rows - 1
+        low, high = 0, 0
+        for d in range(self.count):
+            low = jnp.where(self.starts[d] <= first, self.starts[d], low)
+        for d in reversed(range(self.count)):
+            high = jnp.where(self.ends[d] > last, self.ends[d], high)
+        return low // self.rows, (high + self.rows - 1) // self.rows
+
+    def inside(self, block, yes, no):
+        shape = (8, self.rows)
+        row = lax.broadcasted_iota(jnp.int32, shape, 0)
+        place = block * self.rows + lax.broadcasted_iota(jnp.int32, shape, 1)
+        found = jnp.where(row < self.count, no, 0.0)
+        for d in range(self.count):
+            hit = (row == d) & (place >= self.starts[d]) & (place < self.ends[d])
+            found = jnp.where(hit, yes, found)
+        return found
+
+    def marks(self, block):
+        ones, rest = jnp.ones((8, self.rows)), jnp.zeros((HD - 16, self.rows))
+        return jnp.concatenate([self.inside(block, 1.0, 0.0), ones, rest]).astype(jnp.bfloat16)
+
+    def veto(self, block):
+        rest = jnp.zeros((HD - 8, self.rows))
+        return jnp.concatenate([self.inside(block, 0.0, masked_score), rest])
+
+
+def attend_kernel(
+    lengths, place, query, keys, out, out_low, sums, key_rows, query_aug, acc, stat
+):
     blocks, rows = keys.shape[0], keys.shape[2]
     width = query.shape[1]
     groups = query.shape[0]
+    documents = Documents(lengths, rows)
 
     def turn(j, carry):
-        mark = marks[j]
+        mark = documents.marks(j)
         for h in range(PER_GROUP):
             both = jnp.concatenate([keys[j, h * HD : (h + 1) * HD], mark], axis=0)
             key_rows[h, j] = both.T
@@ -947,9 +1044,11 @@
 
     lax.fori_loop(0, blocks, turn, 0)
     for i in range(groups):
+        block = i * PEERS + place[0]
+        veto = documents.veto(block).astype(jnp.bfloat16)
         for h in range(PER_GROUP):
             query_aug[h, :HD] = query[i, h * HD : (h + 1) * HD] * jnp.bfloat16(0.125)
-            query_aug[h, HD:] = veto[i]
+            query_aug[h, HD:] = veto
         stat[0] = jnp.full(stat.shape[1:], masked_score, jnp.float32)
         stat[1] = jnp.zeros(stat.shape[1:], jnp.float32)
         acc[...] = jnp.zeros(acc.shape, jnp.float32)
@@ -969,7 +1068,7 @@
                 acc[h] = acc[h] * factor + dot(values, probs.astype(jnp.bfloat16))
             return carry
 
-        lax.fori_loop(spans[i, 0], spans[i, 1], step, 0)
+        lax.fori_loop(*documents.span(block), step, 0)
         for h in range(PER_GROUP):
             total = stat[1, h : h + 1]
             shared = acc[h] / total
@@ -978,7 +1077,7 @@
             sums[i, h : h + 1] = stat[0, h : h + 1] + jnp.log(total)
 
 
-def attend(spans, query, keys, marks, veto):
+def attend(lengths, place, query, keys):
     groups, width, rows = query.shape
     blocks = keys.shape[0]
     vmem = pl.BlockSpec(memory_space=pltpu.VMEM)
@@ -989,7 +1088,7 @@
             jax.ShapeDtypeStruct(query.shape, jnp.bfloat16),
             jax.ShapeDtypeStruct((groups, 8, rows), jnp.float32),
         ],
-        in_specs=[pl.BlockSpec(memory_space=pltpu.SMEM)] + [vmem] * 4,
+        in_specs=[pl.BlockSpec(memory_space=pltpu.SMEM)] * 2 + [vmem] * 2,
         out_specs=[vmem] * 3,
         scratch_shapes=[
             pltpu.VMEM((PER_GROUP, blocks, rows, 2 * HD), jnp.bfloat16),
@@ -997,9 +1096,9 @@
             pltpu.VMEM((PER_GROUP, HD, rows), jnp.float32),
             pltpu.VMEM((2, 8, rows), jnp.float32),
         ],
-        compiler_params=params(40),
+        compiler_params=params(60),
         name="attend",
-    )(spans, query, keys, marks, veto)
+    )(lengths, place, query, keys)
 
 
 def three_parts(values):
@@ -1011,11 +1110,10 @@
 
 
 def attend_back_kernel(
-    spans,
+    lengths,
+    place,
     query,
     keys,
-    marks,
-    veto,
     out,
     sums,
     out_grad,
@@ -1034,9 +1132,10 @@
     width = query.shape[1]
     groups = query.shape[0]
     bf16 = jnp.bfloat16
+    documents = Documents(lengths, rows)
 
     def turn(j, carry):
-        mark = marks[j]
+        mark = documents.marks(j)
         for h in range(PER_GROUP):
             both = jnp.concatenate([keys[j, h * HD : (h + 1) * HD], mark], axis=0)
             key_rows[h, j] = both.T
@@ -1053,18 +1152,20 @@
         high, middle, low = three_parts(-values)
         wide = jnp.where(index == 8, high.astype(jnp.float32), 0.0)
         wide = jnp.where(index == 9, middle.astype(jnp.float32), wide)
-        return jnp.where(index == 10, low.astype(jnp.float32), wide).astype(bf16)
+        return jnp.where(index == 10, low.astype(jnp.float32), wide)
 
     for i in range(groups):
+        block = i * PEERS + place[0]
+        veto = documents.veto(block)
         for h in range(PER_GROUP):
             span = slice(h * HD, (h + 1) * HD)
             part = query[i, span] * bf16(0.125)
             grad = out_grad[i, span]
             delta = jnp.sum(grad.astype(jnp.float32) * out[i, span], axis=0, keepdims=True)
             query_aug[h, :HD] = part
-            query_aug[h, HD:] = veto[i] + spread(sums[i, h : h + 1])
+            query_aug[h, HD:] = (veto + spread(sums[i, h : h + 1])).astype(bf16)
             grad_aug[h, :HD] = grad
-            grad_aug[h, HD:] = spread(delta)
+            grad_aug[h, HD:] = spread(delta).astype(bf16)
             query_rows[h] = jnp.concatenate([part, none], axis=0).T
             grad_rows[h] = jnp.concatenate([none, grad], axis=0).T
         query_acc[...] = jnp.zeros(query_acc.shape, jnp.float32)
@@ -1077,7 +1178,7 @@
                 query_acc[h] += dot(keys[j, h * HD : (h + 1) * HD], change)
             return carry
 
-        lax.fori_loop(spans[i, 0], spans[i, 1], step, 0)
+        lax.fori_loop(*documents.span(block), step, 0)
         for h in range(PER_GROUP):
             query_grad[i, h * HD : (h + 1) * HD] = (query_acc[h] * 0.125).astype(bf16)
 
@@ -1091,7 +1192,7 @@
     lax.fori_loop(0, blocks, finish, 0)
 
 
-def attend_back(spans, query, keys, marks, veto, out, sums, out_grad):
+def attend_back(lengths, place, query, keys, out, sums, out_grad):
     groups, width, rows = query.shape
     blocks = keys.shape[0]
     vmem = pl.BlockSpec(memory_space=pltpu.VMEM)
@@ -1102,7 +1203,7 @@
             jax.ShapeDtypeStruct(query.shape, bf16),
             jax.ShapeDtypeStruct(keys.shape, bf16),
         ],
-        in_specs=[pl.BlockSpec(memory_space=pltpu.SMEM)] + [vmem] * 7,
+        in_specs=[pl.BlockSpec(memory_space=pltpu.SMEM)] * 2 + [vmem] * 5,
         out_specs=[vmem] * 2,
         scratch_shapes=[
             pltpu.VMEM((PER_GROUP, blocks, rows, 2 * HD), bf16),
@@ -1114,9 +1215,9 @@
             pltpu.VMEM((PER_GROUP, HD, rows), jnp.float32),
             pltpu.VMEM((PER_GROUP, blocks, rows, 2 * HD), jnp.float32),
         ],
-        compiler_params=params(56),
+        compiler_params=params(60),
         name="attend_back",
-    )(spans, query, keys, marks, veto, out, sums, out_grad)
+    )(lengths, place, query, keys, out, sums, out_grad)
 
 
 def layer_norm(values, gain, offset):
@@ -1133,26 +1234,6 @@
 def doc_index(positions, doc_starts):
     hits = (doc_starts[None, :] <= positions[:, None]).astype(jnp.int32)
     return jnp.sum(hits, axis=1) - 1
-
-
-def doc_tables(doc_lengths, ctx_place, blocks, rows):
-    bf16 = jnp.bfloat16
-    lengths = doc_lengths[0]
-    ends = jnp.cumsum(lengths)
-    starts = ends - lengths
-    count = lengths.shape[0]
-    docs = doc_index(jnp.arange(blocks * rows, dtype=jnp.int32), starts).reshape(blocks, 1, rows)
-    number = lax.broadcasted_iota(jnp.int32, (blocks, HD, rows), 1)
-    ones = (number >= 8) & (number < 16)
-    marks = ((number == docs) | ones).astype(bf16)
-    mine = PEERS * jnp.arange(GROUPS, dtype=jnp.int32) + ctx_place % PEERS
-    my_docs = docs.reshape(GROUPS, PEERS, 1, rows)[:, ctx_place % PEERS]
-    number = number[:GROUPS]
-    veto = jnp.where((number != my_docs) & (number < count), masked_score, 0.0).astype(bf16)
-    first = doc_index(mine * rows, starts)
-    last = doc_index(mine * rows + rows - 1, starts)
-    spans = jnp.stack([starts[first] // rows, (ends[last] + rows - 1) // rows], axis=1)
-    return spans.astype(jnp.int32), marks, veto
 
 
 def body(
@@ -1176,46 +1257,29 @@
     rows, width = patches.shape[1:]
     ctx_place = lax.axis_index("ctx")
     blocks = lax.axis_size("ctx")
-    spans, marks, veto = doc_tables(doc_lengths, ctx_place, blocks, rows)
+    place = (ctx_place % PEERS).astype(jnp.int32).reshape(1)
     vectors = [norm1_gain, norm1_bias, b_qv, b_out, norm2_gain, norm2_bias, b_up, b_down]
     pack = Packed([v.shape[0] for v in vectors])
-    wqkv2, wout2, wup2, small = gather_weights([w_qkv, w_out, w_up], pack.pack(vectors))
-    wqkv = wqkv2.reshape(width, -1)
-    wout = wout2.reshape(width, -1)
-    wup = wup2.reshape(width, -1)
-    far = w_down.shape[0] // 2
-    down_part = lax.dynamic_slice_in_dim(w_down, (ctx_place % 2) * far, far)
+    query, keys, normed1, small, qkv_far, out_far, up_far, down_part = front(
+        pack, patches[0], pack.pack(vectors), w_qkv, w_out, w_up, w_down
+    )
     down_far = lax.ppermute(down_part, "wsh", [(0, 1), (1, 0)])
-
-    def whole(name):
-        start = pack.starts[name]
-        part = small[:, start : start + pack.sizes[name] // LANES]
-        return part.reshape(-1)
-
-    inputs = patches[0].astype(f32)
-    normed1 = layer_norm(inputs, whole("gain1"), whole("bias1")).astype(bf16)
-    projected = jnp.dot(normed1, wqkv, preferred_element_type=f32)
-    bqv = whole("bqv")
-    offset = jnp.concatenate([bqv[:width], jnp.zeros((width,), f32), bqv[width:]])
-    projected = (projected + offset).astype(bf16)
-    part = width // GROUPS
-    by_group = projected.reshape(rows, 3, GROUPS, part).transpose(2, 1, 3, 0)
-    query, keys = spread_heads(by_group.reshape(GROUPS, 3 * part, rows))
-    out_heads, heads_low, sums = attend(spans, query, keys, marks, veto)
+    out_heads, heads_low, sums = attend(doc_lengths, place, query, keys)
     tiles = w_up.shape[1] // width
     chunks = 2 * tiles + 1 + w_qkv.shape[1] // width
     ahead = 4
     firsts = ["x"] * ahead + ["y"] * (chunks - ahead)
     mixed, hidden_grad, grad_heads, send_over_x, send_over_y, keep, vector = middle(
-        pack, firsts, ahead, heads_low, patches[0], cotangent[0], small, wout, wup, w_down, down_far
+        pack, firsts, ahead, heads_low, patches[0], cotangent[0], small, w_out, out_far, w_up,
+        up_far, w_down, down_far,
     )
     across = [(c, c + 2 - c // 2 % 2 * 4) for c in range(blocks)]
     landed_ahead = lax.ppermute(send_over_x, "ctx", across)
     query_grad, key_grad = attend_back(
-        spans, query, keys, marks, veto, out_heads, sums, grad_heads
+        doc_lengths, place, query, keys, out_heads, sums, grad_heads
     )
     inputs_grad, down_total, up_total, out_total, qkv_total, vector_total = last(
-        pack, firsts, query_grad, key_grad, normed1, wqkv, patches[0], hidden_grad, small,
+        pack, firsts, query_grad, key_grad, normed1, w_qkv, qkv_far, patches[0], hidden_grad, small,
         landed_ahead, send_over_y, keep, vector,
     )
     shares = pack.unpack(vector_total)

time: 400 us -> 316 us (0.79); the launches traced: 402 us -> 322 us
  Pallas kernels: 336 us -> 293 us
  local copies, waits for them, and re-layouts: 34.3 us -> 8.58 us
  other arithmetic: 25.3 us -> 10.9 us
  starting transfers between devices: 2.14 us -> 8.71 us
    pallas_call x2 -> x1, Pallas kernels: 85.8 us -> 55.8 us  [front(): pl.pallas_call(functools.partial(front_kernel, pack), out_shape=[jax.Shap...]
    unnamed x82 -> x16, local copies, waits for them, and re-layouts: 14.5 us -> 4.47 us
    pallas_call x1, Pallas kernels: 40.4 us -> 31 us  [attend_back(): pl.pallas_call(attend_back_kernel, out_shape=[jax.ShapeDtypeStruct(query....]
    pallas_call x1, Pallas kernels: 135 us -> 144 us  [last(): pl.pallas_call(functools.partial(last_kernel, pack, firsts, tiles), out_s...]
    ppermute x1, starting transfers between devices: 0.07 us -> 8.42 us  [body(): landed_ahead = lax.ppermute(send_over_x, 'ctx', across)]
    pallas_call x1, Pallas kernels: 35.8 us -> 27.9 us  [attend(): pl.pallas_call(attend_kernel, out_shape=[jax.ShapeDtypeStruct(query.shape...]
    sub x5 -> x0, local copies, waits for them, and re-layouts: 5.42 us -> none  [the longest x4 4.68 us: doc_index(): return jnp.sum(hits, axis=1) - 1]
    pallas_call x1, Pallas kernels: 38.8 us -> 34.7 us  [middle(): pl.pallas_call(functools.partial(middle_kernel, pack, firsts), out_shape=...]
  transfers between devices with their start and end apart: 2 -> 2, of which waited for: 0 -> 0; matrix products, arithmetic and copies ran while one was open for 8% -> 0% of each run, Pallas kernels for 40% -> 18%
where the time goes in v1:
time: 316 us; the launch traced here: 322 us
  Pallas kernels  293 us (93%)
  other arithmetic  10.9 us (3%)
  starting transfers between devices  8.71 us (3%)
  local copies, waits for them, and re-layouts  8.58 us (3%)
    pallas_call x1, Pallas kernels, last(): pl.pallas_call(functools.partial(last_kernel, pack, firsts, tiles), out_s...  144 us
    pallas_call x1, Pallas kernels, front(): pl.pallas_call(functools.partial(front_kernel, pack), out_shape=[jax.Shap...  55.8 us
    pallas_call x1, Pallas kernels, middle(): pl.pallas_call(functools.partial(middle_kernel, pack, firsts), out_shape=...  34.7 us
    pallas_call x1, Pallas kernels, attend_back(): pl.pallas_call(attend_back_kernel, out_shape=[jax.ShapeDtypeStruct(query....  31 us
    pallas_call x1, Pallas kernels, attend(): pl.pallas_call(attend_kernel, out_shape=[jax.ShapeDtypeStruct(query.shape...  27.9 us
    ppermute x1, starting transfers between devices, body(): landed_ahead = lax.ppermute(send_over_x, 'ctx', across)  8.42 us
  transfers between devices with their start and end apart: 2, of which 0 were waited for; matrix products, arithmetic and copies ran while one was open for 0% of the time, Pallas kernels for 18%

profile of v1, /device:TPU:1, one launch (start us, length us, event | category | flops | bytes accessed | tf_op | source)
XLA Modules:
  0.0 322.1 jit_solution(18098726437676677989)
XLA Ops:
  0.6 1.4 add_bitcast_fusion.small_half
  2.1 55.8 %front.1 = (bf16[4,192,256]{2,1,0:T(8,128)(2,1)}, bf16[16,384,256]{2,1,0:T(8,128)(2,1)}, bf16[256,768]{1,0:T(8,128)(2,1)}, f32[2,40,128]{2,1,0:T(8,128)}, bf16[3...) custom-call(bf16[256,768]{1,0:T(8,128)(2,1)} %bitcast.23, ...), custom_call_target="tpu_custom_call" | custom-call | tf_op jit(solution)/shard_map/front/pallas_call | solution.py:326
  57.8 0.3 collective-permute-start
  58.1 27.9 %attend.1 = (f32[4,192,256]{2,1,0:T(8,128)}, bf16[4,192,256]{2,1,0:T(8,128)(2,1)}, f32[4,8,256]{2,1,0:T(8,128)}) custom-call(s32[1,8]{1,0:T(1,128)} %lengths.3, s32[1]{0:T(128)} %bitcast.place, bf16[4,192,256]{2,1,0:T(8,128)(2,1)} %get-tuple-element.40.query, bf16[16,384,256]{2,1,0:T(8,128)(2,1)} %get-tuple-element.41.keys), custom_call_target="tpu_custom_call" | custom-call | tf_op jit(solution)/shard_map/attend/pallas_call | solution.py:1084
  86.1 0.0 collective-permute-done.w_down_far
  86.1 0.0 copy-start.3
  86.1 1.0 copy-done.3
  87.1 34.7 %middle.1 = (bf16[256,768]{1,0:T(8,128)(2,1)}, f32[256,768]{1,0:T(8,128)}, bf16[4,192,256]{2,1,0:T(8,128)(2,1)}, bf16[4,384,384]{2,1,0:T(8,128)(2,1)}, bf16[5,38...) custom-call(bf16[4,192,256]{2,1,0:T(8,128)(2,1)} %get-tuple-element.42.heads, ...), custom_call_target="tpu_custom_call" | custom-call | tf_op jit(solution)/shard_map/middle/pallas_call | solution.py:558
  121.8 8.4 %collective-permute-start.1 = (bf16[4,384,384]{2,1,0:T(8,128)(2,1)}, bf16[4,384,384]{2,1,0:T(8,128)(2,1)S(1)}, u32[]{:S(2)}, u32[]{:S(2)}) collective-permute-start(bf16[4,384,384]{2,1,0:T(8,128)(2,1)} %get-tuple-element.56), channel_id=1, source_target_pairs={{0,4},{2,6},{4,0},{6,2},{8,12},{10,14},{12,8},{14,10},{16,20},{18,... | collective-permute-start | bytes 3538952 | tf_op jit(solution)/shard_map/ppermute | solution.py:1277
  130.2 31.0 %attend_back.1 = (bf16[4,192,256]{2,1,0:T(8,128)(2,1)}, bf16[16,384,256]{2,1,0:T(8,128)(2,1)}) custom-call(s32[1,8]{1,0:T(1,128)} %lengths.3, s32[1]{0:T(128)} %bitcast.place, bf16[4,192,256]{2,1,0:T(8,128)(2,1)} %get-tuple-element.40.query, bf16[16,384,256]{2,1,0:T(8,128)(2,1)} %get-tuple-element.41.keys, f32[4,192,256]{2,1,0:T(8,128)} %get-tuple-element.48.out, ...), custom_call_target="tpu_custom_call" | custom-call | tf_op jit(solution)/shard_map/attend_back/pallas_call | solution.py:1200
  161.2 0.0 collective-permute-done.1.landed_ahead
  161.2 0.0 copy-start.4
  161.2 1.0 copy-done.4
  162.2 143.8 %last.1 = (f32[256,768]{1,0:T(8,128)}, bf16[1536,768]{1,0:T(8,128)(2,1)}, bf16[384,3072]{1,0:T(8,128)(2,1)}, bf16[384,768]{1,0:T(8,128)(2,1)}, bf16[384,2304]{1,0:T(8,128)(2,1)}, /*index=5*/f32[40,128]{1,0:T(8,128)}) custom-call(bf16[4,192,256]{2,1,0:T(8,128)(2,1)} %get-tuple-element.51.query_grad, bf16[16,384,256]{2,1,0:T(8,128)(2,1)} %get-tuple-element.52.key_grad, ...), custom_call_target="tpu_custom_call" | custom-call | tf_op jit(solution)/shard_map/last/pallas_call | solution.py:943
  306.1 0.0 copy-start.2
  306.1 1.4 slice_bitcast_fusion.1
  307.5 1.3 slice_bitcast_fusion
  308.8 1.4 slice_bitcast_fusion.2
  310.2 2.2 convert_element_type.25
  312.3 0.0 copy-done.2
  312.3 2.0 convert_element_type.24
  314.4 0.8 copy-done.1
  315.2 0.0 copy-start
  315.2 2.8 convert_element_type.26
  317.9 0.0 copy-done
  317.9 0.0 copy-start.6
  317.9 0.0 copy-start.5
  317.9 2.5 convert_element_type.27
  320.5 0.0 copy-done.6
  320.5 0.7 copy.31
  321.2 0.0 copy-done.5
  321.2 0.9 copy.32
  (1 shorter events, 0.0 us)
Async XLA Ops:
  57.8 28.2 %collective-permute-start = (bf16[768,768]{1,0:T(8,128)(2,1)}, bf16[768,768]{1,0:T(8,128)(2,1)S(1)}, u32[]{:S(2)}, u32[]{:S(2)}) collective-permute-start(bf16[768,768]{1,0:T(8,128)(2,1)} %get-tuple-element.46), channel_id=1, source_target_pairs={{0,1},{1,0},{2,3},{3,2},{4,5},{5,4},{6,7},{7,6},{8,9},{9,8},{10,11... | collective-permute-start | bytes 3538952 | tf_op jit(solution)/shard_map/ppermute | solution.py:1266
  86.1 1.0 copy-start.3
  121.8 39.4 %collective-permute-start.1 = (bf16[4,384,384]{2,1,0:T(8,128)(2,1)}, bf16[4,384,384]{2,1,0:T(8,128)(2,1)S(1)}, u32[]{:S(2)}, u32[]{:S(2)}) collective-permute-start(bf16[4,384,384]{2,1,0:T(8,128)(2,1)} %get-tuple-element.56), channel_id=1, source_target_pairs={{0,4},{2,6},{4,0},{6,2},{8,12},{10,14},{12,8},{14,10},{16,20},{18,... | collective-permute-start | bytes 3538952 | tf_op jit(solution)/shard_map/ppermute | solution.py:1277
  161.2 1.0 copy-start.4
  306.1 6.3 %copy-start.2 = (bf16[384,2304]{1,0:T(8,128)(2,1)S(1)}, bf16[384,2304]{1,0:T(8,128)(2,1)}, u32[]{:S(2)}) copy-start(bf16[384,2304]{1,0:T(8,128)(2,1)} %get-tuple-element.62) | copy-start | bytes 5308420
  312.3 2.8 copy-start.1
  315.2 2.8 copy-start
  317.9 2.6 copy-start.6
  317.9 3.3 %copy-start.5 = (f32[256,768]{1,0:T(8,128)S(1)}, f32[256,768]{1,0:T(8,128)}, u32[]{:S(2)}) copy-start(f32[256,768]{1,0:T(8,128)} %get-tuple-element.60) | copy-start | bytes 2359300

commit v2 on v1

--- a/solution.py
+++ b/solution.py
@@ -157,6 +157,7 @@
     qkv_far,
     out_far,
     up_far,
+    down_got,
     down_part,
     qkv_own,
     staged,
@@ -174,6 +175,10 @@
     precv,
     nsend,
     nrecv,
+    pxsend,
+    pxrecv,
+    pfsend,
+    pfrecv,
     query_send,
     query_recv,
     zsend,
@@ -197,7 +202,8 @@
     part = query.shape[1]
     half = qkv_half.shape[0]
     quarter = half // PEERS
-    down = down_part.shape[0]
+    down, later = down_half.shape[0] // 2, down_part.shape[0]
+    sooner = down - later
     greet(around + [over_x, over_core, over_y])
     go = Sender()
 
@@ -218,20 +224,35 @@
     copies = [
         pltpu.make_async_copy(small_half, small.at[y], local.at[0]),
         pltpu.make_async_copy(qkv_half, qkv_own, local.at[1]),
-        pltpu.make_async_copy(down_half.at[pl.ds(core * down, down)], down_part, local.at[2]),
+        pltpu.make_async_copy(
+            down_half.at[pl.ds(core * down + sooner, later)], down_part, local.at[2]
+        ),
     ]
     for copy in copies:
         copy.start()
 
-    pieces = [(out_half, out_far, half // 2, 0)]
-    pieces += [(up_half, up_far, half // 8, first) for first in range(0, half // 2, half // 8)]
-
-    def piece_rows(k, pcore):
-        return pl.ds(pcore * (half // 2) + pieces[k][3], pieces[k][2])
-
-    for k, (src, full, count, first) in enumerate(pieces):
-        span = piece_rows(k, core)
-        go(src.at[span], full.at[span], psend.at[k], precv.at[k], over_y)
+    step = quarter // 2
+    pieces = [(up_half, up_far, quarter, quarter, step, i * step, half // 2) for i in range(2)]
+    shared = len(pieces)
+    pieces += [(out_half, out_far, half // 2, half // 2, half // 2, 0, 0)]
+    step = sooner // 2
+    pieces += [(down_half, down_got, down, sooner, step, i * step, 0) for i in range(2)]
+
+    def piece_view(k, px, pcore):
+        unused, full, unused, apart, count, first, across = pieces[k]
+        return full.at[pl.ds(px * across + pcore * apart + first, count)]
+
+    def piece_in(k):
+        view = piece_view(k, x, core)
+        landed(view, precv.at[k])
+        if k < shared:
+            go(view, view, pxsend.at[k], pxrecv.at[k], over_x)
+        go(view, view, nsend.at[k], nrecv.at[k], over_core)
+
+    def piece_over(k):
+        view = piece_view(k, 1 - x, core)
+        landed(view, pxrecv.at[k])
+        go(view, view, pfsend.at[k], pfrecv.at[k], over_core)
 
     copies[0].wait()
     landed(small.at[1 - y], small_sem.at[1])
@@ -245,6 +266,10 @@
         landed(view, yrecv.at[b])
         go(view, view, xsend.at[b], xrecv.at[b], over_x)
         go(view, view, csend.at[b], crecv.at[b], over_core)
+    for k, (src, unused, apart, unused, count, first, across) in enumerate(pieces):
+        span = pl.ds(x * across + core * apart + first, count)
+        go(src.at[span], piece_view(k, x, core), psend.at[k], precv.at[k], over_y)
+
     copies[1].wait()
 
     def block(pz, px, pcore, b):
@@ -294,10 +319,12 @@
             view = block((z + GROUPS - d) % GROUPS, 1 - x, core, b)
             landed(view, kxrecv.at[sem])
             go(view, view, kfsend.at[sem], kfrecv.at[sem], over_core)
-    for k, (src, full, count, first) in enumerate(pieces):
-        view = full.at[piece_rows(k, core)]
-        landed(view, precv.at[k])
-        go(view, view, nsend.at[k], nrecv.at[k], over_core)
+        if 2 <= i < 2 + shared:
+            piece_in(i - 2)
+    for k in range(shared, len(pieces)):
+        piece_in(k)
+    for k in range(shared):
+        piece_over(k)
     for b, d in sequence:
         sem = (b - 1) * GROUPS + d
         pz = (z + GROUPS - d) % GROUPS
@@ -305,8 +332,10 @@
         landed(block(pz, 1 - x, 1 - core, b), kfrecv.at[sem])
     for d in range(1, GROUPS):
         landed(query.at[(z + GROUPS - d) % GROUPS], query_recv.at[d])
-    for k, (src, full, count, first) in enumerate(pieces):
-        landed(full.at[piece_rows(k, 1 - core)], nrecv.at[k])
+    for k in range(len(pieces)):
+        landed(piece_view(k, x, 1 - core), nrecv.at[k])
+    for k in range(shared):
+        landed(piece_view(k, 1 - x, 1 - core), pfrecv.at[k])
     for copy in copies[2:] + own:
         copy.wait()
     go.finish()
@@ -334,9 +363,10 @@
             jax.ShapeDtypeStruct(out_half.shape, bf16),
             jax.ShapeDtypeStruct(up_half.shape, bf16),
             jax.ShapeDtypeStruct((down_half.shape[0] // 2, width), bf16),
+            jax.ShapeDtypeStruct((down_half.shape[0] // 4, width), bf16),
         ],
         in_specs=[vmem, hbm, hbm, hbm, hbm, hbm],
-        out_specs=[vmem] * 8,
+        out_specs=[vmem] * 9,
         scratch_shapes=[
             pltpu.VMEM(qkv_half.shape, bf16),
             pltpu.VMEM((3, GROUPS, part, rows), bf16),
@@ -345,6 +375,7 @@
         + [dma((2,))]
         + pair(3) * 4
         + pair(5) * 2
+        + pair(2) * 2
         + pair(GROUPS)
         + pair(2 * GROUPS) * 4,
         compiler_params=params(60, 1),
@@ -386,6 +417,7 @@
     w_up,
     w_up_far,
     w_down_half,
+    w_down_got,
     w_down_far,
     mixed,
     hidden_grad,
@@ -424,8 +456,9 @@
     far = w_down_far.shape[0]
     greet(around + [over_core])
     go = Sender()
-    far_rows = pl.ds((1 - y) * half + core * far, far)
-    other_rows = pl.ds((1 - y) * half + (1 - core) * far, far)
+    near = half // 2 - far
+    far_rows = pl.ds((1 - y) * half + core * (half // 2) + near, far)
+    other_rows = pl.ds((1 - y) * half + (1 - core) * (half // 2) + near, far)
     for d in (2, 1, 3):
         go(heads.at[(z + d) % GROUPS], o_land.at[z], osend.at[d], orecv.at[d], around[d - 1])
     go(w_down_far, wdown.at[far_rows], wsem.at[0], wsem.at[1], over_core)
@@ -433,6 +466,10 @@
         pltpu.make_async_copy(w_down_half, wdown.at[pl.ds(y * half, half)], local.at[0]),
         pltpu.make_async_copy(w_down_far, wdown.at[far_rows], local.at[1]),
     ]
+    for c in range(2):
+        src = w_down_got.at[pl.ds(c * near, near)]
+        dst = wdown.at[pl.ds((1 - y) * half + c * (half // 2), near)]
+        down_copies.append(pltpu.make_async_copy(src, dst, local.at[8 + c]))
     copies = [
         pltpu.make_async_copy(heads.at[z], o_land.at[z], local.at[2]),
     ]
@@ -566,7 +603,7 @@
             jax.ShapeDtypeStruct((count, width // 2, width // 2), bf16),
             jax.ShapeDtypeStruct((2, pack.rows, LANES), f32),
         ],
-        in_specs=[hbm, vmem, vmem, vmem] + [hbm] * 6,
+        in_specs=[hbm, vmem, vmem, vmem] + [hbm] * 7,
         out_specs=[vmem] * 7,
         scratch_shapes=[
             pltpu.VMEM(heads.shape, bf16),
@@ -580,7 +617,7 @@
             pltpu.VMEM((tiles, 8, width), f32),
             pltpu.VMEM((count, width, width), bf16),
             pltpu.VMEM((count, width, width // 2), bf16),
-            dma((8,)),
+            dma((10,)),
             dma((GROUPS,)),
             dma((GROUPS,)),
             dma((GROUPS,)),
@@ -599,25 +636,25 @@
         self.refs, self.tiles = refs, tiles
 
     def place(self, k, row, count, column, columns):
-        down, up, out, qkv = self.refs
-        width = out.shape[1]
+        width = self.refs[2].shape[1]
+        start = 0
         if k < self.tiles:
-            rows = pl.ds(k * (width // 2) + row, count)
-            return down, rows, pl.ds(pl.multiple_of(column, LANES), columns)
-        if k < 2 * self.tiles:
-            ref, start = up, (k - self.tiles) * width
+            which, row = 0, k * (width // 2) + row
+        elif k < 2 * self.tiles:
+            which, start = 1, (k - self.tiles) * width
         elif k == 2 * self.tiles:
-            ref, start = out, 0
+            which = 2
         else:
-            ref, start = qkv, (k - 2 * self.tiles - 1) * width
-        return ref, pl.ds(row, count), pl.ds(pl.multiple_of(start + column, LANES), columns)
+            which, start = 3, (k - 2 * self.tiles - 1) * width
+        return which, pl.ds(row, count), pl.ds(pl.multiple_of(start + column, LANES), columns)
 
     def view(self, *place):
-        ref, rows, columns = self.place(*place)
-        return ref.at[rows, columns]
+        which, rows, columns = self.place(*place)
+        return self.refs[which].at[rows, columns]
 
     def store(self, values, *place):
-        ref, rows, columns = self.place(*place)
+        which, rows, columns = self.place(*place)
+        ref = self.refs[which]
         ref[rows, columns] = values.astype(ref.dtype)
 
 
@@ -633,16 +670,20 @@
     patches,
     hidden_grad,
     small,
-    landed_ahead,
-    send_on,
+    ahead_x,
+    ahead_y,
     keep,
     vector_in,
     inputs_grad,
+    down_out,
+    up_out,
+    out_out,
+    qkv_out,
+    vector_out,
     down_total,
     up_total,
     out_total,
     qkv_total,
-    vector_out,
     got,
     near,
     both,
@@ -662,6 +703,7 @@
     vectors,
     v_land,
     local,
+    loads,
     n_send,
     n_recv,
     f_send,
@@ -691,22 +733,23 @@
 ):
     f32, bf16 = jnp.float32, jnp.bfloat16
     z, x, core, y = here()
+    pair, side = z // 2, z % 2
     over_x, over_core, over_y = (
         at(z, 1 - x, core, y),
         at(z, x, 1 - core, y),
         at(z, x, core, 1 - y),
     )
     around = [at((z + d) % GROUPS, x, core, y) for d in range(1, GROUPS)]
+    over_near, over_far = at(z + 1 - 2 * side, x, core, y), around[1]
     peer = {"y": over_y, "x": over_x}
     greet(around + [over_x, over_core, over_y])
     go = Sender()
     totals = Totals((down_total, up_total, out_total, qkv_total), tiles)
+    outs = Totals((down_out, up_out, out_out, qkv_out), tiles)
     part = query_grad.shape[1]
     rows, width = patches.shape
-    ahead, chunks = landed_ahead.shape[0], len(firsts)
-    early = ahead + send_on.shape[0]
-    pair, side = z // 2, z % 2
-    over_near, over_far = at(z + 1 - 2 * side, x, core, y), around[1]
+    chunks, early, late = len(firsts), keep.shape[0], c_land.shape[0]
+    ahead = ahead_x.shape[0]
     half = c_land.shape[2]
     quarter, shard = width // 4, width // 16
 
@@ -714,6 +757,7 @@
         remote(view, view, sem, sem, over_core).wait_recv()
 
     order = (2, 1, 3, 0)
+    held = []
     for d in order:
         pz = (z + d) % GROUPS
         for k in range(2):
@@ -721,11 +765,27 @@
             slot = 2 * d + k
             src = key_grad.at[pz * PEERS + px * 2 + 1 - core]
             go(src, near.at[slot], n_send.at[slot], n_recv.at[slot], over_core)
+            src = key_grad.at[pz * PEERS + px * 2 + core]
+            copy = pltpu.make_async_copy(src, both.at[slot], local.at[4 + slot])
+            copy.start()
+            held.append((slot, copy))
+    held = dict(held)
     for d in (2, 1, 3):
         pz = (z + d) % GROUPS
         go(query_grad.at[pz], got.at[z, pl.ds(0, part)], q_send.at[d], q_recv.at[d], around[d - 1])
     own_query = pltpu.make_async_copy(query_grad.at[z], got.at[z, pl.ds(0, part)], local.at[0])
     own_query.start()
+    arrivals = []
+    for k in range(early):
+        src = ahead_x.at[k] if k < ahead else ahead_y.at[k - ahead]
+        arrivals.append(
+            (
+                pltpu.make_async_copy(keep.at[k], half_sum.at[k], loads.at[2 * k]),
+                pltpu.make_async_copy(src, first_land.at[k], loads.at[2 * k + 1]),
+            )
+        )
+        for copy in arrivals[k]:
+            copy.start()
     count = w_qkv.shape[0]
     weights = [
         pltpu.make_async_copy(w_qkv, wqkv.at[pl.ds(y * count, count)], local.at[2]),
@@ -734,39 +794,28 @@
     for copy in weights:
         copy.start()
 
-    def start_first(k, src):
-        go(src, first_land.at[k], asend.at[k], arecv.at[k], peer[firsts[k]])
-
-    for k in range(ahead, early):
-        start_first(k, send_on.at[k - ahead])
-    for step in range(GROUPS + 1):
-        if step < GROUPS:
-            d = order[step]
-            pz = (z + d) % GROUPS
-            for k in range(2):
-                px = (x + 1 + k) % 2
-                slot = 2 * d + k
-                landed(near.at[slot], n_recv.at[slot])
-                mine = key_grad[pz * PEERS + px * 2 + core].astype(f32)
-                both[slot] = (mine + near[slot].astype(f32)).astype(bf16)
-                if k == 0:
-                    go(both.at[slot], far.at[d], f_send.at[d], f_recv.at[d], over_x)
-        if step >= 1:
-            d = order[step - 1]
-            landed(far.at[d], f_recv.at[d])
-            own[d] = (both[2 * d + 1].astype(f32) + far[d].astype(f32)).astype(bf16)
-            place = got.at[z, pl.ds(part, 2 * part)]
-            if d == 0:
-                own_keys = pltpu.make_async_copy(own.at[0], place, local.at[1])
-                own_keys.start()
-            else:
-                sem = GROUPS + d
-                go(own.at[d], place, q_send.at[sem], q_recv.at[sem], around[d - 1])
-    normed_turned = normed_low[...].T
-    normed, scale = normalise(patches[...].astype(f32))
-    gain1 = pack.read(small, "gain1")
-    def kept(k):
-        return keep[k] if k < early else half_sum[k]
+    def collect_near(step):
+        d = order[step]
+        for k in range(2):
+            slot = 2 * d + k
+            landed(near.at[slot], n_recv.at[slot])
+            held[slot].wait()
+            both[slot] = (both[slot].astype(f32) + near[slot].astype(f32)).astype(bf16)
+            if k == 0:
+                go(both.at[slot], far.at[d], f_send.at[d], f_recv.at[d], over_x)
+
+    def collect_far(step):
+        d = order[step]
+        landed(far.at[d], f_recv.at[d])
+        own[d] = (both[2 * d + 1].astype(f32) + far[d].astype(f32)).astype(bf16)
+        place = got.at[z, pl.ds(part, 2 * part)]
+        if d == 0:
+            copy = pltpu.make_async_copy(own.at[0], place, local.at[1])
+            copy.start()
+            return copy
+        sem = GROUPS + d
+        go(own.at[d], place, q_send.at[sem], q_recv.at[sem], around[d - 1])
+        return None
 
     def stage_core(k):
         i = k - early
@@ -781,15 +830,15 @@
             x,
             y,
         )
-        start_first(k, late_send.at[i])
+        go(late_send.at[i], first_land.at[k], asend.at[i], arecv.at[i], peer[firsts[k]])
 
     def stage_first(k):
-        if k < ahead:
-            arrived = landed_ahead[k]
+        if k < early:
+            for copy in arrivals[k]:
+                copy.wait()
         else:
-            landed(first_land.at[k], arecv.at[k])
-            arrived = first_land[k]
-        half_sum[k] = (kept(k).astype(f32) + arrived.astype(f32)).astype(bf16)
+            landed(first_land.at[k], arecv.at[k - early])
+        half_sum[k] = (half_sum[k].astype(f32) + first_land[k].astype(f32)).astype(bf16)
         place = x if firsts[k] == "y" else y
         other = half_sum.at[k, pl.ds((1 - place) * quarter, quarter)]
         second = over_x if firsts[k] == "y" else over_y
@@ -837,6 +886,18 @@
         view = spot(k, 1 - x, 0, 0, quarter)
         landed(view, hrecv.at[k])
         go(view, view, isend.at[2 * k + 1], irecv.at[2 * k + 1], over_core)
+
+    written = []
+
+    def stage_write(k):
+        for px in range(2):
+            place = (x + px) % 2
+            view = totals.view(k, place * quarter, quarter, (1 - core) * half, half)
+            landed(view, irecv.at[2 * k + px])
+        place = (k, 0, 2 * quarter, 0, 2 * half)
+        copy = pltpu.make_async_copy(totals.view(*place), outs.view(*place), loads.at[2 * early + k])
+        copy.start()
+        written.append(copy)
 
     stages = (
         stage_first,
@@ -846,46 +907,8 @@
         stage_back,
         stage_out,
         stage_last,
-    )
-
-    def turn(step):
-        for depth, stage in enumerate(stages):
-            if 0 <= step - depth < chunks:
-                stage(step - depth)
-
-    before = min(early, 4)
-    for step in range(before):
-        turn(step)
-
-    for d in range(1, GROUPS):
-        pz = (z + GROUPS - d) % GROUPS
-        landed(got.at[pz, pl.ds(0, part)], q_recv.at[d])
-        landed(got.at[pz, pl.ds(part, 2 * part)], q_recv.at[GROUPS + d])
-    own_query.wait()
-    own_keys.wait()
-    for copy in weights:
-        copy.wait()
-
-    for k in range(early, chunks):
-        i = k - early
-        turned = got[:, i * part : (i + 1) * part].reshape(width, rows)
-        grads[i] = dot_turned(normed_turned, turned).astype(bf16)
-        others = pl.ds(pl.multiple_of((1 - core) * half, half), half)
-        go(grads.at[i, :, others], c_land.at[i], csend.at[i], crecv.at[i], over_core)
-    vectors[0] = vector_in[...]
-    ones = jnp.ones((8, rows), bf16)
-    normed_grad = jnp.zeros((width, rows), f32)
-    for i in range(chunks - early):
-        turned = got[:, i * part : (i + 1) * part].reshape(width, rows)
-        if i != 1:
-            sums = dot_turned(ones, turned)[0:1]
-            pack.write(vectors.at[0], "bqv", sums, (i // 2) * width)
-        normed_grad += dot(wqkv[:, i * width : (i + 1) * width], turned)
-    change, gain_grad, bias_grad = normalise_back(normed_grad.T, gain1, normed, scale)
-    inputs_grad[...] = hidden_grad[...] + change
-    pack.write(vectors.at[0], "gain1", gain_grad)
-    pack.write(vectors.at[0], "bias1", bias_grad)
-    go(vectors.at[0], v_land.at[0], vsend.at[0], vrecv.at[0], over_core)
+        stage_write,
+    )
 
     def vector_step(n):
         if n == 0:
@@ -910,22 +933,82 @@
             v_land[0] = total
             vector_out[...] = v_land[0, y]
 
-    for k in range(early, chunks):
-        stage_core(k)
-    for step in range(before, chunks + len(stages) - 1):
-        turn(step)
-        vector_step(step - before)
-    for k in range(chunks):
-        for px in range(2):
-            place = (x + px) % 2
-            view = totals.view(k, place * quarter, quarter, (1 - core) * half, half)
-            landed(view, irecv.at[2 * k + px])
+    entry = list(range(early)) + [LATE_TURN + i for i in range(late)]
+    turns = iter(range(entry[-1] + len(stages)))
+
+    def turn():
+        step = next(turns, None)
+        if step is None:
+            return False
+        for depth, stage in enumerate(stages):
+            for k in range(chunks):
+                if step - depth == entry[k]:
+                    stage(k)
+        return True
+
+    collect_near(0)
+    turn()
+    for step in range(1, GROUPS):
+        collect_near(step)
+        collect_far(step - 1)
+        turn()
+    own_keys = collect_far(GROUPS - 1)
+    turn()
+    normed_turned = normed_low[...].T
+    normed, scale = normalise(patches[...].astype(f32))
+    gain1 = pack.read(small, "gain1")
+    turn()
+    for d in range(1, GROUPS):
+        landed(got.at[(z + GROUPS - d) % GROUPS, pl.ds(0, part)], q_recv.at[d])
+    own_query.wait()
+    turn()
+    others = pl.ds(pl.multiple_of((1 - core) * half, half), half)
+
+    def project(i):
+        turned = got[:, i * part : (i + 1) * part].reshape(width, rows)
+        grads[i] = dot_turned(normed_turned, turned).astype(bf16)
+        go(grads.at[i, :, others], c_land.at[i], csend.at[i], crecv.at[i], over_core)
+
+    project(0)
+    for d in range(1, GROUPS):
+        landed(got.at[(z + GROUPS - d) % GROUPS, pl.ds(part, 2 * part)], q_recv.at[GROUPS + d])
+    own_keys.wait()
+    for i in range(1, late):
+        project(i)
+    turn()
+    for copy in weights:
+        copy.wait()
+    vectors[0] = vector_in[...]
+    ones = jnp.ones((8, rows), bf16)
+    normed_grad = jnp.zeros((width, rows), f32)
+    for i in range(late):
+        turned = got[:, i * part : (i + 1) * part].reshape(width, rows)
+        if i != 1:
+            sums = dot_turned(ones, turned)[0:1]
+            pack.write(vectors.at[0], "bqv", sums, (i // 2) * width)
+        normed_grad += dot(wqkv[:, i * width : (i + 1) * width], turned)
+        stage_core(early + i)
+    turn()
+    change, gain_grad, bias_grad = normalise_back(normed_grad.T, gain1, normed, scale)
+    inputs_grad[...] = hidden_grad[...] + change
+    pack.write(vectors.at[0], "gain1", gain_grad)
+    pack.write(vectors.at[0], "bias1", bias_grad)
+    go(vectors.at[0], v_land.at[0], vsend.at[0], vrecv.at[0], over_core)
+    step = 0
+    while turn():
+        vector_step(step)
+        step += 1
+    for copy in written:
+        copy.wait()
     go.finish()
+
+
+LATE_TURN = 9
 
 
 def last(
     pack, firsts, query_grad, key_grad, normed_low, w_qkv, w_qkv_far, patches, hidden_grad, small,
-    landed_ahead, send_on, keep, vector
+    ahead_x, ahead_y, keep, vector
 ):
     f32, bf16 = jnp.float32, jnp.bfloat16
     vmem = pl.BlockSpec(memory_space=pltpu.VMEM)
@@ -936,23 +1019,25 @@
     tiles, chunks, late = (early - 1) // 2, len(firsts), len(firsts) - early
     piece = (2 * part, rows)
     dma = pltpu.SemaphoreType.DMA
+    totals = [
+        (tiles * half, width),
+        (half, tiles * width),
+        (half, width),
+        (half, late * width),
+    ]
 
     def pair(n):
         return [dma((n,))] * 2
 
     return pl.pallas_call(
         functools.partial(last_kernel, pack, firsts, tiles),
-        out_shape=[
-            jax.ShapeDtypeStruct((rows, width), f32),
-            jax.ShapeDtypeStruct((tiles * half, width), bf16),
-            jax.ShapeDtypeStruct((half, tiles * width), bf16),
-            jax.ShapeDtypeStruct((half, width), bf16),
-            jax.ShapeDtypeStruct((half, late * width), bf16),
-            jax.ShapeDtypeStruct(vector.shape[1:], f32),
-        ],
-        in_specs=[hbm, vmem, vmem, hbm, hbm, vmem, vmem, vmem, vmem, hbm, vmem, vmem],
-        out_specs=[vmem] * 6,
-        scratch_shapes=[
+        out_shape=[jax.ShapeDtypeStruct((rows, width), f32)]
+        + [jax.ShapeDtypeStruct(shape, bf16) for shape in totals]
+        + [jax.ShapeDtypeStruct(vector.shape[1:], f32)],
+        in_specs=[hbm, hbm, vmem, hbm, hbm, vmem, vmem, vmem, hbm, hbm, hbm, vmem],
+        out_specs=[vmem] + [hbm] * 4 + [vmem],
+        scratch_shapes=[pltpu.VMEM(shape, bf16) for shape in totals]
+        + [
             pltpu.VMEM((groups, 3 * part, rows), bf16),
             pltpu.VMEM((2 * groups,) + piece, bf16),
             pltpu.VMEM((2 * groups,) + piece, bf16),
@@ -971,22 +1056,21 @@
             pltpu.VMEM((chunks, half // 8, half), bf16),
             pltpu.VMEM((4,) + vector.shape, f32),
             pltpu.VMEM((6,) + vector.shape, f32),
-            dma((4,)),
+            dma((4 + 2 * groups,)),
+            dma((2 * early + chunks,)),
         ]
         + pair(2 * groups)
         + pair(groups)
         + pair(2 * groups)
-        + pair(late)
-        + pair(chunks)
-        + pair(chunks)
-        + pair(chunks) * 5
+        + pair(late) * 2
+        + pair(chunks) * 6
         + pair(2 * chunks)
         + pair(6),
         compiler_params=params(60, 4),
         name="last",
     )(
         query_grad, key_grad, normed_low, w_qkv, w_qkv_far, patches, hidden_grad, small,
-        landed_ahead, send_on, keep, vector,
+        ahead_x, ahead_y, keep, vector,
     )
 
 
@@ -1053,22 +1137,33 @@
         stat[1] = jnp.zeros(stat.shape[1:], jnp.float32)
         acc[...] = jnp.zeros(acc.shape, jnp.float32)
 
-        def step(j, carry):
+        low, high = documents.span(block)
+        steps = (high - low + 1) // 2
+        low = jnp.minimum(low, blocks - 2 * steps)
+
+        def step(n, carry):
+            j = low + 2 * n
+            made = [
+                [dot(key_rows[h, j + k], query_aug[h]) for k in range(2)] for h in range(PER_GROUP)
+            ]
             for h in range(PER_GROUP):
-                scores = dot(key_rows[h, j], query_aug[h])
+                first, second = made[h]
                 old = stat[0, h : h + 1]
-                new = jnp.maximum(old, jnp.max(scores, axis=0, keepdims=True))
-                probs = jnp.exp(scores - new)
+                most = jnp.max(jnp.maximum(first, second), axis=0, keepdims=True)
+                new = jnp.maximum(old, most)
+                first, second = jnp.exp(first - new), jnp.exp(second - new)
                 factor = jnp.exp(old - new)
                 stat[0, h : h + 1] = new
                 stat[1, h : h + 1] = stat[1, h : h + 1] * factor + jnp.sum(
-                    probs, axis=0, keepdims=True
+                    first + second, axis=0, keepdims=True
                 )
-                values = keys[j, width + h * HD : width + (h + 1) * HD]
-                acc[h] = acc[h] * factor + dot(values, probs.astype(jnp.bfloat16))
+                span = slice(width + h * HD, width + (h + 1) * HD)
+                shared = dot(keys[j, span], first.astype(jnp.bfloat16))
+                shared += dot(keys[j + 1, span], second.astype(jnp.bfloat16))
+                acc[h] = acc[h] * factor + shared
             return carry
 
-        lax.fori_loop(*documents.span(block), step, 0)
+        lax.fori_loop(0, steps, step, 0)
         for h in range(PER_GROUP):
             total = stat[1, h : h + 1]
             shared = acc[h] / total
@@ -1138,10 +1233,11 @@
         mark = documents.marks(j)
         for h in range(PER_GROUP):
             both = jnp.concatenate([keys[j, h * HD : (h + 1) * HD], mark], axis=0)
-            key_rows[h, j] = both.T
+            key_rows[h, pl.ds(pl.multiple_of(j * rows, rows), rows)] = both.T
             values = keys[j, width + h * HD : width + (h + 1) * HD]
-            value_rows[h, j] = jnp.concatenate([values, mark], axis=0).T
-            key_acc[h, j] = jnp.zeros(key_acc.shape[2:], jnp.float32)
+            place = pl.ds(pl.multiple_of(j * rows, rows), rows)
+            value_rows[h, place] = jnp.concatenate([values, mark], axis=0).T
+            key_acc[h, place] = jnp.zeros((rows, 2 * HD), jnp.float32)
         return carry
 
     lax.fori_loop(0, blocks, turn, 0)
@@ -1170,21 +1266,31 @@
             grad_rows[h] = jnp.concatenate([none, grad], axis=0).T
         query_acc[...] = jnp.zeros(query_acc.shape, jnp.float32)
 
-        def step(j, carry):
+        low, high = documents.span(block)
+        steps = (high - low + 1) // 2
+        low = jnp.minimum(low, blocks - 2 * steps)
+
+        def step(n, carry):
+            j = low + 2 * n
+            span = pl.ds(pl.multiple_of(j * rows, rows), 2 * rows)
             for h in range(PER_GROUP):
-                probs = jnp.exp(dot(key_rows[h, j], query_aug[h]))
-                change = (probs * dot(value_rows[h, j], grad_aug[h])).astype(bf16)
-                key_acc[h, j] += dot(probs.astype(bf16), grad_rows[h]) + dot(change, query_rows[h])
-                query_acc[h] += dot(keys[j, h * HD : (h + 1) * HD], change)
+                probs = jnp.exp(dot(key_rows[h, span], query_aug[h]))
+                change = (probs * dot(value_rows[h, span], grad_aug[h])).astype(bf16)
+                low_probs = probs.astype(bf16)
+                key_acc[h, span] += dot(low_probs, grad_rows[h]) + dot(change, query_rows[h])
+                turned = slice(h * HD, (h + 1) * HD)
+                query_acc[h] += dot(keys[j, turned], change[:rows]) + dot(
+                    keys[j + 1, turned], change[rows:]
+                )
             return carry
 
-        lax.fori_loop(*documents.span(block), step, 0)
+        lax.fori_loop(0, steps, step, 0)
         for h in range(PER_GROUP):
             query_grad[i, h * HD : (h + 1) * HD] = (query_acc[h] * 0.125).astype(bf16)
 
     def finish(j, carry):
         for h in range(PER_GROUP):
-            both = key_acc[h, j].T.astype(bf16)
+            both = key_acc[h, pl.ds(pl.multiple_of(j * rows, rows), rows)].astype(bf16).T
             key_grad[j, h * HD : (h + 1) * HD] = both[:HD]
             key_grad[j, width + h * HD : width + (h + 1) * HD] = both[HD:]
         return carry
@@ -1206,14 +1312,14 @@
         in_specs=[pl.BlockSpec(memory_space=pltpu.SMEM)] * 2 + [vmem] * 5,
         out_specs=[vmem] * 2,
         scratch_shapes=[
-            pltpu.VMEM((PER_GROUP, blocks, rows, 2 * HD), bf16),
-            pltpu.VMEM((PER_GROUP, blocks, rows, 2 * HD), bf16),
+            pltpu.VMEM((PER_GROUP, blocks * rows, 2 * HD), bf16),
+            pltpu.VMEM((PER_GROUP, blocks * rows, 2 * HD), bf16),
             pltpu.VMEM((PER_GROUP, 2 * HD, rows), bf16),
             pltpu.VMEM((PER_GROUP, 2 * HD, rows), bf16),
             pltpu.VMEM((PER_GROUP, rows, 2 * HD), bf16),
             pltpu.VMEM((PER_GROUP, rows, 2 * HD), bf16),
             pltpu.VMEM((PER_GROUP, HD, rows), jnp.float32),
-            pltpu.VMEM((PER_GROUP, blocks, rows, 2 * HD), jnp.float32),
+            pltpu.VMEM((PER_GROUP, blocks * rows, 2 * HD), jnp.float32),
         ],
         compiler_params=params(60),
         name="attend_back",
@@ -1260,27 +1366,28 @@
     place = (ctx_place % PEERS).astype(jnp.int32).reshape(1)
     vectors = [norm1_gain, norm1_bias, b_qv, b_out, norm2_gain, norm2_bias, b_up, b_down]
     pack = Packed([v.shape[0] for v in vectors])
-    query, keys, normed1, small, qkv_far, out_far, up_far, down_part = front(
+    query, keys, normed1, small, qkv_far, out_far, up_far, down_got, down_part = front(
         pack, patches[0], pack.pack(vectors), w_qkv, w_out, w_up, w_down
     )
     down_far = lax.ppermute(down_part, "wsh", [(0, 1), (1, 0)])
     out_heads, heads_low, sums = attend(doc_lengths, place, query, keys)
     tiles = w_up.shape[1] // width
     chunks = 2 * tiles + 1 + w_qkv.shape[1] // width
-    ahead = 4
+    ahead = tiles + 1
     firsts = ["x"] * ahead + ["y"] * (chunks - ahead)
     mixed, hidden_grad, grad_heads, send_over_x, send_over_y, keep, vector = middle(
         pack, firsts, ahead, heads_low, patches[0], cotangent[0], small, w_out, out_far, w_up,
-        up_far, w_down, down_far,
+        up_far, w_down, down_got, down_far,
     )
     across = [(c, c + 2 - c // 2 % 2 * 4) for c in range(blocks)]
-    landed_ahead = lax.ppermute(send_over_x, "ctx", across)
+    ahead_x = lax.ppermute(send_over_x, "ctx", across)
+    ahead_y = lax.ppermute(send_over_y, "wsh", [(0, 1), (1, 0)])
     query_grad, key_grad = attend_back(
         doc_lengths, place, query, keys, out_heads, sums, grad_heads
     )
     inputs_grad, down_total, up_total, out_total, qkv_total, vector_total = last(
         pack, firsts, query_grad, key_grad, normed1, w_qkv, qkv_far, patches[0], hidden_grad, small,
-        landed_ahead, send_over_y, keep, vector,
+        ahead_x, ahead_y, keep, vector,
     )
     shares = pack.unpack(vector_total)
     return (

time: 316 us -> 282 us (0.89); the launches traced: 322 us -> 281 us
  Pallas kernels: 293 us -> 252 us
  starting transfers between devices: 8.71 us -> 3.01 us
  waiting for transfers between devices: 0.01 us -> 5.34 us
    pallas_call x1, Pallas kernels: 144 us -> 111 us  [last(): pl.pallas_call(functools.partial(last_kernel, pack, firsts, tiles), out_s...]
    pallas_call x1, Pallas kernels: 27.9 us -> 17.2 us  [attend(): pl.pallas_call(attend_kernel, out_shape=[jax.ShapeDtypeStruct(query.shape...]
    pallas_call x1, Pallas kernels: 55.8 us -> 62.2 us  [front(): pl.pallas_call(functools.partial(front_kernel, pack), out_shape=[jax.Shap...]
    ppermute x1 -> x2, starting transfers between devices: 8.42 us -> 2.5 us  [the longest x1 2.02 us: body(): ahead_y = lax.ppermute(send_over_y, 'wsh', [(0, 1), (1, 0)])]
    ppermute x1 -> x2, waiting for transfers between devices: 0.01 us -> 5.34 us  [the longest x1 4.94 us: body(): ahead_x = lax.ppermute(send_over_x, 'ctx', across)]
    pallas_call x1, Pallas kernels: 31 us -> 25.7 us  [attend_back(): pl.pallas_call(attend_back_kernel, out_shape=[jax.ShapeDtypeStruct(query....]
  transfers between devices with their start and end apart: 2 -> 3, of which waited for: 0 -> 2; matrix products, arithmetic and copies ran while one was open for 0% -> 0% of each run, Pallas kernels for 18% -> 15%
where the time goes in v2:
time: 282 us; the launch traced here: 281 us
  Pallas kernels  252 us (89%)
  other arithmetic  10.9 us (4%)
  local copies, waits for them, and re-layouts  8.48 us (3%)
  waiting for transfers between devices  5.34 us (2%)
  starting transfers between devices  3.01 us (1%)
    pallas_call x1, Pallas kernels, last(): pl.pallas_call(functools.partial(last_kernel, pack, firsts, tiles), out_s...  111 us
    pallas_call x1, Pallas kernels, front(): pl.pallas_call(functools.partial(front_kernel, pack), out_shape=[jax.Shap...  62.2 us
    pallas_call x1, Pallas kernels, middle(): pl.pallas_call(functools.partial(middle_kernel, pack, firsts), out_shape=...  36 us
    pallas_call x1, Pallas kernels, attend_back(): pl.pallas_call(attend_back_kernel, out_shape=[jax.ShapeDtypeStruct(query....  25.7 us
    pallas_call x1, Pallas kernels, attend(): pl.pallas_call(attend_kernel, out_shape=[jax.ShapeDtypeStruct(query.shape...  17.2 us
  transfers between devices with their start and end apart: 3, of which 2 were waited for; matrix products, arithmetic and copies ran while one was open for 0% of the time, Pallas kernels for 15%

profile of v2, /device:TPU:1, one launch (start us, length us, event | category | flops | bytes accessed | tf_op | source)
XLA Modules:
  0.0 280.8 jit_solution(540392199139657086)
XLA Ops:
  0.6 1.4 add_bitcast_fusion.small_half
  2.1 62.2 %front.1 = (bf16[4,192,256]{2,1,0:T(8,128)(2,1)}, bf16[16,384,256]{2,1,0:T(8,128)(2,1)}, bf16[256,768]{1,0:T(8,128)(2,1)}, f32[2,40,128]{2,1,0:T(8,128)}, bf16[3...) custom-call(bf16[256,768]{1,0:T(8,128)(2,1)} %bitcast.23, ...), custom_call_target="tpu_custom_call" | custom-call | tf_op jit(solution)/shard_map/front/pallas_call | solution.py:355
  64.3 0.5 collective-permute-start
  64.8 17.2 %attend.1 = (f32[4,192,256]{2,1,0:T(8,128)}, bf16[4,192,256]{2,1,0:T(8,128)(2,1)}, f32[4,8,256]{2,1,0:T(8,128)}) custom-call(s32[1,8]{1,0:T(1,128)} %lengths.3, s32[1]{0:T(128)} %bitcast.place, bf16[4,192,256]{2,1,0:T(8,128)(2,1)} %get-tuple-element.41.query, bf16[16,384,256]{2,1,0:T(8,128)(2,1)} %get-tuple-element.42.keys), custom_call_target="tpu_custom_call" | custom-call | tf_op jit(solution)/shard_map/attend/pallas_call | solution.py:1179
  82.0 0.0 collective-permute-done.w_down_far
  82.0 0.0 copy-start.6
  82.0 0.8 copy-done.6
  82.8 36.0 %middle.1 = (bf16[256,768]{1,0:T(8,128)(2,1)}, f32[256,768]{1,0:T(8,128)}, bf16[4,192,256]{2,1,0:T(8,128)(2,1)}, bf16[5,384,384]{2,1,0:T(8,128)(2,1)}, bf16[4,38...) custom-call(bf16[4,192,256]{2,1,0:T(8,128)(2,1)} %get-tuple-element.43.heads, ...), custom_call_target="tpu_custom_call" | custom-call | tf_op jit(solution)/shard_map/middle/pallas_call | solution.py:595
  118.8 0.5 collective-permute-start.1
  119.3 2.0 collective-permute-start.2
  121.3 25.7 %attend_back.1 = (bf16[4,192,256]{2,1,0:T(8,128)(2,1)}, bf16[16,384,256]{2,1,0:T(8,128)(2,1)}) custom-call(s32[1,8]{1,0:T(1,128)} %lengths.3, s32[1]{0:T(128)} %bitcast.place, bf16[4,192,256]{2,1,0:T(8,128)(2,1)} %get-tuple-element.41.query, bf16[16,384,256]{2,1,0:T(8,128)(2,1)} %get-tuple-element.42.keys, f32[4,192,256]{2,1,0:T(8,128)} %get-tuple-element.50.out, ...), custom_call_target="tpu_custom_call" | custom-call | tf_op jit(solution)/shard_map/attend_back/pallas_call | solution.py:1306
  147.0 0.4 collective-permute-done.2.ahead_y
  147.4 0.0 copy-start.4
  147.4 4.9 %collective-permute-done.1.ahead_x = bf16[5,384,384]{2,1,0:T(8,128)(2,1)S(1)} collective-permute-done((bf16[5,384,384]{2,1,0:T(8,128)(2,1)}, bf16[5,384,384]{2,1,0:T(8,128)(2,1)S(1)}, u32[]{:S(2)}, u32[]{:S(2)}) %collective-permute-start.1) | collective-permute-done | bytes 1474592 | tf_op jit(solution)/shard_map/ppermute | solution.py:1383
  152.4 0.0 copy-done.4
  152.4 1.1 copy-done.3
  153.5 111.3 %last.1 = (f32[256,768]{1,0:T(8,128)}, bf16[1536,768]{1,0:T(8,128)(2,1)}, bf16[384,3072]{1,0:T(8,128)(2,1)}, bf16[384,768]{1,0:T(8,128)(2,1)}, bf16[384,2304]{1,0:T(8,128)(2,1)}, /*index=5*/f32[40,128]{1,0:T(8,128)}) custom-call(bf16[4,192,256]{2,1,0:T(8,128)(2,1)} %get-tuple-element.53.query_grad, bf16[16,384,256]{2,1,0:T(8,128)(2,1)} %get-tuple-element.54.key_grad, ...), custom_call_target="tpu_custom_call" | custom-call | tf_op jit(solution)/shard_map/last/pallas_call | solution.py:1032
  264.8 0.0 copy-start.2
  264.8 1.4 slice_bitcast_fusion.1
  266.2 1.3 slice_bitcast_fusion
  267.5 1.4 slice_bitcast_fusion.2
  268.9 2.2 convert_element_type.25
  271.0 0.0 copy-done.2
  271.0 2.0 convert_element_type.24
  273.1 0.8 copy-done.1
  273.9 2.8 convert_element_type.26
  276.6 0.0 copy-done
  276.6 2.5 convert_element_type.27
  279.2 0.0 copy-done.7
  279.2 0.7 copy.31
  279.9 0.0 copy-done.5
  279.9 0.9 copy.32
  (5 shorter events, 0.0 us)
Async XLA Ops:
  64.3 17.7 %collective-permute-start = (bf16[384,768]{1,0:T(8,128)(2,1)}, bf16[384,768]{1,0:T(8,128)(2,1)S(1)}, u32[]{:S(2)}, u32[]{:S(2)}) collective-permute-start(bf16[384,768]{1,0:T(8,128)(2,1)} %get-tuple-element.48), channel_id=1, source_target_pairs={{0,1},{1,0},{2,3},{3,2},{4,5},{5,4},{6,7},{7,6},{8,9},{9,8},{10,11... | collective-permute-start | bytes 1769480 | tf_op jit(solution)/shard_map/ppermute | solution.py:1372
  82.0 0.8 copy-start.6
  118.8 33.6 %collective-permute-start.1 = (bf16[5,384,384]{2,1,0:T(8,128)(2,1)}, bf16[5,384,384]{2,1,0:T(8,128)(2,1)S(1)}, u32[]{:S(2)}, u32[]{:S(2)}) collective-permute-start(bf16[5,384,384]{2,1,0:T(8,128)(2,1)} %get-tuple-element.58), channel_id=1, source_target_pairs={{0,4},{2,6},{4,0},{6,2},{8,12},{10,14},{12,8},{14,10},{16,20},{18,... | collective-permute-start | bytes 4423688 | tf_op jit(solution)/shard_map/ppermute | solution.py:1383
  119.3 28.1 %collective-permute-start.2 = (bf16[4,384,384]{2,1,0:T(8,128)(2,1)}, bf16[4,384,384]{2,1,0:T(8,128)(2,1)S(1)}, u32[]{:S(2)}, u32[]{:S(2)}) collective-permute-start(bf16[4,384,384]{2,1,0:T(8,128)(2,1)} %get-tuple-element.59), channel_id=1, source_target_pairs={{0,1},{1,0},{2,3},{3,2},{4,5},{5,4},{6,7},{7,6},{8,9},{9,8},{10,11... | collective-permute-start | bytes 3538952 | tf_op jit(solution)/shard_map/ppermute | solution.py:1384
  147.4 4.9 %copy-start.4 = (bf16[4,384,384]{2,1,0:T(8,128)(2,1)}, bf16[4,384,384]{2,1,0:T(8,128)(2,1)S(1)}, u32[]{:S(2)}) copy-start(bf16[4,384,384]{2,1,0:T(8,128)(2,1)S(1)} %collective-permute-done.2.ahead_y) | copy-start | bytes 3538948
  152.4 1.1 copy-start.3
  264.8 6.3 %copy-start.2 = (bf16[384,2304]{1,0:T(8,128)(2,1)S(1)}, bf16[384,2304]{1,0:T(8,128)(2,1)}, u32[]{:S(2)}) copy-start(bf16[384,2304]{1,0:T(8,128)(2,1)} %get-tuple-element.64) | copy-start | bytes 5308420
  271.0 2.8 %copy-start.1 = (bf16[384,3072]{1,0:T(8,128)(2,1)S(1)}, bf16[384,3072]{1,0:T(8,128)(2,1)}, u32[]{:S(2)}) copy-start(bf16[384,3072]{1,0:T(8,128)(2,1)} %get-tuple-element.66) | copy-start | bytes 7077892
  273.9 2.8 copy-start
  276.6 2.6 copy-start.7
  276.6 3.3 %copy-start.5 = (f32[256,768]{1,0:T(8,128)S(1)}, f32[256,768]{1,0:T(8,128)}, u32[]{:S(2)}) copy-start(f32[256,768]{1,0:T(8,128)} %get-tuple-element.62) | copy-start | bytes 2359300

commit v3 on v2

--- a/solution.py
+++ b/solution.py
@@ -424,6 +424,7 @@
     grad_heads,
     send_over_x,
     send_over_y,
+    send_rest,
     keep,
     vector,
     o_land,
@@ -546,7 +547,7 @@
     own.start()
 
     columns = c_land.shape[2]
-    count, ahead = grads.shape[0], send_over_x.shape[0]
+    count = grads.shape[0]
     mine = pl.ds(pl.multiple_of(core * columns, columns), columns)
     others = pl.ds(pl.multiple_of((1 - core) * columns, columns), columns)
 
@@ -556,7 +557,11 @@
     def settle(k):
         landed = c_land.at[k]
         remote(landed, landed, csend.at[k], crecv.at[k], over_core).wait_recv()
-        sent = send_over_x.at[k] if k < ahead else send_over_y.at[k - ahead]
+        place, sent = k, None
+        for ref in (send_over_x, send_over_y, send_rest):
+            if sent is None and place < ref.shape[0]:
+                sent = ref.at[place]
+            place -= ref.shape[0]
         core_sum(firsts[k], lambda r: grads[k, r, mine], c_land.at[k], sent, keep.at[k], x, y)
 
     c_turned = c.T
@@ -599,12 +604,13 @@
             jax.ShapeDtypeStruct((rows, width), f32),
             jax.ShapeDtypeStruct(heads.shape, bf16),
             jax.ShapeDtypeStruct((ahead, width // 2, width // 2), bf16),
-            jax.ShapeDtypeStruct((count - ahead, width // 2, width // 2), bf16),
+            jax.ShapeDtypeStruct((ahead, width // 2, width // 2), bf16),
+            jax.ShapeDtypeStruct((count - 2 * ahead, width // 2, width // 2), bf16),
             jax.ShapeDtypeStruct((count, width // 2, width // 2), bf16),
             jax.ShapeDtypeStruct((2, pack.rows, LANES), f32),
         ],
         in_specs=[hbm, vmem, vmem, vmem] + [hbm] * 7,
-        out_specs=[vmem] * 7,
+        out_specs=[vmem] * 8,
         scratch_shapes=[
             pltpu.VMEM(heads.shape, bf16),
             pltpu.VMEM(heads.shape, bf16),
@@ -672,6 +678,7 @@
     small,
     ahead_x,
     ahead_y,
+    send_rest,
     keep,
     vector_in,
     inputs_grad,
@@ -750,6 +757,7 @@
     rows, width = patches.shape
     chunks, early, late = len(firsts), keep.shape[0], c_land.shape[0]
     ahead = ahead_x.shape[0]
+    hidden = ahead + ahead_y.shape[0]
     half = c_land.shape[2]
     quarter, shard = width // 4, width // 16
 
@@ -777,13 +785,15 @@
     own_query.start()
     arrivals = []
     for k in range(early):
-        src = ahead_x.at[k] if k < ahead else ahead_y.at[k - ahead]
-        arrivals.append(
-            (
-                pltpu.make_async_copy(keep.at[k], half_sum.at[k], loads.at[2 * k]),
-                pltpu.make_async_copy(src, first_land.at[k], loads.at[2 * k + 1]),
-            )
-        )
+        arrivals.append([pltpu.make_async_copy(keep.at[k], half_sum.at[k], loads.at[2 * k])])
+        if k < hidden:
+            src = ahead_x.at[k] if k < ahead else ahead_y.at[k - ahead]
+            copy = pltpu.make_async_copy(src, first_land.at[k], loads.at[2 * k + 1])
+            arrivals[k].append(copy)
+        else:
+            sem = late + k - hidden
+            src = send_rest.at[k - hidden]
+            go(src, first_land.at[k], asend.at[sem], arecv.at[sem], peer[firsts[k]])
         for copy in arrivals[k]:
             copy.start()
     count = w_qkv.shape[0]
@@ -836,8 +846,8 @@
         if k < early:
             for copy in arrivals[k]:
                 copy.wait()
-        else:
-            landed(first_land.at[k], arecv.at[k - early])
+        if k >= hidden:
+            landed(first_land.at[k], arecv.at[k - early if k >= early else late + k - hidden])
         half_sum[k] = (half_sum[k].astype(f32) + first_land[k].astype(f32)).astype(bf16)
         place = x if firsts[k] == "y" else y
         other = half_sum.at[k, pl.ds((1 - place) * quarter, quarter)]
@@ -1008,7 +1018,7 @@
 
 def last(
     pack, firsts, query_grad, key_grad, normed_low, w_qkv, w_qkv_far, patches, hidden_grad, small,
-    ahead_x, ahead_y, keep, vector
+    ahead_x, ahead_y, send_rest, keep, vector
 ):
     f32, bf16 = jnp.float32, jnp.bfloat16
     vmem = pl.BlockSpec(memory_space=pltpu.VMEM)
@@ -1034,7 +1044,7 @@
         out_shape=[jax.ShapeDtypeStruct((rows, width), f32)]
         + [jax.ShapeDtypeStruct(shape, bf16) for shape in totals]
         + [jax.ShapeDtypeStruct(vector.shape[1:], f32)],
-        in_specs=[hbm, hbm, vmem, hbm, hbm, vmem, vmem, vmem, hbm, hbm, hbm, vmem],
+        in_specs=[hbm, hbm, vmem, hbm, hbm, vmem, vmem, vmem, hbm, hbm, hbm, hbm, vmem],
         out_specs=[vmem] + [hbm] * 4 + [vmem],
         scratch_shapes=[pltpu.VMEM(shape, bf16) for shape in totals]
         + [
@@ -1062,7 +1072,8 @@
         + pair(2 * groups)
         + pair(groups)
         + pair(2 * groups)
-        + pair(late) * 2
+        + pair(late)
+        + pair(chunks)
         + pair(chunks) * 6
         + pair(2 * chunks)
         + pair(6),
@@ -1070,7 +1081,7 @@
         name="last",
     )(
         query_grad, key_grad, normed_low, w_qkv, w_qkv_far, patches, hidden_grad, small,
-        ahead_x, ahead_y, keep, vector,
+        ahead_x, ahead_y, send_rest, keep, vector,
     )
 
 
@@ -1373,9 +1384,9 @@
     out_heads, heads_low, sums = attend(doc_lengths, place, query, keys)
     tiles = w_up.shape[1] // width
     chunks = 2 * tiles + 1 + w_qkv.shape[1] // width
-    ahead = tiles + 1
+    ahead = tiles
     firsts = ["x"] * ahead + ["y"] * (chunks - ahead)
-    mixed, hidden_grad, grad_heads, send_over_x, send_over_y, keep, vector = middle(
+    mixed, hidden_grad, grad_heads, send_over_x, send_over_y, send_rest, keep, vector = middle(
         pack, firsts, ahead, heads_low, patches[0], cotangent[0], small, w_out, out_far, w_up,
         up_far, w_down, down_got, down_far,
     )
@@ -1387,7 +1398,7 @@
     )
     inputs_grad, down_total, up_total, out_total, qkv_total, vector_total = last(
         pack, firsts, query_grad, key_grad, normed1, w_qkv, qkv_far, patches[0], hidden_grad, small,
-        ahead_x, ahead_y, keep, vector,
+        ahead_x, ahead_y, send_rest, keep, vector,
     )
     shares = pack.unpack(vector_total)
     return (

time: 282 us -> 278 us (0.986)
    ppermute x1, waiting for transfers between devices: 4.94 us -> 0.46 us  [body(): ahead_x = lax.ppermute(send_over_x, 'ctx', across)]
    pallas_call x1, Pallas kernels: 25.7 us -> 22.5 us  [attend_back(): pl.pallas_call(attend_back_kernel, out_shape=[jax.ShapeDtypeStruct(query....]
  transfers between devices with their start and end apart: 3 -> 3, of which waited for: 2 -> 2; matrix products, arithmetic and copies ran while one was open for 0% -> 0% of each run, Pallas kernels for 15% -> 13%
where the time goes in v3:
time: 278 us
  Pallas kernels  250 us (90%)
  other arithmetic  10.9 us (4%)
  local copies, waits for them, and re-layouts  8.38 us (3%)
  starting transfers between devices  5.18 us (2%)
  waiting for transfers between devices  3.61 us (1%)
    pallas_call x1, Pallas kernels, last(): pl.pallas_call(functools.partial(last_kernel, pack, firsts, tiles), out_s...  114 us
    pallas_call x1, Pallas kernels, front(): pl.pallas_call(functools.partial(front_kernel, pack), out_shape=[jax.Shap...  62.2 us
    pallas_call x1, Pallas kernels, middle(): pl.pallas_call(functools.partial(middle_kernel, pack, firsts), out_shape=...  36.2 us
    pallas_call x1, Pallas kernels, attend_back(): pl.pallas_call(attend_back_kernel, out_shape=[jax.ShapeDtypeStruct(query....  22.5 us
    pallas_call x1, Pallas kernels, attend(): pl.pallas_call(attend_kernel, out_shape=[jax.ShapeDtypeStruct(query.shape...  14.8 us
  transfers between devices with their start and end apart: 3, of which 2 were waited for; matrix products, arithmetic and copies ran while one was open for 0% of the time, Pallas kernels for 13%

profile of v3, /device:TPU:1, one launch (start us, length us, event | category | flops | bytes accessed | tf_op | source)
XLA Modules:
  0.0 278.3 jit_solution(12369308045386685418)
XLA Ops:
  0.6 1.4 add_bitcast_fusion.small_half
  2.1 62.2 %front.1 = (bf16[4,192,256]{2,1,0:T(8,128)(2,1)}, bf16[16,384,256]{2,1,0:T(8,128)(2,1)}, bf16[256,768]{1,0:T(8,128)(2,1)}, f32[2,40,128]{2,1,0:T(8,128)}, bf16[3...) custom-call(bf16[256,768]{1,0:T(8,128)(2,1)} %bitcast.23, ...), custom_call_target="tpu_custom_call" | custom-call | tf_op jit(solution)/shard_map/front/pallas_call | solution.py:355
  64.3 0.5 collective-permute-start
  64.8 14.8 %attend.1 = (f32[4,192,256]{2,1,0:T(8,128)}, bf16[4,192,256]{2,1,0:T(8,128)(2,1)}, f32[4,8,256]{2,1,0:T(8,128)}) custom-call(s32[1,8]{1,0:T(1,128)} %lengths.3, s32[1]{0:T(128)} %bitcast.place, bf16[4,192,256]{2,1,0:T(8,128)(2,1)} %get-tuple-element.42.query, bf16[16,384,256]{2,1,0:T(8,128)(2,1)} %get-tuple-element.43.keys), custom_call_target="tpu_custom_call" | custom-call | tf_op jit(solution)/shard_map/attend/pallas_call | solution.py:1190
  79.7 0.0 collective-permute-done.w_down_far
  79.7 0.0 copy-start.6
  79.7 0.8 copy-done.6
  80.5 36.2 %middle.1 = (bf16[256,768]{1,0:T(8,128)(2,1)}, f32[256,768]{1,0:T(8,128)}, bf16[4,192,256]{2,1,0:T(8,128)(2,1)}, bf16[4,384,384]{2,1,0:T(8,128)(2,1)}, bf16[4,38...) custom-call(bf16[4,192,256]{2,1,0:T(8,128)(2,1)} %get-tuple-element.44, ...), custom_call_target="tpu_custom_call" | custom-call | tf_op jit(solution)/shard_map/middle/pallas_call | solution.py:600
  116.7 0.6 collective-permute-start.1
  117.3 4.1 %collective-permute-start.2 = (bf16[4,384,384]{2,1,0:T(8,128)(2,1)}, bf16[4,384,384]{2,1,0:T(8,128)(2,1)S(1)}, u32[]{:S(2)}, u32[]{:S(2)}) collective-permute-start(bf16[4,384,384]{2,1,0:T(8,128)(2,1)} %get-tuple-element.60), channel_id=1, source_target_pairs={{0,1},{1,0},{2,3},{3,2},{4,5},{5,4},{6,7},{7,6},{8,9},{9,8},{10,11... | collective-permute-start | bytes 3538952 | tf_op jit(solution)/shard_map/ppermute | solution.py:1395
  121.4 22.5 %attend_back.1 = (bf16[4,192,256]{2,1,0:T(8,128)(2,1)}, bf16[16,384,256]{2,1,0:T(8,128)(2,1)}) custom-call(s32[1,8]{1,0:T(1,128)} %lengths.3, s32[1]{0:T(128)} %bitcast.place, bf16[4,192,256]{2,1,0:T(8,128)(2,1)} %get-tuple-element.42.query, bf16[16,384,256]{2,1,0:T(8,128)(2,1)} %get-tuple-element.43.keys, f32[4,192,256]{2,1,0:T(8,128)} %get-tuple-element.51.out, ...), custom_call_target="tpu_custom_call" | custom-call | tf_op jit(solution)/shard_map/attend_back/pallas_call | solution.py:1317
  143.9 0.5 collective-permute-done.1.ahead_x
  144.3 3.1 %collective-permute-done.2.ahead_y = bf16[4,384,384]{2,1,0:T(8,128)(2,1)S(1)} collective-permute-done((bf16[4,384,384]{2,1,0:T(8,128)(2,1)}, bf16[4,384,384]{2,1,0:T(8,128)(2,1)S(1)}, u32[]{:S(2)}, u32[]{:S(2)}) %collective-permute-start.2) | collective-permute-done | bytes 1179680 | tf_op jit(solution)/shard_map/ppermute | solution.py:1395
  147.5 0.0 copy-start.4
  147.5 0.0 copy-done.3
  147.5 1.0 copy-done.4
  148.5 113.8 %last.1 = (f32[256,768]{1,0:T(8,128)}, bf16[1536,768]{1,0:T(8,128)(2,1)}, bf16[384,3072]{1,0:T(8,128)(2,1)}, bf16[384,768]{1,0:T(8,128)(2,1)}, bf16[384,2304]{1,0:T(8,128)(2,1)}, /*index=5*/f32[40,128]{1,0:T(8,128)}) custom-call(bf16[4,192,256]{2,1,0:T(8,128)(2,1)} %get-tuple-element.54.query_grad, bf16[16,384,256]{2,1,0:T(8,128)(2,1)} %get-tuple-element.55.key_grad, ...), custom_call_target="tpu_custom_call" | custom-call | tf_op jit(solution)/shard_map/last/pallas_call | solution.py:1042
  262.3 0.0 copy-start.2
  262.3 1.4 slice_bitcast_fusion.1
  263.7 1.3 slice_bitcast_fusion
  265.0 1.4 slice_bitcast_fusion.2
  266.4 2.2 convert_element_type.25
  268.6 0.0 copy-done.2
  268.6 2.0 convert_element_type.24
  270.6 0.8 copy-done.1
  271.4 2.8 convert_element_type.26
  274.2 0.0 copy-done
  274.2 2.5 convert_element_type.27
  276.7 0.0 copy-done.7
  276.7 0.7 copy.31
  277.5 0.0 copy-done.5
  277.5 0.9 copy.32
  (5 shorter events, 0.0 us)
Async XLA Ops:
  64.3 15.3 %collective-permute-start = (bf16[384,768]{1,0:T(8,128)(2,1)}, bf16[384,768]{1,0:T(8,128)(2,1)S(1)}, u32[]{:S(2)}, u32[]{:S(2)}) collective-permute-start(bf16[384,768]{1,0:T(8,128)(2,1)} %get-tuple-element.49), channel_id=1, source_target_pairs={{0,1},{1,0},{2,3},{3,2},{4,5},{5,4},{6,7},{7,6},{8,9},{9,8},{10,11... | collective-permute-start | bytes 1769480 | tf_op jit(solution)/shard_map/ppermute | solution.py:1383
  79.7 0.8 copy-start.6
  116.7 27.6 %collective-permute-start.1 = (bf16[4,384,384]{2,1,0:T(8,128)(2,1)}, bf16[4,384,384]{2,1,0:T(8,128)(2,1)S(1)}, u32[]{:S(2)}, u32[]{:S(2)}) collective-permute-start(bf16[4,384,384]{2,1,0:T(8,128)(2,1)} %get-tuple-element.59), channel_id=1, source_target_pairs={{0,4},{2,6},{4,0},{6,2},{8,12},{10,14},{12,8},{14,10},{16,20},{18,... | collective-permute-start | bytes 3538952 | tf_op jit(solution)/shard_map/ppermute | solution.py:1394
  117.3 30.2 %collective-permute-start.2 = (bf16[4,384,384]{2,1,0:T(8,128)(2,1)}, bf16[4,384,384]{2,1,0:T(8,128)(2,1)S(1)}, u32[]{:S(2)}, u32[]{:S(2)}) collective-permute-start(bf16[4,384,384]{2,1,0:T(8,128)(2,1)} %get-tuple-element.60), channel_id=1, source_target_pairs={{0,1},{1,0},{2,3},{3,2},{4,5},{5,4},{6,7},{7,6},{8,9},{9,8},{10,11... | collective-permute-start | bytes 3538952 | tf_op jit(solution)/shard_map/ppermute | solution.py:1395
  144.3 3.2 %copy-start.3 = (bf16[4,384,384]{2,1,0:T(8,128)(2,1)}, bf16[4,384,384]{2,1,0:T(8,128)(2,1)S(1)}, u32[]{:S(2)}) copy-start(bf16[4,384,384]{2,1,0:T(8,128)(2,1)S(1)} %collective-permute-done.1.ahead_x) | copy-start | bytes 3538948
  147.5 1.0 copy-start.4
  262.3 6.3 %copy-start.2 = (bf16[384,2304]{1,0:T(8,128)(2,1)S(1)}, bf16[384,2304]{1,0:T(8,128)(2,1)}, u32[]{:S(2)}) copy-start(bf16[384,2304]{1,0:T(8,128)(2,1)} %get-tuple-element.66) | copy-start | bytes 5308420
  268.6 2.8 %copy-start.1 = (bf16[384,3072]{1,0:T(8,128)(2,1)S(1)}, bf16[384,3072]{1,0:T(8,128)(2,1)}, u32[]{:S(2)}) copy-start(bf16[384,3072]{1,0:T(8,128)(2,1)} %get-tuple-element.68) | copy-start | bytes 7077892
  271.4 2.8 copy-start
  274.2 2.6 copy-start.7
  274.2 3.3 %copy-start.5 = (f32[256,768]{1,0:T(8,128)S(1)}, f32[256,768]{1,0:T(8,128)}, u32[]{:S(2)}) copy-start(f32[256,768]{1,0:T(8,128)} %get-tuple-element.64) | copy-start | bytes 2359300

commit v4 on v3

--- a/solution.py
+++ b/solution.py
@@ -943,7 +943,8 @@
             v_land[0] = total
             vector_out[...] = v_land[0, y]
 
-    entry = list(range(early)) + [LATE_TURN + i for i in range(late)]
+    mixed = [2 * k for k in range(ahead)] + [2 * k + 1 for k in range(hidden - ahead)]
+    entry = mixed + list(range(hidden, early)) + [LATE_TURN + i for i in range(late)]
     turns = iter(range(entry[-1] + len(stages)))
 
     def turn():

time: 278 us -> 276 us (level)
    ppermute x1, starting transfers between devices: 4.08 us -> 0.01 us  [body(): ahead_y = lax.ppermute(send_over_y, 'wsh', [(0, 1), (1, 0)])]
  transfers between devices with their start and end apart: 3 -> 3, of which waited for: 2 -> 2; matrix products, arithmetic and copies ran while one was open for 0% -> 0% of each run, Pallas kernels for 13% -> 15%
where the time goes in v4:
time: 276 us; the launch traced here: 277 us
  Pallas kernels  251 us (91%)
  other arithmetic  10.9 us (4%)
  local copies, waits for them, and re-layouts  8.38 us (3%)
  starting transfers between devices  3.67 us (1%)
    pallas_call x1, Pallas kernels, last(): pl.pallas_call(functools.partial(last_kernel, pack, firsts, tiles), out_s...  112 us
    pallas_call x1, Pallas kernels, front(): pl.pallas_call(functools.partial(front_kernel, pack), out_shape=[jax.Shap...  62.2 us
    pallas_call x1, Pallas kernels, middle(): pl.pallas_call(functools.partial(middle_kernel, pack, firsts), out_shape=...  35.9 us
    pallas_call x1, Pallas kernels, attend_back(): pl.pallas_call(attend_back_kernel, out_shape=[jax.ShapeDtypeStruct(query....  24.7 us
    pallas_call x1, Pallas kernels, attend(): pl.pallas_call(attend_kernel, out_shape=[jax.ShapeDtypeStruct(query.shape...  16.4 us
  transfers between devices with their start and end apart: 3, of which 2 were waited for; matrix products, arithmetic and copies ran while one was open for 0% of the time, Pallas kernels for 15%

profile of v4, /device:TPU:1, one launch (start us, length us, event | category | flops | bytes accessed | tf_op | source)
XLA Modules:
  0.0 276.7 jit_solution(504762163620318560)
XLA Ops:
  0.6 1.4 add_bitcast_fusion.small_half
  2.1 62.2 %front.1 = (bf16[4,192,256]{2,1,0:T(8,128)(2,1)}, bf16[16,384,256]{2,1,0:T(8,128)(2,1)}, bf16[256,768]{1,0:T(8,128)(2,1)}, f32[2,40,128]{2,1,0:T(8,128)}, bf16[3...) custom-call(bf16[256,768]{1,0:T(8,128)(2,1)} %bitcast.23, ...), custom_call_target="tpu_custom_call" | custom-call | tf_op jit(solution)/shard_map/front/pallas_call | solution.py:355
  64.3 0.5 collective-permute-start
  64.8 16.4 %attend.1 = (f32[4,192,256]{2,1,0:T(8,128)}, bf16[4,192,256]{2,1,0:T(8,128)(2,1)}, f32[4,8,256]{2,1,0:T(8,128)}) custom-call(s32[1,8]{1,0:T(1,128)} %lengths.3, s32[1]{0:T(128)} %bitcast.place, bf16[4,192,256]{2,1,0:T(8,128)(2,1)} %get-tuple-element.42.query, bf16[16,384,256]{2,1,0:T(8,128)(2,1)} %get-tuple-element.43.keys), custom_call_target="tpu_custom_call" | custom-call | tf_op jit(solution)/shard_map/attend/pallas_call | solution.py:1191
  81.2 0.0 collective-permute-done.w_down_far
  81.2 0.0 copy-start.6
  81.2 0.8 copy-done.6
  82.1 35.9 %middle.1 = (bf16[256,768]{1,0:T(8,128)(2,1)}, f32[256,768]{1,0:T(8,128)}, bf16[4,192,256]{2,1,0:T(8,128)(2,1)}, bf16[4,384,384]{2,1,0:T(8,128)(2,1)}, bf16[4,38...) custom-call(bf16[4,192,256]{2,1,0:T(8,128)(2,1)} %get-tuple-element.44, ...), custom_call_target="tpu_custom_call" | custom-call | tf_op jit(solution)/shard_map/middle/pallas_call | solution.py:600
  117.9 3.2 %collective-permute-start.1 = (bf16[4,384,384]{2,1,0:T(8,128)(2,1)}, bf16[4,384,384]{2,1,0:T(8,128)(2,1)S(1)}, u32[]{:S(2)}, u32[]{:S(2)}) collective-permute-start(bf16[4,384,384]{2,1,0:T(8,128)(2,1)} %get-tuple-element.59), channel_id=1, source_target_pairs={{0,4},{2,6},{4,0},{6,2},{8,12},{10,14},{12,8},{14,10},{16,20},{18,... | collective-permute-start | bytes 3538952 | tf_op jit(solution)/shard_map/ppermute | solution.py:1395
  121.1 0.0 collective-permute-start.2
  121.1 24.7 %attend_back.1 = (bf16[4,192,256]{2,1,0:T(8,128)(2,1)}, bf16[16,384,256]{2,1,0:T(8,128)(2,1)}) custom-call(s32[1,8]{1,0:T(1,128)} %lengths.3, s32[1]{0:T(128)} %bitcast.place, bf16[4,192,256]{2,1,0:T(8,128)(2,1)} %get-tuple-element.42.query, bf16[16,384,256]{2,1,0:T(8,128)(2,1)} %get-tuple-element.43.keys, f32[4,192,256]{2,1,0:T(8,128)} %get-tuple-element.51.out, ...), custom_call_target="tpu_custom_call" | custom-call | tf_op jit(solution)/shard_map/attend_back/pallas_call | solution.py:1318
  145.8 1.5 collective-permute-done.1.ahead_x
  147.3 0.0 copy-start.3
  147.3 0.8 collective-permute-done.2.ahead_y
  148.1 0.2 copy-done.3
  148.3 0.8 copy-done.4
  149.2 111.5 %last.1 = (f32[256,768]{1,0:T(8,128)}, bf16[1536,768]{1,0:T(8,128)(2,1)}, bf16[384,3072]{1,0:T(8,128)(2,1)}, bf16[384,768]{1,0:T(8,128)(2,1)}, bf16[384,2304]{1,0:T(8,128)(2,1)}, /*index=5*/f32[40,128]{1,0:T(8,128)}) custom-call(bf16[4,192,256]{2,1,0:T(8,128)(2,1)} %get-tuple-element.54.query_grad, bf16[16,384,256]{2,1,0:T(8,128)(2,1)} %get-tuple-element.55.key_grad, ...), custom_call_target="tpu_custom_call" | custom-call | tf_op jit(solution)/shard_map/last/pallas_call | solution.py:1043
  260.7 0.0 copy-start.2
  260.7 1.4 slice_bitcast_fusion.1
  262.1 1.3 slice_bitcast_fusion
  263.4 1.4 slice_bitcast_fusion.2
  264.8 2.2 convert_element_type.25
  266.9 0.0 copy-done.2
  266.9 2.0 convert_element_type.24
  269.0 0.8 copy-done.1
  269.8 2.8 convert_element_type.26
  272.5 0.0 copy-done
  272.5 2.5 convert_element_type.27
  275.1 0.0 copy-done.7
  275.1 0.7 copy.31
  275.8 0.0 copy-done.5
  275.8 0.9 copy.32
  (5 shorter events, 0.0 us)
Async XLA Ops:
  64.3 16.9 %collective-permute-start = (bf16[384,768]{1,0:T(8,128)(2,1)}, bf16[384,768]{1,0:T(8,128)(2,1)S(1)}, u32[]{:S(2)}, u32[]{:S(2)}) collective-permute-start(bf16[384,768]{1,0:T(8,128)(2,1)} %get-tuple-element.49), channel_id=1, source_target_pairs={{0,1},{1,0},{2,3},{3,2},{4,5},{5,4},{6,7},{7,6},{8,9},{9,8},{10,11... | collective-permute-start | bytes 1769480 | tf_op jit(solution)/shard_map/ppermute | solution.py:1384
  81.2 0.8 copy-start.6
  117.9 29.4 %collective-permute-start.1 = (bf16[4,384,384]{2,1,0:T(8,128)(2,1)}, bf16[4,384,384]{2,1,0:T(8,128)(2,1)S(1)}, u32[]{:S(2)}, u32[]{:S(2)}) collective-permute-start(bf16[4,384,384]{2,1,0:T(8,128)(2,1)} %get-tuple-element.59), channel_id=1, source_target_pairs={{0,4},{2,6},{4,0},{6,2},{8,12},{10,14},{12,8},{14,10},{16,20},{18,... | collective-permute-start | bytes 3538952 | tf_op jit(solution)/shard_map/ppermute | solution.py:1395
  121.1 27.0 %collective-permute-start.2 = (bf16[4,384,384]{2,1,0:T(8,128)(2,1)}, bf16[4,384,384]{2,1,0:T(8,128)(2,1)S(1)}, u32[]{:S(2)}, u32[]{:S(2)}) collective-permute-start(bf16[4,384,384]{2,1,0:T(8,128)(2,1)} %get-tuple-element.60), channel_id=1, source_target_pairs={{0,1},{1,0},{2,3},{3,2},{4,5},{5,4},{6,7},{7,6},{8,9},{9,8},{10,11... | collective-permute-start | bytes 3538952 | tf_op jit(solution)/shard_map/ppermute | solution.py:1396
  147.3 1.0 copy-start.3
  148.1 1.0 copy-start.4
  260.7 6.3 %copy-start.2 = (bf16[384,2304]{1,0:T(8,128)(2,1)S(1)}, bf16[384,2304]{1,0:T(8,128)(2,1)}, u32[]{:S(2)}) copy-start(bf16[384,2304]{1,0:T(8,128)(2,1)} %get-tuple-element.66) | copy-start | bytes 5308420
  266.9 2.8 %copy-start.1 = (bf16[384,3072]{1,0:T(8,128)(2,1)S(1)}, bf16[384,3072]{1,0:T(8,128)(2,1)}, u32[]{:S(2)}) copy-start(bf16[384,3072]{1,0:T(8,128)(2,1)} %get-tuple-element.68) | copy-start | bytes 7077892
  269.8 2.8 copy-start
  272.5 2.6 copy-start.7
  272.5 3.3 %copy-start.5 = (f32[256,768]{1,0:T(8,128)S(1)}, f32[256,768]{1,0:T(8,128)}, u32[]{:S(2)}) copy-start(f32[256,768]{1,0:T(8,128)} %get-tuple-element.64) | copy-start | bytes 2359300

commit v5 on v4

--- a/solution.py
+++ b/solution.py
@@ -1014,7 +1014,7 @@
     go.finish()
 
 
-LATE_TURN = 9
+LATE_TURN = 8
 
 
 def last(

time: 276 us -> 280 us (1.014)
  Pallas kernels: 251 us -> 255 us
    pallas_call x1, Pallas kernels: 112 us -> 115 us  [last(): pl.pallas_call(functools.partial(last_kernel, pack, firsts, tiles), out_s...]
where the time goes in v5:
time: 280 us
  Pallas kernels  255 us (91%)
  other arithmetic  10.9 us (4%)
  local copies, waits for them, and re-layouts  8.38 us (3%)
  starting transfers between devices  3.15 us (1%)
    pallas_call x1, Pallas kernels, last(): pl.pallas_call(functools.partial(last_kernel, pack, firsts, tiles), out_s...  115 us
    pallas_call x1, Pallas kernels, front(): pl.pallas_call(functools.partial(front_kernel, pack), out_shape=[jax.Shap...  62.2 us
    pallas_call x1, Pallas kernels, middle(): pl.pallas_call(functools.partial(middle_kernel, pack, firsts), out_shape=...  36.3 us
    pallas_call x1, Pallas kernels, attend_back(): pl.pallas_call(attend_back_kernel, out_shape=[jax.ShapeDtypeStruct(query....  24.7 us
    pallas_call x1, Pallas kernels, attend(): pl.pallas_call(attend_kernel, out_shape=[jax.ShapeDtypeStruct(query.shape...  16.4 us
  transfers between devices with their start and end apart: 3, of which 2 were waited for; matrix products, arithmetic and copies ran while one was open for 0% of the time, Pallas kernels for 15%

profile of v5, /device:TPU:1, one launch (start us, length us, event | category | flops | bytes accessed | tf_op | source)
XLA Modules:
  0.0 279.7 jit_solution(8465534984731583597)
XLA Ops:
  0.6 1.4 add_bitcast_fusion.small_half
  2.1 62.2 %front.1 = (bf16[4,192,256]{2,1,0:T(8,128)(2,1)}, bf16[16,384,256]{2,1,0:T(8,128)(2,1)}, bf16[256,768]{1,0:T(8,128)(2,1)}, f32[2,40,128]{2,1,0:T(8,128)}, bf16[3...) custom-call(bf16[256,768]{1,0:T(8,128)(2,1)} %bitcast.23, ...), custom_call_target="tpu_custom_call" | custom-call | tf_op jit(solution)/shard_map/front/pallas_call | solution.py:355
  64.3 0.5 collective-permute-start
  64.8 16.4 %attend.1 = (f32[4,192,256]{2,1,0:T(8,128)}, bf16[4,192,256]{2,1,0:T(8,128)(2,1)}, f32[4,8,256]{2,1,0:T(8,128)}) custom-call(s32[1,8]{1,0:T(1,128)} %lengths.3, s32[1]{0:T(128)} %bitcast.place, bf16[4,192,256]{2,1,0:T(8,128)(2,1)} %get-tuple-element.42.query, bf16[16,384,256]{2,1,0:T(8,128)(2,1)} %get-tuple-element.43.keys), custom_call_target="tpu_custom_call" | custom-call | tf_op jit(solution)/shard_map/attend/pallas_call | solution.py:1191
  81.2 0.0 collective-permute-done.w_down_far
  81.2 0.0 copy-start.6
  81.2 0.8 copy-done.6
  82.1 36.3 %middle.1 = (bf16[256,768]{1,0:T(8,128)(2,1)}, f32[256,768]{1,0:T(8,128)}, bf16[4,192,256]{2,1,0:T(8,128)(2,1)}, bf16[4,384,384]{2,1,0:T(8,128)(2,1)}, bf16[4,38...) custom-call(bf16[4,192,256]{2,1,0:T(8,128)(2,1)} %get-tuple-element.44, ...), custom_call_target="tpu_custom_call" | custom-call | tf_op jit(solution)/shard_map/middle/pallas_call | solution.py:600
  118.4 0.6 collective-permute-start.1
  119.0 2.0 collective-permute-start.2
  121.0 24.7 %attend_back.1 = (bf16[4,192,256]{2,1,0:T(8,128)(2,1)}, bf16[16,384,256]{2,1,0:T(8,128)(2,1)}) custom-call(s32[1,8]{1,0:T(1,128)} %lengths.3, s32[1]{0:T(128)} %bitcast.place, bf16[4,192,256]{2,1,0:T(8,128)(2,1)} %get-tuple-element.42.query, bf16[16,384,256]{2,1,0:T(8,128)(2,1)} %get-tuple-element.43.keys, f32[4,192,256]{2,1,0:T(8,128)} %get-tuple-element.51.out, ...), custom_call_target="tpu_custom_call" | custom-call | tf_op jit(solution)/shard_map/attend_back/pallas_call | solution.py:1318
  145.7 0.3 collective-permute-done.1.ahead_x
  146.0 0.0 copy-start.3
  146.0 1.4 collective-permute-done.2.ahead_y
  147.5 0.0 copy-done.3
  147.5 1.0 copy-done.4
  148.5 115.1 %last.1 = (f32[256,768]{1,0:T(8,128)}, bf16[1536,768]{1,0:T(8,128)(2,1)}, bf16[384,3072]{1,0:T(8,128)(2,1)}, bf16[384,768]{1,0:T(8,128)(2,1)}, bf16[384,2304]{1,0:T(8,128)(2,1)}, /*index=5*/f32[40,128]{1,0:T(8,128)}) custom-call(bf16[4,192,256]{2,1,0:T(8,128)(2,1)} %get-tuple-element.54.query_grad, bf16[16,384,256]{2,1,0:T(8,128)(2,1)} %get-tuple-element.55.key_grad, ...), custom_call_target="tpu_custom_call" | custom-call | tf_op jit(solution)/shard_map/last/pallas_call | solution.py:1043
  263.6 0.0 copy-start.2
  263.6 1.4 slice_bitcast_fusion.1
  265.1 1.3 slice_bitcast_fusion
  266.4 1.4 slice_bitcast_fusion.2
  267.8 2.2 convert_element_type.25
  269.9 0.0 copy-done.2
  269.9 2.0 convert_element_type.24
  271.9 0.8 copy-done.1
  272.7 2.8 convert_element_type.26
  275.5 0.0 copy-done
  275.5 2.5 convert_element_type.27
  278.1 0.0 copy-done.7
  278.1 0.7 copy.31
  278.8 0.0 copy-done.5
  278.8 0.9 copy.32
  (5 shorter events, 0.0 us)
Async XLA Ops:
  64.3 16.9 %collective-permute-start = (bf16[384,768]{1,0:T(8,128)(2,1)}, bf16[384,768]{1,0:T(8,128)(2,1)S(1)}, u32[]{:S(2)}, u32[]{:S(2)}) collective-permute-start(bf16[384,768]{1,0:T(8,128)(2,1)} %get-tuple-element.49), channel_id=1, source_target_pairs={{0,1},{1,0},{2,3},{3,2},{4,5},{5,4},{6,7},{7,6},{8,9},{9,8},{10,11... | collective-permute-start | bytes 1769480 | tf_op jit(solution)/shard_map/ppermute | solution.py:1384
  81.2 0.8 copy-start.6
  118.4 27.6 %collective-permute-start.1 = (bf16[4,384,384]{2,1,0:T(8,128)(2,1)}, bf16[4,384,384]{2,1,0:T(8,128)(2,1)S(1)}, u32[]{:S(2)}, u32[]{:S(2)}) collective-permute-start(bf16[4,384,384]{2,1,0:T(8,128)(2,1)} %get-tuple-element.59), channel_id=1, source_target_pairs={{0,4},{2,6},{4,0},{6,2},{8,12},{10,14},{12,8},{14,10},{16,20},{18,... | collective-permute-start | bytes 3538952 | tf_op jit(solution)/shard_map/ppermute | solution.py:1395
  119.0 28.4 %collective-permute-start.2 = (bf16[4,384,384]{2,1,0:T(8,128)(2,1)}, bf16[4,384,384]{2,1,0:T(8,128)(2,1)S(1)}, u32[]{:S(2)}, u32[]{:S(2)}) collective-permute-start(bf16[4,384,384]{2,1,0:T(8,128)(2,1)} %get-tuple-element.60), channel_id=1, source_target_pairs={{0,1},{1,0},{2,3},{3,2},{4,5},{5,4},{6,7},{7,6},{8,9},{9,8},{10,11... | collective-permute-start | bytes 3538952 | tf_op jit(solution)/shard_map/ppermute | solution.py:1396
  146.0 1.4 copy-start.3
  147.5 1.0 copy-start.4
  263.6 6.3 %copy-start.2 = (bf16[384,2304]{1,0:T(8,128)(2,1)S(1)}, bf16[384,2304]{1,0:T(8,128)(2,1)}, u32[]{:S(2)}) copy-start(bf16[384,2304]{1,0:T(8,128)(2,1)} %get-tuple-element.66) | copy-start | bytes 5308420
  269.9 2.8 %copy-start.1 = (bf16[384,3072]{1,0:T(8,128)(2,1)S(1)}, bf16[384,3072]{1,0:T(8,128)(2,1)}, u32[]{:S(2)}) copy-start(bf16[384,3072]{1,0:T(8,128)(2,1)} %get-tuple-element.68) | copy-start | bytes 7077892
  272.7 2.8 copy-start
  275.5 2.6 copy-start.7
  275.5 3.3 %copy-start.5 = (f32[256,768]{1,0:T(8,128)S(1)}, f32[256,768]{1,0:T(8,128)}, u32[]{:S(2)}) copy-start(f32[256,768]{1,0:T(8,128)} %get-tuple-element.64) | copy-start | bytes 2359300
